TPU v7x, 32 devices: a whole 2x2x4 slice. The times are simulated.
32 devices in a mesh: rep: 8 (over y, x, core), tp: 4 (over z).
Axes of the slice: x: 2, y: 2, z: 4, core: 2. Of those that a mesh axis runs over, the one named last changes fastest.
Arguments:
- hidden: bfloat16 [32, 2048], P('rep'), may hold values from -6 to 6
- lengths: int32 [32], P('rep'), may hold values from 1 to 5119, as said below
- page_table: int32 [32, 40], P('rep', 'tp'), may hold values from 0 to 39, as said below
- move_slot: int32 [8], P('rep'), may hold values from 0 to 3
- lat_pool: bfloat16 [1280, 128, 512], P(('rep', 'tp')), may hold values from -6 to 6
- rope_pool: bfloat16 [1280, 64, 128], P(('rep', 'tp')), may hold values from -460 to 460
- norm_attn: float32 [2048], replicated, may hold values from 0.5 to 1.5
- w_query: bfloat16 [2048, 3072], P(None, 'tp'), may hold values from -0.125 to 0.125
- w_latent: bfloat16 [2048, 576], replicated, may hold values from -0.125 to 0.125
- latent_gain: float32 [512], replicated, may hold values from 0.5 to 1.5
- w_key_up: bfloat16 [16, 128, 512], P('tp'), may hold values from -0.5 to 0.5
- w_value_up: bfloat16 [16, 512, 128], P('tp'), may hold values from -0.25 to 0.25
- w_output: bfloat16 [2048, 2048], P('tp'), may hold values from -0.125 to 0.125
- norm_ffn: float32 [2048], replicated, may hold values from 0.5 to 1.5
- w_router: bfloat16 [2048, 64], replicated, may hold values from -0.125 to 0.125
- route_ids: int32 [32, 6], replicated, may hold values from 0 to 63, all different within a row
- expert_gate: bfloat16 [64, 2048, 1408], P('rep', None, 'tp'), may hold values from -0.125 to 0.125
- expert_up: bfloat16 [64, 2048, 1408], P('rep', None, 'tp'), may hold values from -0.125 to 0.125
- expert_down: bfloat16 [64, 1408, 2048], P('rep', 'tp'), may hold values from -0.15625 to 0.15625
- shared_gate: bfloat16 [2048, 2816], P(None, 'tp'), may hold values from -0.125 to 0.125
- shared_up: bfloat16 [2048, 2816], P(None, 'tp'), may hold values from -0.125 to 0.125
- shared_down: bfloat16 [2816, 2048], P('tp'), may hold values from -0.109375 to 0.109375
Outputs:
- mixed: bfloat16 [32, 2048], P('rep')
- lat_cache: bfloat16 [1280, 128, 512], P(('rep', 'tp'))
- rope_cache: bfloat16 [1280, 64, 128], P(('rep', 'tp'))
Inputs may be any that keep to these rules, and one draw needn't show every extreme that they name: lengths are heavy-tailed; in every draw some request has exactly 5119 cached tokens. `page_table`: the block of one device (rows of one replica, columns of one index of tp) holds each of its pool's pages exactly once. `route_ids`: the 6 ids of a row differ.
All inputs are finite; a program needn't handle non-finite values.
Results may differ from a plain program's by a relative error of at most 0.013.
Values may be sent and summed in bfloat16 or wider, within the bound.
No kernel may reach another device: no remote copies, remote signals or barrier semaphores. Data moves between devices by JAX's collectives and lax.ppermute only.
A program may use at most 192 MiB of HBM per device.

v0:
```python
import jax
import jax.numpy as jnp
from jax import lax
from jax.sharding import PartitionSpec as P

NOPE = 128
ROPE = 64
SINKS = 4
WIN = 4096
PAGE = 128


EPS = 1e-06
ROUTE_SCALE = 2.446
NEG = -1e30


def joined(part, axis, combine):
    gathered = jax.tree.map(lambda a: lax.all_gather(a, axis), part)

    def take(source):
        return jax.tree.map(lambda a: lax.dynamic_index_in_dim(a, source, 0, False), gathered)

    return lax.fori_loop(
        1, lax.axis_size(axis), lambda source, state: combine(state, take(source)), take(0)
    )


def swapped(value, axis, apart):
    mask = 2**apart
    pairs = [(source, source ^ mask) for source in range(lax.axis_size(axis))]
    return lax.ppermute(value, axis, pairs)


def rms_norm(values, gain):
    values = values.astype(jnp.float32)
    return values * lax.rsqrt(jnp.mean(values * values, axis=-1, keepdims=True) + EPS) * gain


def combine(first, second):
    peak = jnp.maximum(first[0], second[0])
    first_factor = jnp.exp(first[0] - peak)
    second_factor = jnp.exp(second[0] - peak)
    return (
        peak,
        first[1] * first_factor + second[1] * second_factor,
        first[2] * first_factor[..., None] + second[2] * second_factor[..., None],
    )


def body(
    hidden,
    lengths,
    page_table,
    move_slot,
    lat_pool,
    rope_pool,
    norm_attn,
    w_query,
    w_latent,
    latent_gain,
    w_key_up,
    w_value_up,
    w_output,
    norm_ffn,
    w_router,
    route_ids,
    expert_gate,
    expert_up,
    expert_down,
    shared_gate,
    shared_up,
    shared_down,
):
    f32 = jnp.float32
    bf16 = jnp.bfloat16
    requests = hidden.shape[0]
    per_dev = page_table.shape[1]
    local_heads = w_key_up.shape[0]
    nope_size = w_key_up.shape[1]
    lat_size = w_key_up.shape[2]
    tp_rank = lax.axis_index("tp")
    half_bit = lax.axis_size("rep").bit_length() - 2
    moved_slot = move_slot[0]
    slot_pages = page_table[moved_slot]
    scale = (NOPE + ROPE) ** (-0.5)
    page_ids = tp_rank * per_dev + jnp.arange(per_dev, dtype=jnp.int32)
    positions = (page_ids[:, None] * PAGE + jnp.arange(PAGE, dtype=jnp.int32)[None, :]).reshape(
        1, per_dev, 1, PAGE
    )
    outgoing = (lat_pool[slot_pages], rope_pool[slot_pages], hidden[moved_slot][None, :])
    got_lat, got_rope, got_row = swapped((outgoing[0], outgoing[1], outgoing[2]), "rep", half_bit)
    got_length = swapped(lengths[moved_slot][None], "rep", half_bit)
    moved_lat = lat_pool.at[slot_pages].set(got_lat)
    moved_rope = rope_pool.at[slot_pages].set(got_rope)
    x_rows = hidden.at[moved_slot].set(got_row[0])
    lens = lengths.at[moved_slot].set(got_length[0])
    normed = rms_norm(x_rows, norm_attn).astype(bf16)
    query = (
        jnp.dot(normed, w_query, preferred_element_type=f32)
        .astype(bf16)
        .reshape(requests, local_heads, -1)
    )
    q_lat = jnp.einsum(
        "rhn,hnl->rhl", query[..., :nope_size], w_key_up, preferred_element_type=f32
    ).astype(bf16)
    q_pos = query[..., nope_size:]
    all_lat = lax.all_gather(q_lat, "tp", axis=1, tiled=True)
    all_pos = lax.all_gather(q_pos, "tp", axis=1, tiled=True)
    latent_full = jnp.dot(normed, w_latent, preferred_element_type=f32)
    c_new = rms_norm(latent_full[:, :lat_size], latent_gain).astype(bf16)
    p_new = latent_full[:, lat_size:].astype(bf16)
    lat_rows = moved_lat[page_table]
    rope_rows = moved_rope[page_table]
    scores = (
        jnp.einsum("rhl,rjcl->rjhc", all_lat, lat_rows, preferred_element_type=f32)
        + jnp.einsum("rhe,rjec->rjhc", all_pos, rope_rows, preferred_element_type=f32)
    ) * scale
    length_now = lens[:, None, None, None]
    allowed = (positions < length_now) & ((positions < SINKS) | (positions >= length_now + 1 - WIN))
    page_max = jnp.max(jnp.where(allowed, scores, NEG), axis=3)
    weights = jnp.where(allowed, jnp.exp(scores - page_max[..., None]), 0.0).astype(bf16)
    totals = jnp.sum(weights.astype(f32), axis=3)
    sums = jnp.einsum("rjhc,rjcl->rjhl", weights, lat_rows, preferred_element_type=f32)
    local_peak = jnp.max(page_max, axis=1)
    factor = jnp.exp(page_max - local_peak[:, None, :])
    local_total = jnp.sum(factor * totals, axis=1)
    local_sums = jnp.sum(factor[..., None] * sums, axis=1)
    peak, denom, numer = joined((local_peak, local_total, local_sums), "tp", combine)
    finish_denom = denom
    finish_numer = numer
    new_score = (
        jnp.sum(all_lat.astype(f32) * c_new.astype(f32)[:, None, :], -1)
        + jnp.sum(all_pos.astype(f32) * p_new.astype(f32)[:, None, :], -1)
    ) * scale
    final_peak = jnp.maximum(peak, new_score)
    old_factor = jnp.exp(peak - final_peak)
    new_factor = jnp.exp(new_score - final_peak)
    finish_denom = finish_denom * old_factor + new_factor
    finish_numer = (
        finish_numer * old_factor[..., None] + new_factor[..., None] * c_new.astype(f32)[:, None, :]
    )
    o_lat = (finish_numer / finish_denom[..., None]).astype(bf16)
    own_heads = lax.dynamic_slice_in_dim(o_lat, tp_rank * local_heads, local_heads, 1)
    o_val = (
        jnp.einsum("rhl,hlv->rhv", own_heads, w_value_up, preferred_element_type=f32)
        .astype(bf16)
        .reshape(requests, -1)
    )
    partial_out = jnp.dot(o_val, w_output, preferred_element_type=f32)
    attn = lax.psum(partial_out, "tp")
    h_one, c_new, p_new = ((x_rows.astype(f32) + attn).astype(bf16), c_new, p_new)
    page_local = lens // PAGE - tp_rank * per_dev
    owned = (page_local >= 0) & (page_local < per_dev)
    target = jnp.take_along_axis(page_table, jnp.clip(page_local, 0, per_dev - 1)[:, None], axis=1)[
        :, 0
    ]
    target = jnp.where(owned, target, moved_lat.shape[0])
    row_in = lens % PAGE
    lat_cache = moved_lat.at[target, row_in].set(c_new, mode="drop")
    rope_cache = moved_rope.at[target, :, row_in].set(p_new, mode="drop")
    ffn_in = rms_norm(h_one, norm_ffn).astype(bf16)
    local_experts = expert_gate.shape[0]
    first_expert = lax.axis_index("rep") * local_experts
    expert_ids = first_expert + jnp.arange(local_experts, dtype=jnp.int32)
    piece = lax.all_gather(ffn_in, "rep", axis=0, tiled=True)
    gates = jax.nn.sigmoid(jnp.dot(piece, w_router, preferred_element_type=f32))
    chosen = jnp.take_along_axis(gates, route_ids, axis=1)
    route_weight = chosen / jnp.sum(chosen, axis=1, keepdims=True) * ROUTE_SCALE
    matches = route_ids[:, :, None] == expert_ids[None, None, :]
    coef = jnp.sum(jnp.where(matches, route_weight[:, :, None], 0.0), axis=1)
    gate_val = jnp.einsum("rd,edf->erf", piece, expert_gate, preferred_element_type=f32)
    up_val = jnp.einsum("rd,edf->erf", piece, expert_up, preferred_element_type=f32)
    hid = (jax.nn.silu(gate_val) * up_val).astype(bf16)
    output = jnp.einsum("erf,efd->erd", hid, expert_down, preferred_element_type=f32)
    routed = jnp.einsum("re,erd->rd", coef, output, preferred_element_type=f32)
    shared_hid = (
        jax.nn.silu(jnp.dot(ffn_in, shared_gate, preferred_element_type=f32))
        * jnp.dot(ffn_in, shared_up, preferred_element_type=f32)
    ).astype(bf16)
    shared_part = jnp.dot(shared_hid, shared_down, preferred_element_type=f32)
    routed_all, shared_all = lax.psum((routed, shared_part), "tp")
    own_rows = lax.psum_scatter(routed_all, "rep", scatter_dimension=0, tiled=True)
    total = own_rows + shared_all
    mixed = (h_one.astype(f32) + total).astype(bf16)
    return (mixed, lat_cache, rope_cache)


def solution(mesh):
    in_specs = (
        P("rep", None),
        P("rep"),
        P("rep", "tp"),
        P("rep"),
        P(("rep", "tp"), None, None),
        P(("rep", "tp"), None, None),
        P(),
        P(None, "tp"),
        P(),
        P(),
        P("tp", None, None),
        P("tp", None, None),
        P("tp", None),
        P(),
        P(),
        P(),
        P("rep", None, "tp"),
        P("rep", None, "tp"),
        P("rep", "tp", None),
        P(None, "tp"),
        P(None, "tp"),
        P("tp", None),
    )
    out_specs = (P("rep", None), P(("rep", "tp"), None, None), P(("rep", "tp"), None, None))
    return jax.shard_map(body, mesh=mesh, in_specs=in_specs, out_specs=out_specs, check_vma=False)
```

profile of v0, /device:TPU:0, one launch (start us, length us, event | category | flops | bytes accessed | tf_op | source)
XLA Modules:
  0.0 268.2 jit_solution(3504948415906280634)
XLA Ops:
  8.0 2.1 copy.152
  10.8 5.5 %copy.151 = bf16[40,128,512]{2,1,0:T(8,128)(2,1)} copy(bf16[40,128,512]{2,1,0:T(8,128)(2,1)} %param.32) | data formatting | bytes 10485760
  17.6 3.0 %collective-permute-start.1 = (s32[1]{0:T(128)}, s32[1]{0:T(128)}, u32[]{:S(2)}, u32[]{:S(2)}) collective-permute-start(s32[1]{0:T(128)} %dynamic_slice.54), channel_id=1, source_target_pairs={{0,16},{4,20},{8,24},{12,28},{16,0},{20,4},{24,8},{28,12},{1,17},{... | collective-permute-start | bytes 20 | tf_op jit(solution)/shard_map/ppermute | solution.py:32
  20.6 1.7 gather_fusion.2
  23.0 2.0 collective-permute-start
  25.0 4.3 %gather_fusion = bf16[10,128,512]{2,1,0:T(8,128)(2,1)} fusion(bf16[40,128,512]{2,1,0:T(8,128)(2,1)} %copy.151, s32[1024]{0:T(1024)S(1)} %pad_clamp_fusion.1), kind=kCustom, calls=%fused_computation | custom fusion | bytes 2621480 | tf_op jit(solution)/shard_map/gather | solution.py:91
  30.3 1.3 dynamic-slice.13
  32.3 1.5 and_reduce_fusion
  33.7 1.5 fusion.60
  37.4 1.4 broadcast_select_fusion
  39.7 2.4 fusion.69
  42.1 1.2 fusion.9
  43.3 13.9 %all_gather.27 = bf16[4,16,512]{2,0,1:T(4,128)(2,1)S(1)} all-gather(bf16[4,4,512]{2,0,1:T(4,128)(2,1)S(1)} %fusion.9), channel_id=1, replica_groups=mesh['rep'=8,'tp'=4] {'tp'}, dimensions={1}, use_global_device_ids=true | all-gather | bytes 81920 | tf_op jit(solution)/shard_map/all_gather | solution.py:108
  57.7 13.1 %all_gather.28 = bf16[4,16,64]{2,0,1:T(4,128)(2,1)S(1)} all-gather(bf16[4,4,64]{2,0,1:T(4,128)(2,1)S(1)} %copy.112), channel_id=1, replica_groups=mesh['rep'=8,'tp'=4] {'tp'}, dimensions={1}, use_global_device_ids=true | all-gather | bytes 10240 | tf_op jit(solution)/shard_map/all_gather | solution.py:109
  74.2 1.3 copy.101
  75.7 5.6 %scatter_fusion = bf16[40,128,512]{2,1,0:T(8,128)(2,1)} fusion(bf16[40,128,512]{2,1,0:T(8,128)(2,1)} %copy.151, s32[10]{0:T(128)S(1)} %copy-done.11, bf16[10,128,512]{2,1,0:T(8,128)(2,1)} %collective-permute-done.2), kind=kCustom, calls=%fused_computation.6 | custom fusion | bytes 3932200 | tf_op jit(solution)/shard_map/scatter | solution.py:94
  81.3 7.1 %gather_fusion.1 = bf16[40,128,512]{2,1,0:T(8,128)(2,1)} fusion(bf16[40,128,512]{2,1,0:T(8,128)(2,1)} %scatter_fusion, s32[1024]{0:T(1024)S(1)} %pad_clamp_fusion), kind=kCustom, calls=%fused_computation.1 | custom fusion | bytes 10485920 | tf_op jit(solution)/shard_map/gather | solution.py:113
  88.4 4.2 %select_reduce_fusion = (f32[4,10,16]{2,1,0:T(8,128)S(1)}, f32[4,10,128,16]{2,3,1,0:T(8,128)S(1)}) fusion(pred[4,10,128]{2,1,0:T(8,128)(4,1)S(1)} %or_and_fusion, f32[4,10,128,16]{2,3,1,0:T(8,128)S(1)} %fusion.45, bf16[4,10,128,512]{3,2,1,0:T(8,128)(2,1)} %bitcast.111, bf16[4,16,512,1]{2,0,1,3:T(4,128)(2,1)S(1)} %bitcast.116), kind=kOutput, calls=%fused_computation.49 | convolution fusion | flops 84213120 | bytes 5971456 | tf_op jit(solution)/shard_map/rhl,rjcl->rjhc/dot_general | solution.py:116
  92.9 11.9 %all-gather.3 = f32[4,4,16]{2,1,0:T(4,128)S(1)} all-gather(f32[1,4,16]{2,1,0:T(4,128)S(1)} %bitcast.118), channel_id=2, replica_groups=mesh['rep'=8,'tp'=4] {'tp'}, dimensions={0}, use_global_device_ids=true | all-gather | bytes 1280 | tf_op jit(solution)/shard_map/all_gather | solution.py:19
  104.8 11.9 %all-gather.4 = f32[4,4,16]{2,1,0:T(4,128)S(1)} all-gather(f32[1,4,16]{2,1,0:T(4,128)S(1)} %bitcast.119), channel_id=3, replica_groups=mesh['rep'=8,'tp'=4] {'tp'}, dimensions={0}, use_global_device_ids=true | all-gather | bytes 1280 | tf_op jit(solution)/shard_map/all_gather | solution.py:19
  117.6 14.9 %all-gather.2 = f32[16,16,512]{2,1,0:T(8,128)S(1)} all-gather(f32[4,16,512]{2,1,0:T(8,128)S(1)} %fusion.5), channel_id=4, replica_groups=mesh['rep'=8,'tp'=4] {'tp'}, dimensions={0}, use_global_device_ids=true | all-gather | bytes 655360 | tf_op jit(solution)/shard_map/all_gather | solution.py:19
  133.4 1.6 fusion.16
  135.0 17.0 %psum.21 = f32[4,2048]{1,0:T(4,128)S(1)} all-reduce(f32[4,2048]{1,0:T(4,128)S(1)} %fusion.16), channel_id=1, replica_groups=mesh['rep'=8,'tp'=4] {'tp'}, use_global_device_ids=true, to_apply=%region_14.15 | all-reduce | flops 8192 | bytes 65536 | tf_op jit(solution)/shard_map/psum | solution.py:151
  152.2 9.4 %all-gather.5 = bf16[8,4,2048]{2,1,0:T(4,128)(2,1)S(1)} all-gather(bf16[1,4,2048]{2,1,0:T(4,128)(2,1)S(1)} %fusion.76), channel_id=1, replica_groups=mesh['rep'=8,'tp'=4] {'rep'}, dimensions={0}, use_global_device_ids=true | all-gather | bytes 147456 | tf_op jit(solution)/shard_map/all_gather | solution.py:166
  161.9 1.6 gather_fusion.4
  163.9 7.7 %convolution_bitcast_fusion.1 = f32[8,32,352]{2,1,0:T(8,128)S(1)} fusion(bf16[32,2048,1]{1,0,2:T(8,128)(2,1)S(1)} %reshape.349, bf16[8,2048,352]{1,2,0:T(8,128)(2,1)} %param.44), kind=kOutput, calls=%fused_computation.25 | convolution fusion | flops 369098752 | bytes 12025856 | tf_op jit(solution)/shard_map/rd,edf->erf/dot_general | solution.py:172
  171.7 12.9 %fusion.15 = bf16[8,32,2048]{2,1,0:T(8,128)(2,1)S(1)} fusion(bf16[8,352,2048]{2,1,0:T(8,128)(2,1)} %param.46, bf16[32,2048,1]{1,0,2:T(8,128)(2,1)S(1)} %reshape.349, bf16[8,2048,352]{1,2,0:T(8,128)(2,1)} %param.45, f32[8,32,352]{2,1,0:T(8,128)S(1)} %convolution_bitcast_fusion.1), kind=kOutput, calls=%fused_computation.40 | convolution fusion | flops 738738176 | bytes 24608768 | tf_op jit(solution)/shard_map/erf,efd->erd/dot_general | solution.py:175
  186.2 2.8 %fusion.74 = f32[4,704]{1,0:T(4,128)S(1)} fusion(bf16[2048,704]{0,1:T(8,128)(2,1)} %param.47, bf16[4,2048]{1,0:T(4,128)(2,1)S(1)} %get-tuple-element.249, f32[2048]{0:T(1024)S(1)} %copy-done.7, f32[4]{0:T(128)S(1)} %add_rsqrt_fusion), kind=kOutput, calls=%fused_computation.155 | convolution fusion | flops 11567104 | bytes 2919440 | tf_op jit(solution)/shard_map/dot_general | solution.py:178
  189.0 2.1 scatter_fusion.2
  191.2 46.2 %all-reduce.3.cloned.1.call-done = f32[32,2048]{1,0:T(8,128)} async-done(((f32[32,2048]{1,0:T(8,128)}), f32[32,2048]{1,0:T(8,128)}) %all-reduce.3.cloned.1.call-update) | async-done | bytes 262160
  237.4 4.3 %convolution_add_fusion = f32[4,2048]{1,0:T(4,128)S(1)} fusion(bf16[704,2048]{1,0:T(8,128)(2,1)} %param.49, bf16[2048,704]{0,1:T(8,128)(2,1)} %param.48, f32[32,2048]{1,0:T(8,128)} %all-reduce.3.cloned.1.call-done, u32[]{:T(128)S(6)} %multiply.23, f32[4,704]{1,0:T(4,128)S(1)} %fusion.74, bf16[4,2048]{1,0:T(4,128)(2,1)S(1)} %get-tuple-element.249, ...), kind=kOutput, calls=%fused_computation.18 | convolution fusion | flops 23126528 | bytes 5868564 | tf_op jit(solution)/shard_map/dot_general | solution.py:181
  241.7 19.0 %psum.25 = f32[4,2048]{1,0:T(4,128)S(1)} all-reduce(f32[4,2048]{1,0:T(4,128)S(1)} %convolution_add_fusion), channel_id=1, replica_groups=mesh['rep'=8,'tp'=4] {'tp'}, use_global_device_ids=true, to_apply=%region_18.19 | all-reduce | flops 8192 | bytes 65536 | tf_op jit(solution)/shard_map/psum | solution.py:182
  (117 shorter events, 16.4 us)
Async XLA Ops:
  7.2 31.8 %copy-start = (bf16[2048,768]{1,0:T(8,128)(2,1)S(1)}, bf16[2048,768]{1,0:T(8,128)(2,1)}, u32[]{:S(2)}) copy-start(bf16[2048,768]{1,0:T(8,128)(2,1)} %param.35) | copy-start | bytes 9437188
  7.2 230.2 %all-reduce.3.cloned.1.call-start = ((), (), s32[]{:S(2)}) async-start(), calls=%async_computation | async-start | bytes 524288
  10.8 9.8 %copy-start.2 = (s32[4,10]{1,0:T(4,128)S(1)}, s32[4,10]{1,0:T(4,128)}, u32[]{:S(2)}) copy-start(s32[4,10]{1,0:T(4,128)} %param.30) | copy-start | bytes 484
  10.8 18.7 %copy-start.8 = (s32[32,6]{0,1:T(8,128)S(1)}, s32[32,6]{0,1:T(8,128)}, u32[]{:S(2)}) copy-start(s32[32,6]{0,1:T(8,128)} %param.43) | copy-start | bytes 2308
  16.3 22.7 %copy-start.9 = (f32[2048]{0:T(1024)S(1)}, f32[2048]{0:T(1024)}, u32[]{:S(2)}) copy-start(f32[2048]{0:T(1024)} %param.34) | copy-start | bytes 24580
  17.6 16.1 %collective-permute-start.1 = (s32[1]{0:T(128)}, s32[1]{0:T(128)}, u32[]{:S(2)}, u32[]{:S(2)}) collective-permute-start(s32[1]{0:T(128)} %dynamic_slice.54), channel_id=1, source_target_pairs={{0,16},{4,20},{8,24},{12,28},{16,0},{20,4},{24,8},{28,12},{1,17},{... | collective-permute-start | bytes 20 | tf_op jit(solution)/shard_map/ppermute | solution.py:32
  20.6 14.6 %copy-start.10 = (s32[10]{0:T(128)}, s32[10]{0:T(128)S(1)}, u32[]{:S(2)}) copy-start(s32[10]{0:T(128)S(1)} %fusion.62) | copy-start | bytes 124
  22.3 48.7 %collective-permute-start.3 = (bf16[10,64,128]{2,1,0:T(8,128)(2,1)S(1)}, bf16[10,64,128]{2,1,0:T(8,128)(2,1)S(1)}, u32[]{:S(2)}, u32[]{:S(2)}) collective-permute-start(bf16[10,64,128]{2,1,0:T(8,128)(2,1)S(1)} %gather_fusion.2), channel_id=1, source_target_pairs={{0,16},{4,20},{8,24},{12,28},{16,0},{20,4},{24,8},{28,12},{1,17},{... | collective-permute-start | bytes 491528 | tf_op jit(solution)/shard_map/ppermute | solution.py:32
  23.0 14.4 %collective-permute-start = (bf16[1,2048]{1,0:T(2,128)(2,1)}, bf16[1,2048]{1,0:T(2,128)(2,1)}, u32[]{:S(2)}, u32[]{:S(2)}) collective-permute-start(bf16[1,2048]{1,0:T(2,128)(2,1)} %constant_dynamic-slice_fusion.4), channel_id=1, source_target_pairs={{0,16},{4,20},{8,24},{12,28},{16,0},{20,4},{24,8},{28,12},{1,17},{... | collective-permute-start | bytes 12296 | tf_op jit(solution)/shard_map/ppermute | solution.py:32
  29.2 46.4 %collective-permute-start.2 = (bf16[10,128,512]{2,1,0:T(8,128)(2,1)}, bf16[10,128,512]{2,1,0:T(8,128)(2,1)}, u32[]{:S(2)}, u32[]{:S(2)}) collective-permute-start(bf16[10,128,512]{2,1,0:T(8,128)(2,1)} %gather_fusion), channel_id=1, source_target_pairs={{0,16},{4,20},{8,24},{12,28},{16,0},{20,4},{24,8},{28,12},{1,17},{... | collective-permute-start | bytes 3932168 | tf_op jit(solution)/shard_map/ppermute | solution.py:32
  35.2 0.7 copy-start.12
  37.3 20.1 %copy-start.13 = (f32[512]{0:T(512)S(1)}, f32[512]{0:T(512)}, u32[]{:S(2)}) copy-start(f32[512]{0:T(512)} %param.37) | copy-start | bytes 6148
  39.0 32.0 %copy-start.11 = (s32[10]{0:T(128)S(1)}, s32[10]{0:T(128)}, u32[]{:S(2)}) copy-start(s32[10]{0:T(128)} %copy-done.10) | copy-start | bytes 124
  39.6 31.4 %copy-start.4 = (bf16[40,64,128]{2,1,0:T(8,128)(2,1)S(1)}, bf16[40,64,128]{2,1,0:T(8,128)(2,1)}, u32[]{:S(2)}) copy-start(bf16[40,64,128]{2,1,0:T(8,128)(2,1)} %copy.152) | copy-start | bytes 1966084
  88.4 28.3 %copy-start.3 = (bf16[40,128,512]{2,1,0:T(8,128)(2,1)S(1)}, bf16[40,128,512]{2,1,0:T(8,128)(2,1)}, u32[]{:S(2)}) copy-start(bf16[40,128,512]{2,1,0:T(8,128)(2,1)} %gather_fusion.1) | copy-start | bytes 15728644
  116.7 16.6 %copy-start.5 = (bf16[512,2048]{1,0:T(8,128)(2,1)S(1)}, bf16[512,2048]{1,0:T(8,128)(2,1)}, u32[]{:S(2)}) copy-start(bf16[512,2048]{1,0:T(8,128)(2,1)} %param.40) | copy-start | bytes 6291460
  117.6 34.5 %copy-start.7 = (f32[2048]{0:T(1024)S(1)}, f32[2048]{0:T(1024)}, u32[]{:S(2)}) copy-start(f32[2048]{0:T(1024)} %param.41) | copy-start | bytes 24580
  132.5 29.2 %copy-start.6 = (bf16[2048,64]{0,1:T(8,128)(2,1)S(1)}, bf16[2048,64]{0,1:T(8,128)(2,1)}, u32[]{:S(2)}) copy-start(bf16[2048,64]{0,1:T(8,128)(2,1)} %param.42) | copy-start | bytes 786436
  161.9 1.9 copy-start.14
  186.2 75.1 %copy-start.1 = (bf16[2048,768]{1,0:T(8,128)(2,1)S(1)}, bf16[2048,768]{1,0:T(8,128)(2,1)}, u32[]{:S(2)}) copy-start(bf16[2048,768]{1,0:T(8,128)(2,1)} %param.35) | copy-start | bytes 9437188
Sparse Core Ops, SparseCore 0:
  186.3 50.9 all-reduce.2
where the time goes:
time: 269 us; the launch traced here: 268 us
  blocking collectives  111 us (41%)
  waiting for transfers between devices  46.2 us (17%)
  local copies, waits for them, and re-layouts  41.2 us (15%)
  matrix products  39.9 us (15%)
  between operations  15.8 us (6%)
  other arithmetic  8.72 us (3%)
  starting transfers between devices  5.1 us (2%)
    unnamed x2, waiting for transfers between devices  46.2 us
    all_gather x3, blocking collectives, joined(): gathered = jax.tree.map(lambda a: lax.all_gather(a, axis), part)  38.7 us
    psum x1, blocking collectives, body(): routed_all, shared_all = lax.psum((routed, shared_part), 'tp')  19 us
    psum x1, blocking collectives, body(): attn = lax.psum(partial_out, 'tp')  17 us
    all_gather x1, blocking collectives, body(): all_lat = lax.all_gather(q_lat, 'tp', axis=1, tiled=True)  13.9 us
    all_gather x1, blocking collectives, body(): all_pos = lax.all_gather(q_pos, 'tp', axis=1, tiled=True)  13.1 us
    dot_general x1, matrix products, body(): jnp.einsum('erf,efd->erd', hid, expert_down, preferred_element_type=f32)  12.9 us
    unnamed x40, local copies, waits for them, and re-layouts  11.8 us
  transfers between devices with their start and end apart: 5, of which 1 were waited for; matrix products, arithmetic and copies ran while one was open for 11% of the time, Pallas kernels for 0%

commit v1 on v0

v1 whole, which is shorter than its diff:
```python
import functools

import jax
import jax.numpy as jnp
from jax import lax
from jax.experimental import pallas as pl
from jax.experimental.pallas import tpu as pltpu
from jax.sharding import PartitionSpec as P

NOPE = 128
ROPE = 64
SINKS = 4
WIN = 4096
PAGE = 128
LANES = 128
ROWS = 16
EPS = 1e-06
ROUTE_SCALE = 2.446
NEG = -1e30
F32 = jnp.float32
BF16 = jnp.bfloat16
NT = (((1,), (1,)), ((), ()))

VMEM = pl.BlockSpec(memory_space=pltpu.VMEM)
SMEM = pl.BlockSpec(memory_space=pltpu.SMEM)
ANY = pl.BlockSpec(memory_space=pl.ANY)


def xored(value, axis, mask):
    pairs = [(source, source ^ mask) for source in range(lax.axis_size(axis))]
    return lax.ppermute(value, axis, pairs)


def call(kernel, out_shape, in_specs, out_specs, scratch=(), vmem=8, flops=0, nbytes=0, aliases=None):
    return pl.pallas_call(
        kernel,
        out_shape=out_shape,
        in_specs=in_specs,
        out_specs=out_specs,
        scratch_shapes=list(scratch),
        input_output_aliases=aliases or {},
        compiler_params=pltpu.CompilerParams(vmem_limit_bytes=vmem * 1024 * 1024),
        cost_estimate=pl.CostEstimate(flops=flops, bytes_accessed=nbytes, transcendentals=0),
    )


def struct(shape, dtype):
    return jax.ShapeDtypeStruct(shape, dtype)


def in_hbm(value):
    return pltpu.with_memory_space_constraint(value, pltpu.HBM)


def rms_norm(values, gain):
    return values * lax.rsqrt(jnp.mean(values * values, axis=-1, keepdims=True) + EPS) * gain


def silu(value):
    return value / (1.0 + jnp.exp(-value))


def query_kernel(
    first, table_in, slot_in, x_in, gain_in, w_in, key_in, lat, rope,
    q_out, normed_out, lat_out, rope_out,
    table, slot, x, gain, w_query, key_up, sems, in_sems,
):
    per_dev = table.shape[1]
    size = x.shape[1]
    parts = in_sems.shape[0] - 5
    step = size // parts
    small = [
        pltpu.make_async_copy(source, target, in_sems.at[i])
        for i, (source, target) in enumerate(
            [(table_in, table), (slot_in, slot), (x_in, x), (gain_in, gain)]
        )
    ]
    for copy in small:
        copy.start()
    big = []
    for i in range(parts):
        piece = pl.ds(i * step, step)
        big.append(pltpu.make_async_copy(w_in.at[piece], w_query.at[piece], in_sems.at[4 + i]))
    big.append(pltpu.make_async_copy(key_in, key_up, in_sems.at[4 + parts]))
    for copy in big:
        copy.start()
    small[0].wait()
    small[1].wait()
    copies = []
    for j in range(per_dev):
        page = table[slot[0], j]
        if j < first:
            copies.append(pltpu.make_async_copy(lat.at[page], lat_out.at[j], sems.at[0, j]))
        copies.append(pltpu.make_async_copy(rope.at[page], rope_out.at[j], sems.at[1, j]))
    for copy in copies:
        copy.start()
    small[2].wait()
    small[3].wait()
    normed = rms_norm(x[...].astype(F32), gain[...]).astype(BF16)
    normed_out[...] = normed
    heads, nope, _ = key_up.shape
    query = None
    for i in range(parts):
        big[i].wait()
        piece = slice(i * step, (i + 1) * step)
        term = jnp.dot(normed[:, piece], w_query[piece, :], preferred_element_type=F32)
        query = term if query is None else query + term
    big[parts].wait()
    wide = query.shape[1] // heads
    rows = []
    for h in range(heads):
        one = query[:, h * wide : (h + 1) * wide]
        q_lat = jnp.dot(one[:, :nope].astype(BF16), key_up[h], preferred_element_type=F32)
        rows.append(jnp.concatenate([q_lat, one[:, nope:]], axis=1))
    q_out[...] = jnp.concatenate(rows, axis=0).astype(BF16)
    for copy in copies:
        copy.wait()


def fetch_kernel(
    table, lengths, normed, gain, w_latent, lat, rope,
    lat_v, rope_v, new_out, latent_v, sems, w_sem,
):
    requests, per_dev = table.shape
    weights = pltpu.make_async_copy(w_latent, latent_v, w_sem.at[0])
    weights.start()
    copies = []
    for r in range(requests):
        for j in range(per_dev):
            n = r * per_dev + j
            page = table[r, j]
            copies.append(pltpu.make_async_copy(lat.at[page], lat_v.at[n], sems.at[0, n]))
            copies.append(pltpu.make_async_copy(rope.at[page], rope_v.at[n], sems.at[1, n]))
    for copy in copies:
        copy.start()
    size = gain.shape[1]
    weights.wait()
    latent = lax.dot_general(normed[...], latent_v[...], NT, preferred_element_type=F32)
    c_new = rms_norm(latent[:, :size], gain[...]).astype(BF16).astype(F32)
    p_new = latent[:, size:].astype(BF16).astype(F32)
    lane = lax.broadcasted_iota(jnp.int32, (1, LANES), 1)
    marks = []
    for r in range(requests):
        page = jnp.full((1, LANES), lengths[r] // PAGE, jnp.int32)
        inside = jnp.full((1, LANES), lengths[r] % PAGE, jnp.int32)
        marks.append(jnp.where(lane == 0, page, jnp.where(lane == 1, inside, 0)))
    mark = jnp.concatenate(marks, axis=0).astype(F32)
    new = jnp.concatenate([c_new, p_new, mark[:, : LANES - ROPE]], axis=1)
    new_out[...] = new
    for copy in copies:
        copy.wait()


def attention_kernel(blocks, per_dev, requests, lat_size, *refs):
    lengths, rank = refs[:2]
    queries = refs[2 : 2 + blocks]
    lat, rope, value_up, w_out = refs[2 + blocks : 6 + blocks]
    outs = refs[6 + blocks : 6 + 2 * blocks]
    value_v, out_v, q_all, result, sems = refs[6 + 2 * blocks :]
    weights_in = [
        pltpu.make_async_copy(value_up, value_v, sems.at[0]),
        pltpu.make_async_copy(w_out, out_v, sems.at[1]),
    ]
    for copy in weights_in:
        copy.start()
    rows = queries[0].shape[0]
    heads = blocks * rows // requests
    scale = (NOPE + ROPE) ** (-0.5)
    tiles = lat_size // LANES
    for k in range(blocks):
        block = queries[k][...].astype(F32)
        for i in range(tiles + 1):
            piece = block[:, i * LANES : (i + 1) * LANES]
            q_all[i, k * rows : (k + 1) * rows, : piece.shape[1]] = piece
    base = rank[0] * (per_dev * PAGE)
    side = lax.broadcasted_iota(jnp.int32, (heads, LANES), 1)

    def attend(r, count):
        mine = pl.ds(r, heads, stride=requests)
        length = lengths[r]
        q_lat = jnp.concatenate([q_all[i, mine, :] for i in range(tiles)], axis=1).astype(BF16)
        q_pos = q_all[tiles, mine, :][:, :ROPE].astype(BF16)
        start = r * per_dev
        latents = lat[start : start + count].reshape(count * PAGE, lat_size)
        scores = lax.dot_general(q_lat, latents, NT, preferred_element_type=F32)
        scores += jnp.concatenate(
            [
                jnp.dot(q_pos, rope[start + j], preferred_element_type=F32)
                for j in range(count)
            ],
            axis=1,
        )
        scores *= scale
        position = base + lax.broadcasted_iota(jnp.int32, scores.shape, 1)
        allowed = (position < length) & ((position < SINKS) | (position >= length + 1 - WIN))
        peak = jnp.max(jnp.where(allowed, scores, NEG), axis=1, keepdims=True)
        weights = jnp.where(allowed, jnp.exp(scores - peak), 0.0).astype(BF16)
        total = jnp.sum(weights.astype(F32), axis=1, keepdims=True)
        sums = jnp.dot(weights, latents, preferred_element_type=F32)
        for i in range(tiles):
            result[i, mine, :] = sums[:, i * LANES : (i + 1) * LANES]
        result[tiles, mine, :] = jnp.where(side < LANES // 2, peak, total)

    few = min(2, per_dev)
    for r in range(requests):
        length = lengths[r]
        past = length <= base
        short = length <= base + few * PAGE

        @pl.when(past)
        def _():
            mine = pl.ds(r, heads, stride=requests)
            for i in range(tiles):
                result[i, mine, :] = jnp.zeros((heads, LANES), F32)
            result[tiles, mine, :] = jnp.where(side < LANES // 2, NEG, 0.0)

        @pl.when(jnp.logical_not(past) & short)
        def _():
            attend(r, few)

        @pl.when(jnp.logical_not(short))
        def _():
            attend(r, per_dev)

    for k in range(blocks):
        for i in range(tiles + 1):
            outs[k][:, i * LANES : (i + 1) * LANES] = result[i, k * rows : (k + 1) * rows, :]
    for copy in weights_in:
        copy.wait()


def finish_kernel(blocks, requests, lat_size, *refs):
    parts = refs[:blocks]
    query, new, value_up, w_out, out = refs[blocks:]
    local_heads = value_up.shape[0]
    scale = (NOPE + ROPE) ** (-0.5)
    half = lat_size + LANES // 2
    fresh = jnp.concatenate([new[:, : lat_size + ROPE]] * local_heads, axis=0)
    q_own = query[...].astype(F32)
    new_score = jnp.sum(q_own * fresh, axis=1, keepdims=True) * scale
    peak = new_score
    for part in parts:
        peak = jnp.maximum(peak, part[:, lat_size : lat_size + 1])
    new_factor = jnp.exp(new_score - peak)
    denom = new_factor
    numer = new_factor * fresh[:, :lat_size]
    for part in parts:
        factor = jnp.exp(part[:, lat_size : lat_size + 1] - peak)
        denom += factor * part[:, half : half + 1]
        numer += factor * part[:, :lat_size]
    o_lat = numer / denom
    vals = []
    for h in range(local_heads):
        one = o_lat[h * requests : (h + 1) * requests, :].astype(BF16)
        vals.append(jnp.dot(one, value_up[h], preferred_element_type=F32).astype(BF16))
    o_val = jnp.concatenate(vals, axis=1)
    out[...] = jnp.dot(o_val, w_out[...], preferred_element_type=F32)


def norm_kernel(blocks, *refs):
    slot = refs[0]
    parts = refs[1 : 1 + blocks]
    x, gain = refs[1 + blocks : 3 + blocks]
    row_out, h_out = refs[-2:]
    attn = parts[0][...]
    for part in parts[1:]:
        attn += part[...]
    h_one = (x[...].astype(F32) + attn).astype(BF16)
    h_out[...] = h_one
    wide = h_one.astype(F32)
    normed = rms_norm(wide, gain[...])
    mark = jnp.full((wide.shape[0], LANES), slot[0], jnp.int32).astype(F32)
    row_out[...] = jnp.concatenate([normed, mark], axis=1).astype(BF16)


def copy_pages(table, slot, lat, lat_out, sems, first, count):
    copies = [
        pltpu.make_async_copy(
            lat.at[table[slot[0], first + j]], lat_out.at[pl.ds(j * PAGE, PAGE)], sems.at[j]
        )
        for j in range(count)
    ]
    for copy in copies:
        copy.start()
    return copies


def order_kernel(groups, requests, first, count, *refs):
    table, slot, rank, route_ids, router, lat = refs[:6]
    pieces = refs[6 : 6 + groups]
    h_one, new = refs[6 + groups : 8 + groups]
    x_out, coef_out, own_out, lat_out, sems = refs[9 + groups :]
    copies = copy_pages(table, slot, lat, lat_out, sems, first, count)
    both = jnp.concatenate([h_one[...].astype(F32), new[...]], axis=1)
    row = lax.broadcasted_iota(jnp.int32, both.shape, 0)
    both = jnp.sum(jnp.where(row == slot[0], both, 0.0), axis=0, keepdims=True)
    lat_size = lat_out.shape[1]
    lines = [both[:, b : b + lat_size] for b in range(0, both.shape[1], lat_size)]
    lines[-1] = jnp.pad(lines[-1], ((0, 0), (0, lat_size - lines[-1].shape[1])))
    lines.append(jnp.zeros((ROWS - len(lines), lat_size), F32))
    lat_out[count * PAGE :, :] = jnp.concatenate(lines, axis=0).astype(BF16)
    size = router.shape[1]
    per = pieces[0].shape[0]
    rows = groups * per
    reps = rows // requests
    wide = jnp.concatenate([p[...].astype(F32) for p in pieces], axis=0)
    moved = wide[:, size : size + 1]
    other = jnp.concatenate([moved[rows // 2 :], moved[: rows // 2]], axis=0)
    row = lax.broadcasted_iota(jnp.int32, (rows, 1), 0)
    place = row // requests
    across = ((place + reps // 2) % reps) * requests
    source = jnp.where(
        row % requests == moved.astype(jnp.int32), across + other.astype(jnp.int32), row
    )
    column = lax.broadcasted_iota(jnp.int32, (rows, rows), 1)
    picks = (column == source).astype(F32).astype(BF16)
    x = jnp.dot(picks, wide[:, :size].astype(BF16), preferred_element_type=F32)
    own_out[...] = x[:requests, :].astype(BF16)
    x = x.astype(BF16)
    x_out[...] = x
    gates = jax.nn.sigmoid(lax.dot_general(x, router[...], NT, preferred_element_type=F32))
    home = (place ^ rank[0]) * requests + row % requests
    turns = (column == home).astype(F32).astype(BF16)
    ids = jnp.dot(turns, route_ids[...].astype(F32).astype(BF16), preferred_element_type=F32)
    ids = ids.astype(jnp.int32)
    expert = lax.broadcasted_iota(jnp.int32, gates.shape, 1)
    chosen = jnp.zeros(gates.shape, F32)
    for k in range(ids.shape[1]):
        chosen += jnp.where(expert == ids[:, k : k + 1], gates, 0.0)
    coef_out[...] = chosen / jnp.sum(chosen, axis=1, keepdims=True) * ROUTE_SCALE
    for copy in copies:
        copy.wait()


def expert_kernel(
    requests, chunk, hidden, rank, x, coef, gate, up, down, kept, sent, gate_v, up_v, down_v, total, sems,
):
    units = gate.shape[0]
    pieces = [slice(b, min(b + chunk, units)) for b in range(0, units, chunk)]

    def fetch(which, source, target, i):
        piece = pl.ds(pieces[i].start, pieces[i].stop - pieces[i].start)
        return pltpu.make_async_copy(source.at[piece], target.at[piece], sems.at[which, i])

    copies = [
        [fetch(w, s, t, i) for w, (s, t) in enumerate([(gate, gate_v), (up, up_v), (down, down_v)])]
        for i in range(len(pieces))
    ]
    for trio in copies:
        for copy in trio:
            copy.start()
    count = units // hidden
    first = rank[0] * count
    weights = coef[...]
    expert = lax.broadcasted_iota(jnp.int32, weights.shape, 1)
    shares = [
        jnp.sum(jnp.where(expert == first + e, weights, 0.0), axis=1, keepdims=True)
        for e in range(count)
    ]
    rows = x.shape[0]
    for i, piece in enumerate(pieces):
        copies[i][0].wait()
        gate_val = lax.dot_general(x[...], gate_v[piece, :], NT, preferred_element_type=F32)
        copies[i][1].wait()
        up_val = lax.dot_general(x[...], up_v[piece, :], NT, preferred_element_type=F32)
        unit = piece.start + lax.broadcasted_iota(jnp.int32, gate_val.shape, 1)
        low, high = piece.start // hidden, (piece.stop - 1) // hidden
        share = jnp.broadcast_to(shares[high], gate_val.shape)
        for e in range(high - 1, low - 1, -1):
            share = jnp.where(unit < (e + 1) * hidden, shares[e], share)
        hid = (silu(gate_val) * up_val * share).astype(BF16)
        copies[i][2].wait()
        term = jnp.dot(hid, down_v[piece, :], preferred_element_type=F32)
        if i == 0:
            total[...] = term
        else:
            total[...] += term
    value = total[...]
    blocks = [value[p * requests : (p + 1) * requests] for p in range(rows // requests)]
    kept[...] = jnp.concatenate(blocks[0::2], axis=0)
    sent[...] = jnp.concatenate(blocks[1::2], axis=0).astype(BF16)


def pair_kernel(requests, kept, got, _, own, *blocks):
    total = kept[...] + got[...].astype(F32)
    own[...] = total[:requests]
    for k, block in enumerate(blocks):
        block[...] = total[(k + 1) * requests : (k + 2) * requests].astype(BF16)


def shared_kernel(x, gate, up, down, _, out, gate_v, up_v, down_v, sems):
    copies = [
        pltpu.make_async_copy(gate, gate_v, sems.at[0]),
        pltpu.make_async_copy(up, up_v, sems.at[1]),
        pltpu.make_async_copy(down, down_v, sems.at[2]),
    ]
    for copy in copies:
        copy.start()
    copies[0].wait()
    gate_val = lax.dot_general(x[...], gate_v[...], NT, preferred_element_type=F32)
    copies[1].wait()
    up_val = lax.dot_general(x[...], up_v[...], NT, preferred_element_type=F32)
    hid = (silu(gate_val) * up_val).astype(BF16)
    copies[2].wait()
    out[...] = jnp.dot(hid, down_v[...], preferred_element_type=F32)


def total_kernel(first, count, table, slot, lat, own, shared, *refs):
    others, (total, lat_out, sems) = refs[:-3], refs[-3:]
    copies = copy_pages(table, slot, lat, lat_out, sems, first, count)
    value = own[...] + shared[...]
    for other in others:
        value += other[...].astype(F32)
    total[...] = value
    for copy in copies:
        copy.wait()


def token_spot(r, table, lengths, rank):
    per_dev = table.shape[1]
    local = lengths[r] // PAGE - rank[0] * per_dev
    owned = (local >= 0) & (local < per_dev)
    local = jnp.clip(local, 0, per_dev - 1)
    inside = lengths[r] % PAGE
    return owned, local, table[r, local], inside, pl.multiple_of(inside // 16 * 16, 16)


def cache_kernel(
    first, table, slot, _, lat, rope, got_lat, got_rope,
    lat_out, rope_out, token, lat_v, rope_v, got_sems, in_sems, sems,
):
    requests, per_dev = table.shape
    moved = slot[0]
    start = moved * per_dev
    fetches = [
        pltpu.make_async_copy(got_lat, lat_v.at[pl.ds(start, first)], got_sems.at[0]),
        pltpu.make_async_copy(got_rope, rope_v.at[pl.ds(start, per_dev)], got_sems.at[1]),
    ]

    def reads(r, j):
        n = r * per_dev + j
        page = table[r, j]
        return (
            pltpu.make_async_copy(lat.at[page], lat_v.at[n], in_sems.at[0, n]),
            pltpu.make_async_copy(rope.at[page], rope_v.at[n], in_sems.at[1, n]),
        )

    def lat_write(r, j):
        n = r * per_dev + j
        return pltpu.make_async_copy(lat_v.at[n], lat_out.at[table[r, j]], sems.at[0, n])

    def rope_write(r, j):
        n = r * per_dev + j
        return pltpu.make_async_copy(rope_v.at[n], rope_out.at[table[r, j]], sems.at[1, n])

    for r in range(requests):
        @pl.when(moved != r)
        def _():
            for j in range(per_dev):
                for copy in reads(r, j):
                    copy.start()

    for copy in fetches:
        copy.start()
    token[...] = jnp.zeros_like(token)
    for r in range(requests):
        @pl.when(moved != r)
        def _():
            for j in range(per_dev):
                for copy in reads(r, j):
                    copy.wait()
                lat_write(r, j).start()
                rope_write(r, j).start()

    for copy in fetches:
        copy.wait()
    for j in range(per_dev):
        if j < first:
            lat_write(moved, j).start()
        rope_write(moved, j).start()
    for r in range(requests):
        for j in range(per_dev):
            rope_write(r, j).wait()
            if j < first:
                lat_write(r, j).wait()
            else:
                @pl.when(moved != r)
                def _():
                    lat_write(r, j).wait()


def token_kernel(
    first, last, table, slot, lengths, rank, new_lat, new_rope, got, _, lat_in, rope_in,
    lat_out, rope_out, got_v, lat_tile, rope_tile, got_sem, sems, tile_sems,
):
    requests, _ = table.shape
    moved = slot[0]
    fetch = pltpu.make_async_copy(got.at[pl.ds(0, got_v.shape[0])], got_v, got_sem.at[0])
    fetch.start()
    spots = [token_spot(r, table, lengths, rank) for r in range(requests)]

    def received(r):
        local = spots[r][1]
        return (moved == r) & (local >= first) & (local < last)

    def lat_read(r):
        _, _, page, _, group = spots[r]
        return pltpu.make_async_copy(lat_in.at[page, pl.ds(group, 16), :], lat_tile.at[r], tile_sems.at[0, r])

    def rope_read(r):
        return pltpu.make_async_copy(rope_in.at[spots[r][2]], rope_tile.at[r], tile_sems.at[1, r])

    def lat_write(r):
        _, _, page, _, group = spots[r]
        return pltpu.make_async_copy(lat_tile.at[r], lat_out.at[page, pl.ds(group, 16), :], tile_sems.at[0, r])

    def rope_write(r):
        return pltpu.make_async_copy(rope_tile.at[r], rope_out.at[spots[r][2]], tile_sems.at[1, r])

    def in_pool(r):
        owned, local = spots[r][:2]
        return owned & ((moved != r) | (local < first))

    for r in range(requests):
        @pl.when(spots[r][0])
        def _():
            rope_read(r).start()

        @pl.when(in_pool(r))
        def _():
            lat_read(r).start()

    fetch.wait()
    for r in range(requests):
        owned, local, _, inside, group = spots[r]

        @pl.when(owned & received(r))
        def _():
            index = jnp.clip(local - first, 0, last - first - 1)
            piece = pl.ds(pl.multiple_of(index * PAGE + group, 16), 16)
            tile = got_v[piece, :].astype(F32)
            row = lax.broadcasted_iota(jnp.int32, tile.shape, 0)
            got_v[piece, :] = jnp.where(
                row == inside - group, new_lat[r : r + 1, :], tile
            ).astype(BF16)

    pages = [
        pltpu.make_async_copy(
            got_v.at[pl.ds(j * PAGE, PAGE)], lat_out.at[table[moved, first + j]], sems.at[j]
        )
        for j in range(last - first)
    ]
    for copy in pages:
        copy.start()
    for r in range(requests):
        owned, local, _, inside, group = spots[r]

        @pl.when(owned)
        def _():
            rope_read(r).wait()
            lane = lax.broadcasted_iota(jnp.int32, rope_tile.shape[1:], 1)
            rope_tile[r] = jnp.where(
                lane == inside, new_rope[:, r : r + 1], rope_tile[r].astype(F32)
            ).astype(BF16)
            rope_write(r).start()

        @pl.when(in_pool(r))
        def _():
            lat_read(r).wait()
            row = lax.broadcasted_iota(jnp.int32, lat_tile.shape[1:], 0)
            lat_tile[r] = jnp.where(
                row == inside - group, new_lat[r : r + 1, :], lat_tile[r].astype(F32)
            ).astype(BF16)
            lat_write(r).start()

    for r in range(requests):
        @pl.when(spots[r][0])
        def _():
            rope_write(r).wait()

        @pl.when(in_pool(r))
        def _():
            lat_write(r).wait()
    for copy in pages:
        copy.wait()


def last_kernel(first, table, slot, lengths, rank, new_lat, got, _, lat_out, pages, in_sem, sems):
    per_dev = table.shape[1]
    moved = slot[0]
    count = per_dev - first
    fetch = pltpu.make_async_copy(got, pages, in_sem.at[0])
    fetch.start()
    fetch.wait()
    owned, local, _, inside, group = token_spot(moved, table, lengths, rank)

    @pl.when(owned & (local >= first))
    def _():
        index = jnp.maximum(local - first, 0)
        piece = pl.ds(pl.multiple_of(index * PAGE + group, 16), 16)
        tile = pages[piece, :].astype(F32)
        row = lax.broadcasted_iota(jnp.int32, tile.shape, 0)
        pages[piece, :] = jnp.where(
            row == inside - group, new_lat[pl.ds(moved, 1), :], tile
        ).astype(BF16)

    copies = [
        pltpu.make_async_copy(
            pages.at[pl.ds(j * PAGE, PAGE)], lat_out.at[table[moved, first + j]], sems.at[j]
        )
        for j in range(count)
    ]
    for copy in copies:
        copy.start()
    for copy in copies:
        copy.wait()


def body(
    hidden,
    lengths,
    page_table,
    move_slot,
    lat_pool,
    rope_pool,
    norm_attn,
    w_query,
    w_latent,
    latent_gain,
    w_key_up,
    w_value_up,
    w_output,
    norm_ffn,
    w_router,
    route_ids,
    expert_gate,
    expert_up,
    expert_down,
    shared_gate,
    shared_up,
    shared_down,
):
    requests, size = hidden.shape
    per_dev = page_table.shape[1]
    local_heads, nope_size, lat_size = w_key_up.shape
    local_experts, _, units = expert_gate.shape
    n_tp, n_rep = lax.axis_size("tp"), lax.axis_size("rep")
    groups = n_rep // 2
    half = n_rep // 2
    rows = local_heads * requests
    everyone = n_rep * requests
    pages = requests * per_dev
    width = lat_size + LANES
    tp_one = lax.axis_index("tp").astype(jnp.int32)[None]
    rep_one = lax.axis_index("rep").astype(jnp.int32)[None]
    page_bytes = PAGE * (lat_size + ROPE) * 2
    dma = pltpu.SemaphoreType.DMA
    cuts = (per_dev * 6 // 10, per_dev * 8 // 10)
    first_span, second_span, third_span = cuts[0], cuts[1] - cuts[0], per_dev - cuts[1]
    lat_page = lat_pool.shape[1:]
    rope_page = rope_pool.shape[1:]
    lat_hbm, rope_hbm = in_hbm(lat_pool), in_hbm(rope_pool)
    gate_t = jnp.swapaxes(expert_gate, 1, 2).reshape(-1, size)
    up_t = jnp.swapaxes(expert_up, 1, 2).reshape(-1, size)

    q_own, normed, out_first, out_rope = call(
        functools.partial(query_kernel, first_span),
        (
            struct((rows, lat_size + ROPE), BF16),
            struct((requests, size), BF16),
            struct((first_span,) + lat_page, BF16),
            struct((per_dev,) + rope_page, BF16),
        ),
        [ANY] * 8,
        (VMEM,) * 4,
        [
            pltpu.SMEM(page_table.shape, jnp.int32),
            pltpu.SMEM((1,), jnp.int32),
            pltpu.VMEM(hidden.shape, BF16),
            pltpu.VMEM((1, size), F32),
            pltpu.VMEM(w_query.shape, BF16),
            pltpu.VMEM(w_key_up.shape, BF16),
            dma((2, per_dev)),
            dma((9,)),
        ],
        vmem=8,
        flops=2 * requests * w_query.size,
        nbytes=2 * w_query.size,
    )(
        page_table, move_slot, in_hbm(hidden), in_hbm(norm_attn[None, :]),
        in_hbm(w_query), in_hbm(w_key_up), lat_hbm, rope_hbm,
    )
    got_first = xored(out_first, "rep", half)
    got_rope = xored(out_rope, "rep", half)
    q_blocks = [q_own] + [xored(q_own, "tp", k) for k in range(1, n_tp)]

    lat_v, rope_v, new = call(
        fetch_kernel,
        (
            pltpu.VMEM((pages,) + lat_page, BF16),
            pltpu.VMEM((pages,) + rope_page, BF16),
            struct((requests, width), F32),
        ),
        [SMEM] * 2 + [VMEM] * 2 + [ANY] * 3,
        (VMEM,) * 3,
        [pltpu.VMEM((w_latent.shape[1], size), BF16), dma((2, pages)), dma((1,))],
        vmem=6,
        flops=2 * requests * w_latent.size,
        nbytes=pages * page_bytes + 2 * w_latent.size,
    )(page_table, lengths, normed, latent_gain[None, :], in_hbm(w_latent.T), lat_hbm, rope_hbm)

    *partial, value_v, out_v = call(
        functools.partial(attention_kernel, n_tp, per_dev, requests, lat_size),
        tuple(struct((rows, width), F32) for _ in range(n_tp))
        + (pltpu.VMEM(w_value_up.shape, BF16), pltpu.VMEM(w_output.shape, BF16)),
        [SMEM, SMEM] + [VMEM] * (n_tp + 2) + [ANY, ANY],
        (VMEM,) * (n_tp + 2),
        [pltpu.VMEM((width // LANES, n_tp * rows, LANES), F32)] * 2 + [dma((2,))],
        vmem=6,
        flops=4 * n_tp * rows * per_dev * PAGE * lat_size,
        nbytes=pages * page_bytes,
    )(lengths, tp_one, *q_blocks, lat_v, rope_v, in_hbm(w_value_up), in_hbm(w_output))
    parts = [partial[0]] + [xored(partial[k], "tp", k) for k in range(1, n_tp)]

    out_part = call(
        functools.partial(finish_kernel, n_tp, requests, lat_size),
        struct((requests, size), F32),
        [VMEM] * (n_tp + 4),
        VMEM,
        vmem=4,
        flops=2 * requests * size * w_output.shape[0],
        nbytes=2 * w_output.size + 2 * w_value_up.size,
    )(*parts, q_own, new, value_v, out_v)
    out_parts = [out_part] + [xored(out_part, "tp", k) for k in range(1, n_tp)]

    ffn_row, h_one = call(
        functools.partial(norm_kernel, n_tp),
        (
            struct((requests, size + LANES), BF16),
            struct((requests, size), BF16),
        ),
        [SMEM] + [VMEM] * (n_tp + 2) + [ANY] * 2,
        (VMEM,) * 2,
        vmem=4,
        nbytes=8 * n_tp * requests * size,
    )(move_slot, *out_parts, hidden, norm_ffn[None, :], got_first, got_rope)

    pair = jnp.concatenate([ffn_row, xored(ffn_row, "rep", 1)], axis=0)
    pieces = [pair] + [xored(pair, "rep", 2 * k) for k in range(1, groups)]

    lat_most, rope_most, cache_token = call(
        functools.partial(cache_kernel, first_span),
        (struct(lat_pool.shape, BF16), struct(rope_pool.shape, BF16), struct((8, LANES), F32)),
        [SMEM] * 2 + [VMEM] + [ANY] * 4,
        (ANY, ANY, VMEM),
        [
            pltpu.VMEM((pages,) + lat_page, BF16),
            pltpu.VMEM((pages,) + rope_page, BF16),
            dma((2,)),
            dma((2, pages)),
            dma((2, pages)),
        ],
        vmem=8,
        nbytes=2 * pages * page_bytes,
    )(page_table, move_slot, pair, lat_hbm, rope_hbm, got_first, got_rope)

    x_all, coef, x_own, out_second = call(
        functools.partial(order_kernel, groups, requests, cuts[0], second_span),
        (
            struct((everyone, size), BF16),
            struct((everyone, w_router.shape[1]), F32),
            struct((requests, size), BF16),
            struct((second_span * PAGE + ROWS, lat_size), BF16),
        ),
        [SMEM] * 3 + [VMEM] * 2 + [ANY] + [VMEM] * (groups + 3),
        (VMEM,) * 4,
        [dma((second_span,))],
        vmem=6,
        flops=4 * everyone * size * everyone,
        nbytes=4 * everyone * size,
    )(page_table, move_slot, rep_one, route_ids, w_router.T, lat_hbm, *pieces, h_one, new, cache_token)
    got_second = xored(out_second, "rep", half)
    got_row = got_second[second_span * PAGE :].reshape(1, -1)[:, : size + width]

    kept, sent = call(
        functools.partial(expert_kernel, requests, 256, units),
        (struct((groups * requests, size), F32), struct((groups * requests, size), BF16)),
        [SMEM] + [VMEM] * 2 + [ANY] * 3,
        (VMEM, VMEM),
        [pltpu.VMEM((local_experts * units, size), BF16)] * 3
        + [pltpu.VMEM((everyone, size), F32), dma((3, pl.cdiv(local_experts * units, 256)))],
        vmem=40,
        flops=6 * everyone * expert_gate.size,
        nbytes=6 * expert_gate.size,
    )(
        rep_one, x_all, coef,
        in_hbm(gate_t),
        in_hbm(up_t),
        in_hbm(expert_down.reshape(-1, size)),
    )
    summed = call(
        functools.partial(pair_kernel, requests),
        (struct((requests, size), F32),) + (struct((requests, size), BF16),) * (groups - 1),
        [VMEM, VMEM, ANY],
        (VMEM,) * groups,
        vmem=4,
        nbytes=8 * everyone * size,
    )(kept, xored(sent, "rep", 1), got_second)
    others = [xored(summed[k], "rep", 2 * k) for k in range(1, groups)]
    shared_part = call(
        shared_kernel,
        struct((requests, size), F32),
        [VMEM] + [ANY] * 4,
        VMEM,
        [
            pltpu.VMEM((shared_gate.shape[1], size), BF16),
            pltpu.VMEM((shared_gate.shape[1], size), BF16),
            pltpu.VMEM(shared_down.shape, BF16),
            dma((3,)),
        ],
        vmem=12,
        flops=6 * requests * shared_gate.size,
        nbytes=6 * shared_gate.size,
    )(x_own, in_hbm(shared_gate.T), in_hbm(shared_up.T), in_hbm(shared_down), summed[0])
    total, out_third = call(
        functools.partial(total_kernel, cuts[1], third_span),
        (struct((requests, size), F32), struct((third_span * PAGE, lat_size), BF16)),
        [SMEM, SMEM, ANY] + [VMEM] * (groups + 1),
        (VMEM, VMEM),
        [dma((third_span,))],
        vmem=4,
        nbytes=8 * everyone * size,
    )(page_table, move_slot, lat_hbm, summed[0], shared_part, *others)
    got_third = xored(out_third, "rep", half)

    is_moved = (jnp.arange(requests, dtype=jnp.int32) == move_slot[0])[:, None]
    new_served = jnp.where(is_moved, got_row[:, size:].astype(F32), new)
    marks = new_served[:, lat_size + ROPE : lat_size + ROPE + 2].astype(jnp.int32)
    len_served = marks[:, 0] * PAGE + marks[:, 1]
    lat_new = new_served[:, :lat_size]
    rope_new = new_served[:, lat_size : lat_size + ROPE].T
    lat_most, rope_cache = call(
        functools.partial(token_kernel, cuts[0], cuts[1]),
        (struct(lat_pool.shape, BF16), struct(rope_pool.shape, BF16)),
        [SMEM] * 4 + [VMEM] * 2 + [ANY, VMEM] + [ANY] * 2,
        (ANY, ANY),
        [
            pltpu.VMEM((second_span * PAGE, lat_size), BF16),
            pltpu.VMEM((requests, 16, lat_size), BF16),
            pltpu.VMEM((requests,) + rope_page, BF16),
            dma((1,)),
            dma((second_span,)),
            dma((2, requests)),
        ],
        vmem=2,
        nbytes=2 * second_span * page_bytes,
        aliases={8: 0, 9: 1},
    )(
        page_table, move_slot, len_served, tp_one, lat_new, rope_new, got_second, total,
        lat_most, rope_most,
    )

    total_all = total
    for other in [xored(total, "tp", k) for k in range(1, n_tp)]:
        total_all = total_all + other
    h_served = jnp.where(is_moved, got_row[:, :size], h_one)
    mixed = (h_served.astype(F32) + total_all).astype(BF16)

    lat_cache = call(
        functools.partial(last_kernel, cuts[1]),
        struct(lat_pool.shape, BF16),
        [SMEM] * 4 + [VMEM] + [ANY] * 2,
        ANY,
        [pltpu.VMEM((third_span * PAGE, lat_size), BF16), dma((1,)), dma((third_span,))],
        vmem=2,
        nbytes=2 * third_span * page_bytes,
        aliases={6: 0},
    )(page_table, move_slot, len_served, tp_one, lat_new, got_third, lat_most)
    return (mixed, lat_cache, rope_cache)


def solution(mesh):
    in_specs = (
        P("rep", None),
        P("rep"),
        P("rep", "tp"),
        P("rep"),
        P(("rep", "tp"), None, None),
        P(("rep", "tp"), None, None),
        P(),
        P(None, "tp"),
        P(),
        P(),
        P("tp", None, None),
        P("tp", None, None),
        P("tp", None),
        P(),
        P(),
        P(),
        P("rep", None, "tp"),
        P("rep", None, "tp"),
        P("rep", "tp", None),
        P(None, "tp"),
        P(None, "tp"),
        P("tp", None),
    )
    out_specs = (P("rep", None), P(("rep", "tp"), None, None), P(("rep", "tp"), None, None))
    return jax.shard_map(body, mesh=mesh, in_specs=in_specs, out_specs=out_specs, check_vma=False)
```

time: 269 us -> 96.6 us (0.36)
  blocking collectives: 111 us -> 0 us
  Pallas kernels: 0 us -> 48.5 us
  local copies, waits for them, and re-layouts: 41.2 us -> 0.96 us
  matrix products: 39.9 us -> 0 us
  waiting for transfers between devices: 46.2 us -> 13.7 us
  starting transfers between devices: 5.1 us -> 30.5 us
  between operations: 15.8 us -> 1.77 us
  other arithmetic: 8.72 us -> 1.06 us
    all_gather x6 -> x0, blocking collectives: 75.2 us -> none  [the longest x3 38.7 us: joined(): gathered = jax.tree.map(lambda a: lax.all_gather(a, axis), part)]
    pallas_call x0 -> x13, Pallas kernels: none -> 48.5 us  [the longest x1 18.3 us: body(): call(functools.partial(expert_kernel, requests, 256, units), (struct((gro...]
    unnamed x2 -> x0, waiting for transfers between devices: 46.2 us -> none
    dot_general x13 -> x0, matrix products: 39.9 us -> none  [the longest x1 12.9 us: body(): jnp.einsum('erf,efd->erd', hid, expert_down, preferred_element_type=f32)]
    psum x2 -> x0, blocking collectives: 36 us -> none  [the longest x1 19 us: body(): routed_all, shared_all = lax.psum((routed, shared_part), 'tp')]
    ppermute x4 -> x24, starting transfers between devices: 5.06 us -> 30.5 us  [xored(): return lax.ppermute(value, axis, pairs)]
    gather x10 -> x0, local copies, waits for them, and re-layouts: 16.3 us -> none  [the longest x1 7.11 us: body(): lat_rows = moved_lat[page_table]]
    ppermute x4 -> x24, waiting for transfers between devices: 0.01 us -> 13.7 us  [xored(): return lax.ppermute(value, axis, pairs)]
  transfers between devices with their start and end apart: 5 -> 24, of which waited for: 1 -> 8; matrix products, arithmetic and copies ran while one was open for 11% -> 1% of each run, Pallas kernels for 0% -> 42%
where the time goes in v1:
time: 96.6 us; the launch traced here: 96.5 us
  Pallas kernels  48.5 us (50%)
  starting transfers between devices  30.5 us (32%)
  waiting for transfers between devices  13.7 us (14%)
  between operations  1.77 us (2%)
  other arithmetic  1.06 us (1%)
    ppermute x24, starting transfers between devices, xored(): return lax.ppermute(value, axis, pairs)  30.5 us
    pallas_call x1, Pallas kernels, body(): call(functools.partial(expert_kernel, requests, 256, units), (struct((gro...  18.3 us
    ppermute x24, waiting for transfers between devices, xored(): return lax.ppermute(value, axis, pairs)  13.7 us
    pallas_call x1, Pallas kernels, body(): call(functools.partial(cache_kernel, first_span), (struct(lat_pool.shape,...  6.54 us
    pallas_call x1, Pallas kernels, body(): call(fetch_kernel, (pltpu.VMEM((pages,) + lat_page, BF16), pltpu.VMEM((pa...  5.85 us
    pallas_call x1, Pallas kernels, body(): call(shared_kernel, struct((requests, size), F32), [VMEM] + [ANY] * 4, VM...  4.46 us
    pallas_call x1, Pallas kernels, body(): call(functools.partial(query_kernel, first_span), (struct((rows, lat_size...  2.7 us
    pallas_call x1, Pallas kernels, body(): call(functools.partial(attention_kernel, n_tp, per_dev, requests, lat_siz...  2.65 us
  transfers between devices with their start and end apart: 24, of which 8 were waited for; matrix products, arithmetic and copies ran while one was open for 1% of the time, Pallas kernels for 42%

profile of v1, /device:TPU:0, one launch (start us, length us, event | category | flops | bytes accessed | tf_op | source)
XLA Modules:
  0.0 96.5 jit_solution(193957935038154153)
XLA Ops:
  2.0 2.7 %shard_map.229 = (bf16[16,576]{1,0:T(8,128)(2,1)S(1)}, bf16[4,2048]{1,0:T(4,128)(2,1)S(1)}, bf16[6,128,512]{2,1,0:T(8,128)(2,1)S(1)}, bf16[10,64,128]{2,1,0:T(8,128)(2,1)S(1)}) custom-call(s32[4,10]{1,0:T(4,128)S(1)} %copy-done.1, s32[1]{0:T(128)} %copy.36.slot_in.refs_0_.slot.refs_1_, bf16[4,2048]{1,0:T(4,128)(2,1)} %refs_5_.2, f32[1,2048]{1,0:T(1,128)} %bitcast.35, ...), custom_call_target="tpu_custom_call" | custom-call | flops 12582912 | bytes 3145728 | tf_op jit(solution)/shard_map/pallas_call | solution.py:666
  4.7 3.0 %collective-permute-start.9 = (bf16[6,128,512]{2,1,0:T(8,128)(2,1)S(1)}, bf16[6,128,512]{2,1,0:T(8,128)(2,1)S(1)}, u32[]{:S(2)}, u32[]{:S(2)}) collective-permute-start(bf16[6,128,512]{2,1,0:T(8,128)(2,1)S(1)} %get-tuple-element.46), channel_id=1, source_target_pairs={{0,16},{4,20},{8,24},{12,28},{16,0},{20,4},{24,8},{28,12},{1,17},{... | collective-permute-start | bytes 2359304 | tf_op jit(solution)/shard_map/ppermute | solution.py:31
  7.8 2.0 %collective-permute-start = (bf16[16,576]{1,0:T(8,128)(2,1)S(1)}, bf16[16,576]{1,0:T(8,128)(2,1)S(1)}, u32[]{:S(2)}, u32[]{:S(2)}) collective-permute-start(bf16[16,576]{1,0:T(8,128)(2,1)S(1)} %get-tuple-element.35.refs_2_.refs_4_), channel_id=1, source_target_pairs={{0,1},{1,0},{2,3},{3,2},{4,5},{5,4},{6,7},{7,6},{8,9},{9,8},{10,11... | collective-permute-start | bytes 55304 | tf_op jit(solution)/shard_map/ppermute | solution.py:31
  9.8 2.6 %collective-permute-start.1 = (bf16[16,576]{1,0:T(8,128)(2,1)S(1)}, bf16[16,576]{1,0:T(8,128)(2,1)S(1)}, u32[]{:S(2)}, u32[]{:S(2)}) collective-permute-start(bf16[16,576]{1,0:T(8,128)(2,1)S(1)} %get-tuple-element.35.refs_2_.refs_4_), channel_id=1, source_target_pairs={{0,2},{1,3},{2,0},{3,1},{4,6},{5,7},{6,4},{7,5},{8,10},{9,11},{10,... | collective-permute-start | bytes 55304 | tf_op jit(solution)/shard_map/ppermute | solution.py:31
  12.4 5.8 %shard_map.230 = (bf16[40,128,512]{2,1,0:T(8,128)(2,1)S(1)}, bf16[40,64,128]{2,1,0:T(8,128)(2,1)S(1)}, f32[4,640]{1,0:T(4,128)S(1)}) custom-call(s32[4,10]{1,0:T(4,128)S(1)} %copy-done.2, s32[4]{0:T(128)S(1)} %copy-done.6, bf16[4,2048]{1,0:T(4,128)(2,1)S(1)} %get-tuple-element.36.normed, f32[1,512]{1,0:T(1,128)S(1)} %bitcast.26, bf16[576,2048]{1,0:T(8,128)(2,1)} %bitcast.32, ...), custom_call_target="tpu_custom_call" | custom-call | flops 9437184 | bytes 8257536 | tf_op jit(solution)/shard_map/pallas_call | solution.py:697
  18.4 2.6 %shard_map.231 = (f32[16,640]{1,0:T(8,128)S(1)}, f32[16,640]{1,0:T(8,128)S(1)}, f32[16,640]{1,0:T(8,128)S(1)}, f32[16,640]{1,0:T(8,128)S(1)}, bf16[4,512,128]{2,...) custom-call(s32[4]{0:T(128)S(1)} %copy-done.6, s32[1]{0:T(128)} %bitcast.3.refs_1_.rank, ...), custom_call_target="tpu_custom_call" | custom-call | flops 167772160 | bytes 5898240 | tf_op jit(solution)/shard_map/pallas_call | solution.py:712
  21.6 3.5 %collective-permute-start.4 = (f32[16,640]{1,0:T(8,128)S(1)}, f32[16,640]{1,0:T(8,128)S(1)}, u32[]{:S(2)}, u32[]{:S(2)}) collective-permute-start(f32[16,640]{1,0:T(8,128)S(1)} %get-tuple-element.41), channel_id=1, source_target_pairs={{0,2},{1,3},{2,0},{3,1},{4,6},{5,7},{6,4},{7,5},{8,10},{9,11},{10,... | collective-permute-start | bytes 122888 | tf_op jit(solution)/shard_map/ppermute | solution.py:31
  25.5 2.5 %collective-permute-done.4.refs_2_ = f32[16,640]{1,0:T(8,128)S(1)} collective-permute-done((f32[16,640]{1,0:T(8,128)S(1)}, f32[16,640]{1,0:T(8,128)S(1)}, u32[]{:S(2)}, u32[]{:S(2)}) %collective-permute-start.4) | collective-permute-done | bytes 40992 | tf_op jit(solution)/shard_map/ppermute | solution.py:31
  28.0 2.9 %collective-permute-done.5.refs_3_ = f32[16,640]{1,0:T(8,128)S(1)} collective-permute-done((f32[16,640]{1,0:T(8,128)S(1)}, f32[16,640]{1,0:T(8,128)S(1)}, u32[]{:S(2)}, u32[]{:S(2)}) %collective-permute-start.5) | collective-permute-done | bytes 40992 | tf_op jit(solution)/shard_map/ppermute | solution.py:31
  31.6 1.0 %collective-permute-start.7 = (f32[4,2048]{1,0:T(4,128)S(1)}, f32[4,2048]{1,0:T(4,128)S(1)}, u32[]{:S(2)}, u32[]{:S(2)}) collective-permute-start(f32[4,2048]{1,0:T(4,128)S(1)} %shard_map.232.refs_1_), channel_id=1, source_target_pairs={{0,2},{1,3},{2,0},{3,1},{4,6},{5,7},{6,4},{7,5},{8,10},{9,11},{10,... | collective-permute-start | bytes 98312 | tf_op jit(solution)/shard_map/ppermute | solution.py:31
  32.6 3.4 %collective-permute-start.8 = (f32[4,2048]{1,0:T(4,128)S(1)}, f32[4,2048]{1,0:T(4,128)S(1)}, u32[]{:S(2)}, u32[]{:S(2)}) collective-permute-start(f32[4,2048]{1,0:T(4,128)S(1)} %shard_map.232.refs_1_), channel_id=1, source_target_pairs={{0,3},{1,2},{2,1},{3,0},{4,7},{5,6},{6,5},{7,4},{8,11},{9,10},{10,... | collective-permute-start | bytes 98312 | tf_op jit(solution)/shard_map/ppermute | solution.py:31
  36.5 1.9 %collective-permute-done.8.refs_4_ = f32[4,2048]{1,0:T(4,128)S(1)} collective-permute-done((f32[4,2048]{1,0:T(4,128)S(1)}, f32[4,2048]{1,0:T(4,128)S(1)}, u32[]{:S(2)}, u32[]{:S(2)}) %collective-permute-start.8) | collective-permute-done | bytes 32800 | tf_op jit(solution)/shard_map/ppermute | solution.py:31
  38.6 1.2 %collective-permute-done.11 = bf16[4,2176]{1,0:T(4,128)(2,1)S(1)} collective-permute-done((bf16[4,2176]{1,0:T(4,128)(2,1)S(1)}, bf16[4,2176]{1,0:T(4,128)(2,1)S(1)}, u32[]{:S(2)}, u32[]{:S(2)}) %collective-permute-start.11) | collective-permute-done | bytes 17440 | tf_op jit(solution)/shard_map/ppermute | solution.py:31
  39.8 2.1 %collective-permute-start.12 = (bf16[8,2176]{1,0:T(8,128)(2,1)S(1)}, bf16[8,2176]{1,0:T(8,128)(2,1)S(1)}, u32[]{:S(2)}, u32[]{:S(2)}) collective-permute-start(bf16[8,2176]{1,0:T(8,128)(2,1)S(1)} %pad_maximum_fusion._.refs_6_), channel_id=1, source_target_pairs={{0,8},{4,12},{8,0},{12,4},{16,24},{20,28},{24,16},{28,20},{1,9},{5... | collective-permute-start | bytes 104456 | tf_op jit(solution)/shard_map/ppermute | solution.py:31
  41.9 1.1 %collective-permute-start.13 = (bf16[8,2176]{1,0:T(8,128)(2,1)S(1)}, bf16[8,2176]{1,0:T(8,128)(2,1)S(1)}, u32[]{:S(2)}, u32[]{:S(2)}) collective-permute-start(bf16[8,2176]{1,0:T(8,128)(2,1)S(1)} %pad_maximum_fusion._.refs_6_), channel_id=1, source_target_pairs={{0,16},{4,20},{8,24},{12,28},{16,0},{20,4},{24,8},{28,12},{1,17},{... | collective-permute-start | bytes 104456 | tf_op jit(solution)/shard_map/ppermute | solution.py:31
  43.5 6.5 %shard_map.234 = (bf16[40,128,512]{2,1,0:T(8,128)(2,1)}, bf16[40,64,128]{2,1,0:T(8,128)(2,1)}, f32[8,128]{1,0:T(8,128)S(1)}) custom-call(s32[4,10]{1,0:T(4,128)S(1)} %copy-done.2, s32[1]{0:T(128)} %copy.36.slot_in.refs_0_.slot.refs_1_, bf16[8,2176]{1,0:T(8,128)(2,1)S(1)} %pad_maximum_fusion._.refs_6_, bf16[40,128,512]{2,1,0:T(8,128)(2,1)} %lat.7, ...), custom_call_target="tpu_custom_call" | custom-call | bytes 11796480 | tf_op jit(solution)/shard_map/pallas_call | solution.py:751
  50.1 2.0 %shard_map.235 = (bf16[32,2048]{1,0:T(8,128)(2,1)S(1)}, f32[32,64]{1,0:T(8,128)S(1)}, bf16[4,2048]{1,0:T(4,128)(2,1)S(1)}, bf16[272,512]{1,0:T(8,128)(2,1)S(1)}) custom-call(s32[4,10]{1,0:T(4,128)S(1)} %copy-done.2, s32[1]{0:T(128)} %copy.36.slot_in.refs_0_.slot.refs_1_, s32[1]{0:T(128)} %bitcast.1.refs_2_.rank, s32[32,6]{1,0:T(8,128)S(1)} %copy.30.refs_3_, ...), custom_call_target="tpu_custom_call" | custom-call | flops 8388608 | bytes 262144 | tf_op jit(solution)/shard_map/pallas_call | solution.py:767
  52.1 2.1 %collective-permute-start.15 = (bf16[272,512]{1,0:T(8,128)(2,1)S(1)}, bf16[272,512]{1,0:T(8,128)(2,1)S(1)}, u32[]{:S(2)}, u32[]{:S(2)}) collective-permute-start(bf16[272,512]{1,0:T(8,128)(2,1)S(1)} %get-tuple-element.51), channel_id=1, source_target_pairs={{0,16},{4,20},{8,24},{12,28},{16,0},{20,4},{24,8},{28,12},{1,17},{... | collective-permute-start | bytes 835592 | tf_op jit(solution)/shard_map/ppermute | solution.py:31
  54.3 18.3 %shard_map.236 = (f32[16,2048]{1,0:T(8,128)S(1)}, bf16[16,2048]{1,0:T(8,128)(2,1)S(1)}) custom-call(s32[1]{0:T(128)} %bitcast.1.refs_2_.rank, bf16[32,2048]{1,0:T(8,128)(2,1)S(1)} %get-tuple-element.52.x, f32[32,64]{1,0:T(8,128)S(1)} %get-tuple-element.53.coef, bf16[2816,2048]{1,0:T(8,128)(2,1)} %bitcast.27, bf16[2816,2048]{1,0:T(8,128)(2,1)} %bitcast.28, ...), custom_call_target="tpu_custom_call" | custom-call | flops 1107296256 | bytes 34603008 | tf_op jit(solution)/shard_map/pallas_call | solution.py:785
  72.9 1.0 %collective-permute-done.16.got = bf16[16,2048]{1,0:T(8,128)(2,1)S(1)} collective-permute-done((bf16[16,2048]{1,0:T(8,128)(2,1)S(1)}, bf16[16,2048]{1,0:T(8,128)(2,1)S(1)}, u32[]{:S(2)}, u32[]{:S(2)}) %collective-permute-start.16) | collective-permute-done | bytes 65568 | tf_op jit(solution)/shard_map/ppermute | solution.py:31
  73.9 1.1 %collective-permute-start.17 = (bf16[4,2048]{1,0:T(4,128)(2,1)S(1)}, bf16[4,2048]{1,0:T(4,128)(2,1)S(1)}, u32[]{:S(2)}, u32[]{:S(2)}) collective-permute-start(bf16[4,2048]{1,0:T(4,128)(2,1)S(1)} %get-tuple-element.58), channel_id=1, source_target_pairs={{0,8},{4,12},{8,0},{12,4},{16,24},{20,28},{24,16},{28,20},{1,9},{5... | collective-permute-start | bytes 49160 | tf_op jit(solution)/shard_map/ppermute | solution.py:31
  75.0 0.9 collective-permute-start.18
  75.8 1.6 %collective-permute-start.19 = (bf16[4,2048]{1,0:T(4,128)(2,1)S(1)}, bf16[4,2048]{1,0:T(4,128)(2,1)S(1)}, u32[]{:S(2)}, u32[]{:S(2)}) collective-permute-start(bf16[4,2048]{1,0:T(4,128)(2,1)S(1)} %get-tuple-element.60), channel_id=1, source_target_pairs={{0,24},{4,28},{8,16},{12,20},{16,8},{20,12},{24,0},{28,4},{1,25},{... | collective-permute-start | bytes 49160 | tf_op jit(solution)/shard_map/ppermute | solution.py:31
  77.5 4.5 %shard_map.238.shared = f32[4,2048]{1,0:T(4,128)S(1)} custom-call(bf16[4,2048]{1,0:T(4,128)(2,1)S(1)} %get-tuple-element.57.x, bf16[704,2048]{1,0:T(8,128)(2,1)} %bitcast.30, bf16[704,2048]{1,0:T(8,128)(2,1)} %bitcast.31, bf16[704,2048]{1,0:T(8,128)(2,1)} %down.1, f32[4,2048]{1,0:T(4,128)S(1)} %get-tuple-element.56._.own), custom_call_target="tpu_custom_call" | custom-call | flops 34603008 | bytes 8650752 | tf_op jit(solution)/shard_map/pallas_call | solution.py:810
  82.0 1.6 %shard_map.239 = (f32[4,2048]{1,0:T(4,128)S(1)}, bf16[256,512]{1,0:T(8,128)(2,1)S(1)}) custom-call(s32[4,10]{1,0:T(4,128)S(1)} %copy-done.2, s32[1]{0:T(128)} %copy.36.slot_in.refs_0_.slot.refs_1_, bf16[40,128,512]{2,1,0:T(8,128)(2,1)} %lat.7, f32[4,2048]{1,0:T(4,128)S(1)} %get-tuple-element.56._.own, f32[4,2048]{1,0:T(4,128)S(1)} %shard_map.238.shared, ...), custom_call_target="tpu_custom_call" | custom-call | bytes 524288 | tf_op jit(solution)/shard_map/pallas_call | solution.py:825
  83.5 3.1 %collective-permute-start.22 = (f32[4,2048]{1,0:T(4,128)S(1)}, f32[4,2048]{1,0:T(4,128)S(1)}, u32[]{:S(2)}, u32[]{:S(2)}) collective-permute-start(f32[4,2048]{1,0:T(4,128)S(1)} %get-tuple-element.61._), channel_id=1, source_target_pairs={{0,3},{1,2},{2,1},{3,0},{4,7},{5,6},{6,5},{7,4},{8,11},{9,10},{10,... | collective-permute-start | bytes 98312 | tf_op jit(solution)/shard_map/ppermute | solution.py:31
  86.7 1.3 %collective-permute-start.20 = (f32[4,2048]{1,0:T(4,128)S(1)}, f32[4,2048]{1,0:T(4,128)S(1)}, u32[]{:S(2)}, u32[]{:S(2)}) collective-permute-start(f32[4,2048]{1,0:T(4,128)S(1)} %get-tuple-element.61._), channel_id=1, source_target_pairs={{0,1},{1,0},{2,3},{3,2},{4,5},{5,4},{6,7},{7,6},{8,9},{9,8},{10,11... | collective-permute-start | bytes 98312 | tf_op jit(solution)/shard_map/ppermute | solution.py:31
  88.3 2.3 %shard_map.240 = (bf16[40,128,512]{2,1,0:T(8,128)(2,1)}, bf16[40,64,128]{2,1,0:T(8,128)(2,1)}) custom-call(s32[4,10]{1,0:T(4,128)S(1)} %copy-done.2, s32[1]{0:T(128)} %copy.36.slot_in.refs_0_.slot.refs_1_, s32[4]{0:T(128)S(1)} %add_reduce_fusion.lengths, s32[1]{0:T(128)} %bitcast.3.refs_1_.rank, ...), custom_call_target="tpu_custom_call", output_to_operand_aliasing={{0}: (8, {}), {1}: (9, {})} | custom-call | bytes 589824 | tf_op jit(solution)/shard_map/pallas_call | solution.py:842
  90.6 0.8 collective-permute-done.21
  91.5 0.7 add_convert_fusion
  92.2 2.8 %collective-permute-done.23.got = bf16[256,512]{1,0:T(8,128)(2,1)S(1)} collective-permute-done((bf16[256,512]{1,0:T(8,128)(2,1)S(1)}, bf16[256,512]{1,0:T(8,128)(2,1)S(1)}, u32[]{:S(2)}, u32[]{:S(2)}) %collective-permute-start.23) | collective-permute-done | bytes 262176 | tf_op jit(solution)/shard_map/ppermute | solution.py:31
  95.0 1.3 %shard_map.241 = bf16[40,128,512]{2,1,0:T(8,128)(2,1)} custom-call(s32[4,10]{1,0:T(4,128)S(1)} %copy-done.2, s32[1]{0:T(128)} %copy.36.slot_in.refs_0_.slot.refs_1_, s32[4]{0:T(128)S(1)} %add_reduce_fusion.lengths, s32[1]{0:T(128)} %bitcast.3.refs_1_.rank, f32[4,512]{1,0:T(4,128)S(1)} %slice.39.new_lat, ...), custom_call_target="tpu_custom_call", output_to_operand_aliasing={{}: (6, {})} | custom-call | bytes 589824 | tf_op jit(solution)/shard_map/pallas_call | solution.py:869
  (59 shorter events, 4.3 us)
Async XLA Ops:
  0.6 11.8 %copy-start.2 = (s32[4,10]{1,0:T(4,128)S(1)}, s32[4,10]{1,0:T(4,128)}, u32[]{:S(2)}) copy-start(s32[4,10]{1,0:T(4,128)} %table.9) | copy-start | bytes 484
  0.6 11.8 %copy-start.6 = (s32[4]{0:T(128)S(1)}, s32[4]{0:T(128)}, u32[]{:S(2)}) copy-start(s32[4]{0:T(128)} %refs_0_.3) | copy-start | bytes 52
  1.3 0.7 copy-start.1
  2.0 10.4 %copy-start.5 = (f32[512]{0:T(512)S(1)}, f32[512]{0:T(512)}, u32[]{:S(2)}) copy-start(f32[512]{0:T(512)} %param.31) | copy-start | bytes 6148
  4.7 33.6 %collective-permute-start.9 = (bf16[6,128,512]{2,1,0:T(8,128)(2,1)S(1)}, bf16[6,128,512]{2,1,0:T(8,128)(2,1)S(1)}, u32[]{:S(2)}, u32[]{:S(2)}) collective-permute-start(bf16[6,128,512]{2,1,0:T(8,128)(2,1)S(1)} %get-tuple-element.46), channel_id=1, source_target_pairs={{0,16},{4,20},{8,24},{12,28},{16,0},{20,4},{24,8},{28,12},{1,17},{... | collective-permute-start | bytes 2359304 | tf_op jit(solution)/shard_map/ppermute | solution.py:31
  7.7 30.6 %collective-permute-start.10 = (bf16[10,64,128]{2,1,0:T(8,128)(2,1)S(1)}, bf16[10,64,128]{2,1,0:T(8,128)(2,1)S(1)}, u32[]{:S(2)}, u32[]{:S(2)}) collective-permute-start(bf16[10,64,128]{2,1,0:T(8,128)(2,1)S(1)} %get-tuple-element.47), channel_id=1, source_target_pairs={{0,16},{4,20},{8,24},{12,28},{16,0},{20,4},{24,8},{28,12},{1,17},{... | collective-permute-start | bytes 491528 | tf_op jit(solution)/shard_map/ppermute | solution.py:31
  7.8 10.5 %collective-permute-start = (bf16[16,576]{1,0:T(8,128)(2,1)S(1)}, bf16[16,576]{1,0:T(8,128)(2,1)S(1)}, u32[]{:S(2)}, u32[]{:S(2)}) collective-permute-start(bf16[16,576]{1,0:T(8,128)(2,1)S(1)} %get-tuple-element.35.refs_2_.refs_4_), channel_id=1, source_target_pairs={{0,1},{1,0},{2,3},{3,2},{4,5},{5,4},{6,7},{7,6},{8,9},{9,8},{10,11... | collective-permute-start | bytes 55304 | tf_op jit(solution)/shard_map/ppermute | solution.py:31
  9.8 8.5 %collective-permute-start.1 = (bf16[16,576]{1,0:T(8,128)(2,1)S(1)}, bf16[16,576]{1,0:T(8,128)(2,1)S(1)}, u32[]{:S(2)}, u32[]{:S(2)}) collective-permute-start(bf16[16,576]{1,0:T(8,128)(2,1)S(1)} %get-tuple-element.35.refs_2_.refs_4_), channel_id=1, source_target_pairs={{0,2},{1,3},{2,0},{3,1},{4,6},{5,7},{6,4},{7,5},{8,10},{9,11},{10,... | collective-permute-start | bytes 55304 | tf_op jit(solution)/shard_map/ppermute | solution.py:31
  12.4 5.9 %collective-permute-start.2 = (bf16[16,576]{1,0:T(8,128)(2,1)S(1)}, bf16[16,576]{1,0:T(8,128)(2,1)S(1)}, u32[]{:S(2)}, u32[]{:S(2)}) collective-permute-start(bf16[16,576]{1,0:T(8,128)(2,1)S(1)} %get-tuple-element.35.refs_2_.refs_4_), channel_id=1, source_target_pairs={{0,3},{1,2},{2,1},{3,0},{4,7},{5,6},{6,5},{7,4},{8,11},{9,10},{10,... | collective-permute-start | bytes 55304 | tf_op jit(solution)/shard_map/ppermute | solution.py:31
  18.3 20.0 %copy-start.3 = (bf16[4,2048]{1,0:T(4,128)(2,1)S(1)}, bf16[4,2048]{1,0:T(4,128)(2,1)}, u32[]{:S(2)}) copy-start(bf16[4,2048]{1,0:T(4,128)(2,1)} %refs_5_.2) | copy-start | bytes 49156
  18.3 20.0 %copy-start.4 = (f32[2048]{0:T(1024)S(1)}, f32[2048]{0:T(1024)}, u32[]{:S(2)}) copy-start(f32[2048]{0:T(1024)} %param.35) | copy-start | bytes 24580
  18.3 25.1 %copy-start.7 = (s32[32,6]{0,1:T(8,128)S(1)}, s32[32,6]{0,1:T(8,128)}, u32[]{:S(2)}) copy-start(s32[32,6]{0,1:T(8,128)} %param.37) | copy-start | bytes 2308
  21.0 4.5 %collective-permute-start.3 = (f32[16,640]{1,0:T(8,128)S(1)}, f32[16,640]{1,0:T(8,128)S(1)}, u32[]{:S(2)}, u32[]{:S(2)}) collective-permute-start(f32[16,640]{1,0:T(8,128)S(1)} %get-tuple-element.40), channel_id=1, source_target_pairs={{0,1},{1,0},{2,3},{3,2},{4,5},{5,4},{6,7},{7,6},{8,9},{9,8},{10,11... | collective-permute-start | bytes 122888 | tf_op jit(solution)/shard_map/ppermute | solution.py:31
  21.6 6.3 %collective-permute-start.4 = (f32[16,640]{1,0:T(8,128)S(1)}, f32[16,640]{1,0:T(8,128)S(1)}, u32[]{:S(2)}, u32[]{:S(2)}) collective-permute-start(f32[16,640]{1,0:T(8,128)S(1)} %get-tuple-element.41), channel_id=1, source_target_pairs={{0,2},{1,3},{2,0},{3,1},{4,6},{5,7},{6,4},{7,5},{8,10},{9,11},{10,... | collective-permute-start | bytes 122888 | tf_op jit(solution)/shard_map/ppermute | solution.py:31
  25.1 5.8 %collective-permute-start.5 = (f32[16,640]{1,0:T(8,128)S(1)}, f32[16,640]{1,0:T(8,128)S(1)}, u32[]{:S(2)}, u32[]{:S(2)}) collective-permute-start(f32[16,640]{1,0:T(8,128)S(1)} %get-tuple-element.42), channel_id=1, source_target_pairs={{0,3},{1,2},{2,1},{3,0},{4,7},{5,6},{6,5},{7,4},{8,11},{9,10},{10,... | collective-permute-start | bytes 122888 | tf_op jit(solution)/shard_map/ppermute | solution.py:31
  30.9 19.2 %copy-start = (bf16[2048,64]{0,1:T(8,128)(2,1)S(1)}, bf16[2048,64]{0,1:T(8,128)(2,1)}, u32[]{:S(2)}) copy-start(bf16[2048,64]{0,1:T(8,128)(2,1)} %param.36) | copy-start | bytes 786436
  31.6 4.4 %collective-permute-start.6 = (f32[4,2048]{1,0:T(4,128)S(1)}, f32[4,2048]{1,0:T(4,128)S(1)}, u32[]{:S(2)}, u32[]{:S(2)}) collective-permute-start(f32[4,2048]{1,0:T(4,128)S(1)} %shard_map.232.refs_1_), channel_id=1, source_target_pairs={{0,1},{1,0},{2,3},{3,2},{4,5},{5,4},{6,7},{7,6},{8,9},{9,8},{10,11... | collective-permute-start | bytes 98312 | tf_op jit(solution)/shard_map/ppermute | solution.py:31
  31.6 4.9 %collective-permute-start.7 = (f32[4,2048]{1,0:T(4,128)S(1)}, f32[4,2048]{1,0:T(4,128)S(1)}, u32[]{:S(2)}, u32[]{:S(2)}) collective-permute-start(f32[4,2048]{1,0:T(4,128)S(1)} %shard_map.232.refs_1_), channel_id=1, source_target_pairs={{0,2},{1,3},{2,0},{3,1},{4,6},{5,7},{6,4},{7,5},{8,10},{9,11},{10,... | collective-permute-start | bytes 98312 | tf_op jit(solution)/shard_map/ppermute | solution.py:31
  32.6 5.7 %collective-permute-start.8 = (f32[4,2048]{1,0:T(4,128)S(1)}, f32[4,2048]{1,0:T(4,128)S(1)}, u32[]{:S(2)}, u32[]{:S(2)}) collective-permute-start(f32[4,2048]{1,0:T(4,128)S(1)} %shard_map.232.refs_1_), channel_id=1, source_target_pairs={{0,3},{1,2},{2,1},{3,0},{4,7},{5,6},{6,5},{7,4},{8,11},{9,10},{10,... | collective-permute-start | bytes 98312 | tf_op jit(solution)/shard_map/ppermute | solution.py:31
  38.5 1.3 %collective-permute-start.11 = (bf16[4,2176]{1,0:T(4,128)(2,1)S(1)}, bf16[4,2176]{1,0:T(4,128)(2,1)S(1)}, u32[]{:S(2)}, u32[]{:S(2)}) collective-permute-start(bf16[4,2176]{1,0:T(4,128)(2,1)S(1)} %get-tuple-element.48), channel_id=1, source_target_pairs={{0,4},{4,0},{8,12},{12,8},{16,20},{20,16},{24,28},{28,24},{1,5},{5... | collective-permute-start | bytes 52232 | tf_op jit(solution)/shard_map/ppermute | solution.py:31
  39.8 10.3 %collective-permute-start.12 = (bf16[8,2176]{1,0:T(8,128)(2,1)S(1)}, bf16[8,2176]{1,0:T(8,128)(2,1)S(1)}, u32[]{:S(2)}, u32[]{:S(2)}) collective-permute-start(bf16[8,2176]{1,0:T(8,128)(2,1)S(1)} %pad_maximum_fusion._.refs_6_), channel_id=1, source_target_pairs={{0,8},{4,12},{8,0},{12,4},{16,24},{20,28},{24,16},{28,20},{1,9},{5... | collective-permute-start | bytes 104456 | tf_op jit(solution)/shard_map/ppermute | solution.py:31
  41.9 8.2 %collective-permute-start.13 = (bf16[8,2176]{1,0:T(8,128)(2,1)S(1)}, bf16[8,2176]{1,0:T(8,128)(2,1)S(1)}, u32[]{:S(2)}, u32[]{:S(2)}) collective-permute-start(bf16[8,2176]{1,0:T(8,128)(2,1)S(1)} %pad_maximum_fusion._.refs_6_), channel_id=1, source_target_pairs={{0,16},{4,20},{8,24},{12,28},{16,0},{20,4},{24,8},{28,12},{1,17},{... | collective-permute-start | bytes 104456 | tf_op jit(solution)/shard_map/ppermute | solution.py:31
  43.0 7.1 %collective-permute-start.14 = (bf16[8,2176]{1,0:T(8,128)(2,1)S(1)}, bf16[8,2176]{1,0:T(8,128)(2,1)S(1)}, u32[]{:S(2)}, u32[]{:S(2)}) collective-permute-start(bf16[8,2176]{1,0:T(8,128)(2,1)S(1)} %pad_maximum_fusion._.refs_6_), channel_id=1, source_target_pairs={{0,24},{4,28},{8,16},{12,20},{16,8},{20,12},{24,0},{28,4},{1,25},{... | collective-permute-start | bytes 104456 | tf_op jit(solution)/shard_map/ppermute | solution.py:31
  52.1 20.5 %collective-permute-start.15 = (bf16[272,512]{1,0:T(8,128)(2,1)S(1)}, bf16[272,512]{1,0:T(8,128)(2,1)S(1)}, u32[]{:S(2)}, u32[]{:S(2)}) collective-permute-start(bf16[272,512]{1,0:T(8,128)(2,1)S(1)} %get-tuple-element.51), channel_id=1, source_target_pairs={{0,16},{4,20},{8,24},{12,28},{16,0},{20,4},{24,8},{28,12},{1,17},{... | collective-permute-start | bytes 835592 | tf_op jit(solution)/shard_map/ppermute | solution.py:31
  72.5 1.3 %collective-permute-start.16 = (bf16[16,2048]{1,0:T(8,128)(2,1)S(1)}, bf16[16,2048]{1,0:T(8,128)(2,1)S(1)}, u32[]{:S(2)}, u32[]{:S(2)}) collective-permute-start(bf16[16,2048]{1,0:T(8,128)(2,1)S(1)} %get-tuple-element.55), channel_id=1, source_target_pairs={{0,4},{4,0},{8,12},{12,8},{16,20},{20,16},{24,28},{28,24},{1,5},{5... | collective-permute-start | bytes 196616 | tf_op jit(solution)/shard_map/ppermute | solution.py:31
  73.9 8.1 %collective-permute-start.17 = (bf16[4,2048]{1,0:T(4,128)(2,1)S(1)}, bf16[4,2048]{1,0:T(4,128)(2,1)S(1)}, u32[]{:S(2)}, u32[]{:S(2)}) collective-permute-start(bf16[4,2048]{1,0:T(4,128)(2,1)S(1)} %get-tuple-element.58), channel_id=1, source_target_pairs={{0,8},{4,12},{8,0},{12,4},{16,24},{20,28},{24,16},{28,20},{1,9},{5... | collective-permute-start | bytes 49160 | tf_op jit(solution)/shard_map/ppermute | solution.py:31
  75.0 7.0 %collective-permute-start.18 = (bf16[4,2048]{1,0:T(4,128)(2,1)S(1)}, bf16[4,2048]{1,0:T(4,128)(2,1)S(1)}, u32[]{:S(2)}, u32[]{:S(2)}) collective-permute-start(bf16[4,2048]{1,0:T(4,128)(2,1)S(1)} %get-tuple-element.59), channel_id=1, source_target_pairs={{0,16},{4,20},{8,24},{12,28},{16,0},{20,4},{24,8},{28,12},{1,17},{... | collective-permute-start | bytes 49160 | tf_op jit(solution)/shard_map/ppermute | solution.py:31
  75.8 6.1 %collective-permute-start.19 = (bf16[4,2048]{1,0:T(4,128)(2,1)S(1)}, bf16[4,2048]{1,0:T(4,128)(2,1)S(1)}, u32[]{:S(2)}, u32[]{:S(2)}) collective-permute-start(bf16[4,2048]{1,0:T(4,128)(2,1)S(1)} %get-tuple-element.60), channel_id=1, source_target_pairs={{0,24},{4,28},{8,16},{12,20},{16,8},{20,12},{24,0},{28,4},{1,25},{... | collective-permute-start | bytes 49160 | tf_op jit(solution)/shard_map/ppermute | solution.py:31
  83.5 7.1 %collective-permute-start.22 = (f32[4,2048]{1,0:T(4,128)S(1)}, f32[4,2048]{1,0:T(4,128)S(1)}, u32[]{:S(2)}, u32[]{:S(2)}) collective-permute-start(f32[4,2048]{1,0:T(4,128)S(1)} %get-tuple-element.61._), channel_id=1, source_target_pairs={{0,3},{1,2},{2,1},{3,0},{4,7},{5,6},{6,5},{7,4},{8,11},{9,10},{10,... | collective-permute-start | bytes 98312 | tf_op jit(solution)/shard_map/ppermute | solution.py:31
  86.7 4.8 %collective-permute-start.21 = (f32[4,2048]{1,0:T(4,128)S(1)}, f32[4,2048]{1,0:T(4,128)S(1)}, u32[]{:S(2)}, u32[]{:S(2)}) collective-permute-start(f32[4,2048]{1,0:T(4,128)S(1)} %get-tuple-element.61._), channel_id=1, source_target_pairs={{0,2},{1,3},{2,0},{3,1},{4,6},{5,7},{6,4},{7,5},{8,10},{9,11},{10,... | collective-permute-start | bytes 98312 | tf_op jit(solution)/shard_map/ppermute | solution.py:31
  86.7 4.8 %collective-permute-start.20 = (f32[4,2048]{1,0:T(4,128)S(1)}, f32[4,2048]{1,0:T(4,128)S(1)}, u32[]{:S(2)}, u32[]{:S(2)}) collective-permute-start(f32[4,2048]{1,0:T(4,128)S(1)} %get-tuple-element.61._), channel_id=1, source_target_pairs={{0,1},{1,0},{2,3},{3,2},{4,5},{5,4},{6,7},{7,6},{8,9},{9,8},{10,11... | collective-permute-start | bytes 98312 | tf_op jit(solution)/shard_map/ppermute | solution.py:31
  88.3 6.7 %collective-permute-start.23 = (bf16[256,512]{1,0:T(8,128)(2,1)S(1)}, bf16[256,512]{1,0:T(8,128)(2,1)S(1)}, u32[]{:S(2)}, u32[]{:S(2)}) collective-permute-start(bf16[256,512]{1,0:T(8,128)(2,1)S(1)} %get-tuple-element.62), channel_id=1, source_target_pairs={{0,16},{4,20},{8,24},{12,28},{16,0},{20,4},{24,8},{28,12},{1,17},{... | collective-permute-start | bytes 786440 | tf_op jit(solution)/shard_map/ppermute | solution.py:31

commit v2 on v1

--- a/solution.py
+++ b/solution.py
@@ -117,13 +117,9 @@
         copy.wait()
 
 
-def fetch_kernel(
-    table, lengths, normed, gain, w_latent, lat, rope,
-    lat_v, rope_v, new_out, latent_v, sems, w_sem,
-):
+def fetch_kernel(table, _, lat, rope, lat_v, rope_v, token, sems):
+    token[...] = jnp.zeros_like(token)
     requests, per_dev = table.shape
-    weights = pltpu.make_async_copy(w_latent, latent_v, w_sem.at[0])
-    weights.start()
     copies = []
     for r in range(requests):
         for j in range(per_dev):
@@ -133,36 +129,59 @@
             copies.append(pltpu.make_async_copy(rope.at[page], rope_v.at[n], sems.at[1, n]))
     for copy in copies:
         copy.start()
+    for copy in copies:
+        copy.wait()
+
+
+def token_weights_kernel(
+    lengths, normed, gain, _, w_latent, value_up, w_out, value_v, out_v, new_out, latent_v, sems,
+):
+    copies = [
+        pltpu.make_async_copy(w_latent, latent_v, sems.at[0]),
+        pltpu.make_async_copy(value_up, value_v, sems.at[1]),
+        pltpu.make_async_copy(w_out, out_v, sems.at[2]),
+    ]
+    for copy in copies:
+        copy.start()
     size = gain.shape[1]
-    weights.wait()
+    copies[0].wait()
     latent = lax.dot_general(normed[...], latent_v[...], NT, preferred_element_type=F32)
     c_new = rms_norm(latent[:, :size], gain[...]).astype(BF16).astype(F32)
     p_new = latent[:, size:].astype(BF16).astype(F32)
     lane = lax.broadcasted_iota(jnp.int32, (1, LANES), 1)
     marks = []
-    for r in range(requests):
+    for r in range(normed.shape[0]):
         page = jnp.full((1, LANES), lengths[r] // PAGE, jnp.int32)
         inside = jnp.full((1, LANES), lengths[r] % PAGE, jnp.int32)
         marks.append(jnp.where(lane == 0, page, jnp.where(lane == 1, inside, 0)))
     mark = jnp.concatenate(marks, axis=0).astype(F32)
-    new = jnp.concatenate([c_new, p_new, mark[:, : LANES - ROPE]], axis=1)
-    new_out[...] = new
-    for copy in copies:
-        copy.wait()
+    new_out[...] = jnp.concatenate([c_new, p_new, mark[:, : LANES - ROPE]], axis=1)
+    copies[1].wait()
+    copies[2].wait()
 
 
 def attention_kernel(blocks, per_dev, requests, lat_size, *refs):
-    lengths, rank = refs[:2]
-    queries = refs[2 : 2 + blocks]
-    lat, rope, value_up, w_out = refs[2 + blocks : 6 + blocks]
+    table, slot, lengths, rank = refs[:4]
+    queries = refs[4 : 4 + blocks]
+    lat, rope = refs[4 + blocks : 6 + blocks]
     outs = refs[6 + blocks : 6 + 2 * blocks]
-    value_v, out_v, q_all, result, sems = refs[6 + 2 * blocks :]
-    weights_in = [
-        pltpu.make_async_copy(value_up, value_v, sems.at[0]),
-        pltpu.make_async_copy(w_out, out_v, sems.at[1]),
-    ]
-    for copy in weights_in:
-        copy.start()
+    lat_out, rope_out, q_all, result, sems = refs[6 + 2 * blocks :]
+
+    def own_pages(r):
+        copies = []
+        for j in range(per_dev):
+            n = r * per_dev + j
+            page = table[r, j]
+            copies.append(pltpu.make_async_copy(lat.at[n], lat_out.at[page], sems.at[0, n]))
+            copies.append(pltpu.make_async_copy(rope.at[n], rope_out.at[page], sems.at[1, n]))
+        return copies
+
+    for r in range(requests):
+        @pl.when(slot[0] != r)
+        def _():
+            for copy in own_pages(r):
+                copy.start()
+
     rows = queries[0].shape[0]
     heads = blocks * rows // requests
     scale = (NOPE + ROPE) ** (-0.5)
@@ -223,38 +242,59 @@
             attend(r, per_dev)
 
     for k in range(blocks):
-        for i in range(tiles + 1):
-            outs[k][:, i * LANES : (i + 1) * LANES] = result[i, k * rows : (k + 1) * rows, :]
-    for copy in weights_in:
-        copy.wait()
+        block = pl.ds(k * rows, rows)
+        marks = result[tiles, block, :]
+        peak, total = marks[:, :1], marks[:, LANES // 2 : LANES // 2 + 1]
+        some = total > 0.0
+        safe = jnp.where(some, total, 1.0)
+        level = jnp.where(some, peak + jnp.log(safe), NEG)
+        high = level.astype(BF16).astype(F32)
+        middle = (level - high).astype(BF16).astype(F32)
+        low = level - high - middle
+        lane = lax.broadcasted_iota(jnp.int32, marks.shape, 1)
+        split = jnp.where(lane == 0, high, jnp.where(lane == 1, middle, low))
+        share = 1.0 / safe
+        pieces = [result[i, block, :] * share for i in range(tiles)] + [split]
+        outs[k][...] = jnp.concatenate(pieces, axis=1).astype(BF16)
+    for r in range(requests):
+        @pl.when(slot[0] != r)
+        def _():
+            for copy in own_pages(r):
+                copy.wait()
 
 
 def finish_kernel(blocks, requests, lat_size, *refs):
     parts = refs[:blocks]
-    query, new, value_up, w_out, out = refs[blocks:]
+    query, new, value_up, w_out, out, sent = refs[blocks:]
     local_heads = value_up.shape[0]
     scale = (NOPE + ROPE) ** (-0.5)
-    half = lat_size + LANES // 2
     fresh = jnp.concatenate([new[:, : lat_size + ROPE]] * local_heads, axis=0)
     q_own = query[...].astype(F32)
     new_score = jnp.sum(q_own * fresh, axis=1, keepdims=True) * scale
     peak = new_score
+    means = []
     for part in parts:
-        peak = jnp.maximum(peak, part[:, lat_size : lat_size + 1])
+        wide = part[...].astype(F32)
+        marks = wide[:, lat_size:]
+        level = marks[:, 0:1] + marks[:, 1:2] + marks[:, 2:3]
+        means.append((level, wide[:, :lat_size]))
+        peak = jnp.maximum(peak, level)
     new_factor = jnp.exp(new_score - peak)
     denom = new_factor
     numer = new_factor * fresh[:, :lat_size]
-    for part in parts:
-        factor = jnp.exp(part[:, lat_size : lat_size + 1] - peak)
-        denom += factor * part[:, half : half + 1]
-        numer += factor * part[:, :lat_size]
+    for level, mean in means:
+        factor = jnp.exp(level - peak)
+        denom += factor
+        numer += factor * mean
     o_lat = numer / denom
     vals = []
     for h in range(local_heads):
         one = o_lat[h * requests : (h + 1) * requests, :].astype(BF16)
         vals.append(jnp.dot(one, value_up[h], preferred_element_type=F32).astype(BF16))
     o_val = jnp.concatenate(vals, axis=1)
-    out[...] = jnp.dot(o_val, w_out[...], preferred_element_type=F32)
+    value = jnp.dot(o_val, w_out[...], preferred_element_type=F32)
+    out[...] = value
+    sent[...] = value.astype(BF16)
 
 
 def norm_kernel(blocks, *refs):
@@ -264,7 +304,7 @@
     row_out, h_out = refs[-2:]
     attn = parts[0][...]
     for part in parts[1:]:
-        attn += part[...]
+        attn += part[...].astype(F32)
     h_one = (x[...].astype(F32) + attn).astype(BF16)
     h_out[...] = h_one
     wide = h_one.astype(F32)
@@ -285,25 +325,13 @@
     return copies
 
 
-def order_kernel(groups, requests, first, count, *refs):
-    table, slot, rank, route_ids, router, lat = refs[:6]
-    pieces = refs[6 : 6 + groups]
-    h_one, new = refs[6 + groups : 8 + groups]
-    x_out, coef_out, own_out, lat_out, sems = refs[9 + groups :]
-    copies = copy_pages(table, slot, lat, lat_out, sems, first, count)
-    both = jnp.concatenate([h_one[...].astype(F32), new[...]], axis=1)
-    row = lax.broadcasted_iota(jnp.int32, both.shape, 0)
-    both = jnp.sum(jnp.where(row == slot[0], both, 0.0), axis=0, keepdims=True)
-    lat_size = lat_out.shape[1]
-    lines = [both[:, b : b + lat_size] for b in range(0, both.shape[1], lat_size)]
-    lines[-1] = jnp.pad(lines[-1], ((0, 0), (0, lat_size - lines[-1].shape[1])))
-    lines.append(jnp.zeros((ROWS - len(lines), lat_size), F32))
-    lat_out[count * PAGE :, :] = jnp.concatenate(lines, axis=0).astype(BF16)
+def order_kernel(groups, requests, rank, route_ids, router, *refs):
+    pieces = refs[:groups]
+    x_out, coef_out, own_out, _ = refs[groups + 1 :]
     size = router.shape[1]
-    per = pieces[0].shape[0]
-    rows = groups * per
+    wide = jnp.concatenate([p[...].astype(F32) for p in pieces], axis=0)
+    rows = wide.shape[0]
     reps = rows // requests
-    wide = jnp.concatenate([p[...].astype(F32) for p in pieces], axis=0)
     moved = wide[:, size : size + 1]
     other = jnp.concatenate([moved[rows // 2 :], moved[: rows // 2]], axis=0)
     row = lax.broadcasted_iota(jnp.int32, (rows, 1), 0)
@@ -328,8 +356,6 @@
     for k in range(ids.shape[1]):
         chosen += jnp.where(expert == ids[:, k : k + 1], gates, 0.0)
     coef_out[...] = chosen / jnp.sum(chosen, axis=1, keepdims=True) * ROUTE_SCALE
-    for copy in copies:
-        copy.wait()
 
 
 def expert_kernel(
@@ -388,7 +414,9 @@
         block[...] = total[(k + 1) * requests : (k + 2) * requests].astype(BF16)
 
 
-def shared_kernel(x, gate, up, down, _, out, gate_v, up_v, down_v, sems):
+def shared_kernel(
+    first, count, table, slot, x, gate, up, down, lat, _, out, lat_out, gate_v, up_v, down_v, sems, page_sems,
+):
     copies = [
         pltpu.make_async_copy(gate, gate_v, sems.at[0]),
         pltpu.make_async_copy(up, up_v, sems.at[1]),
@@ -396,24 +424,25 @@
     ]
     for copy in copies:
         copy.start()
+    pages = copy_pages(table, slot, lat, lat_out, page_sems, first, count)
     copies[0].wait()
     gate_val = lax.dot_general(x[...], gate_v[...], NT, preferred_element_type=F32)
     copies[1].wait()
     up_val = lax.dot_general(x[...], up_v[...], NT, preferred_element_type=F32)
     hid = (silu(gate_val) * up_val).astype(BF16)
     copies[2].wait()
+    for copy in pages:
+        copy.wait()
     out[...] = jnp.dot(hid, down_v[...], preferred_element_type=F32)
 
 
-def total_kernel(first, count, table, slot, lat, own, shared, *refs):
-    others, (total, lat_out, sems) = refs[:-3], refs[-3:]
-    copies = copy_pages(table, slot, lat, lat_out, sems, first, count)
+def total_kernel(own, shared, *refs):
+    others, (total, sent) = refs[:-2], refs[-2:]
     value = own[...] + shared[...]
     for other in others:
         value += other[...].astype(F32)
     total[...] = value
-    for copy in copies:
-        copy.wait()
+    sent[...] = value.astype(BF16)
 
 
 def token_spot(r, table, lengths, rank):
@@ -426,67 +455,38 @@
 
 
 def cache_kernel(
-    first, table, slot, _, lat, rope, got_lat, got_rope,
-    lat_out, rope_out, token, lat_v, rope_v, got_sems, in_sems, sems,
+    first, count, table, slot, _, h_one, new, lat, got_lat, got_rope, lat_in, rope_in,
+    next_out, lat_out, rope_out, lat_v, rope_v, page_sems, got_sems, sems,
 ):
-    requests, per_dev = table.shape
+    del lat_in, rope_in
+    per_dev = table.shape[1]
     moved = slot[0]
-    start = moved * per_dev
     fetches = [
-        pltpu.make_async_copy(got_lat, lat_v.at[pl.ds(start, first)], got_sems.at[0]),
-        pltpu.make_async_copy(got_rope, rope_v.at[pl.ds(start, per_dev)], got_sems.at[1]),
+        pltpu.make_async_copy(got_lat, lat_v, got_sems.at[0]),
+        pltpu.make_async_copy(got_rope, rope_v, got_sems.at[1]),
     ]
-
-    def reads(r, j):
-        n = r * per_dev + j
-        page = table[r, j]
-        return (
-            pltpu.make_async_copy(lat.at[page], lat_v.at[n], in_sems.at[0, n]),
-            pltpu.make_async_copy(rope.at[page], rope_v.at[n], in_sems.at[1, n]),
-        )
-
-    def lat_write(r, j):
-        n = r * per_dev + j
-        return pltpu.make_async_copy(lat_v.at[n], lat_out.at[table[r, j]], sems.at[0, n])
-
-    def rope_write(r, j):
-        n = r * per_dev + j
-        return pltpu.make_async_copy(rope_v.at[n], rope_out.at[table[r, j]], sems.at[1, n])
-
-    for r in range(requests):
-        @pl.when(moved != r)
-        def _():
-            for j in range(per_dev):
-                for copy in reads(r, j):
-                    copy.start()
-
     for copy in fetches:
         copy.start()
-    token[...] = jnp.zeros_like(token)
-    for r in range(requests):
-        @pl.when(moved != r)
-        def _():
-            for j in range(per_dev):
-                for copy in reads(r, j):
-                    copy.wait()
-                lat_write(r, j).start()
-                rope_write(r, j).start()
-
+    copies = copy_pages(table, slot, lat, next_out, page_sems, first, count)
+    both = jnp.concatenate([h_one[...].astype(F32), new[...]], axis=1)
+    row = lax.broadcasted_iota(jnp.int32, both.shape, 0)
+    both = jnp.sum(jnp.where(row == moved, both, 0.0), axis=0, keepdims=True)
+    lat_size = next_out.shape[1]
+    lines = [both[:, b : b + lat_size] for b in range(0, both.shape[1], lat_size)]
+    lines[-1] = jnp.pad(lines[-1], ((0, 0), (0, lat_size - lines[-1].shape[1])))
+    lines.append(jnp.zeros((ROWS - len(lines), lat_size), F32))
+    next_out[count * PAGE :, :] = jnp.concatenate(lines, axis=0).astype(BF16)
     for copy in fetches:
         copy.wait()
     for j in range(per_dev):
+        page = table[moved, j]
         if j < first:
-            lat_write(moved, j).start()
-        rope_write(moved, j).start()
-    for r in range(requests):
-        for j in range(per_dev):
-            rope_write(r, j).wait()
-            if j < first:
-                lat_write(r, j).wait()
-            else:
-                @pl.when(moved != r)
-                def _():
-                    lat_write(r, j).wait()
+            copies.append(pltpu.make_async_copy(lat_v.at[j], lat_out.at[page], sems.at[0, j]))
+            copies[-1].start()
+        copies.append(pltpu.make_async_copy(rope_v.at[j], rope_out.at[page], sems.at[1, j]))
+        copies[-1].start()
+    for copy in copies:
+        copy.wait()
 
 
 def token_kernel(
@@ -694,44 +694,61 @@
     got_rope = xored(out_rope, "rep", half)
     q_blocks = [q_own] + [xored(q_own, "tp", k) for k in range(1, n_tp)]
 
-    lat_v, rope_v, new = call(
+    lat_v, rope_v, _ = call(
         fetch_kernel,
         (
             pltpu.VMEM((pages,) + lat_page, BF16),
             pltpu.VMEM((pages,) + rope_page, BF16),
-            struct((requests, width), F32),
+            struct((8, LANES), F32),
         ),
-        [SMEM] * 2 + [VMEM] * 2 + [ANY] * 3,
+        [SMEM, VMEM, ANY, ANY],
         (VMEM,) * 3,
-        [pltpu.VMEM((w_latent.shape[1], size), BF16), dma((2, pages)), dma((1,))],
+        [dma((2, pages))],
         vmem=6,
         flops=2 * requests * w_latent.size,
-        nbytes=pages * page_bytes + 2 * w_latent.size,
-    )(page_table, lengths, normed, latent_gain[None, :], in_hbm(w_latent.T), lat_hbm, rope_hbm)
-
-    *partial, value_v, out_v = call(
+        nbytes=pages * page_bytes + 2 * (w_latent.size + w_output.size + w_value_up.size),
+    )(page_table, q_own, lat_hbm, rope_hbm)
+
+    *partial, lat_most, rope_most = call(
         functools.partial(attention_kernel, n_tp, per_dev, requests, lat_size),
-        tuple(struct((rows, width), F32) for _ in range(n_tp))
-        + (pltpu.VMEM(w_value_up.shape, BF16), pltpu.VMEM(w_output.shape, BF16)),
-        [SMEM, SMEM] + [VMEM] * (n_tp + 2) + [ANY, ANY],
-        (VMEM,) * (n_tp + 2),
-        [pltpu.VMEM((width // LANES, n_tp * rows, LANES), F32)] * 2 + [dma((2,))],
+        tuple(struct((rows, width), BF16) for _ in range(n_tp))
+        + (struct(lat_pool.shape, BF16), struct(rope_pool.shape, BF16)),
+        [SMEM] * 4 + [VMEM] * (n_tp + 2),
+        (VMEM,) * n_tp + (ANY, ANY),
+        [pltpu.VMEM((width // LANES, n_tp * rows, LANES), F32)] * 2 + [dma((2, pages))],
         vmem=6,
         flops=4 * n_tp * rows * per_dev * PAGE * lat_size,
         nbytes=pages * page_bytes,
-    )(lengths, tp_one, *q_blocks, lat_v, rope_v, in_hbm(w_value_up), in_hbm(w_output))
+    )(page_table, move_slot, lengths, tp_one, *q_blocks, lat_v, rope_v)
     parts = [partial[0]] + [xored(partial[k], "tp", k) for k in range(1, n_tp)]
-
-    out_part = call(
+    value_v, out_v, new = call(
+        token_weights_kernel,
+        (
+            pltpu.VMEM(w_value_up.shape, BF16),
+            pltpu.VMEM(w_output.shape, BF16),
+            struct((requests, width), F32),
+        ),
+        [SMEM] + [VMEM] * 3 + [ANY] * 3,
+        (VMEM,) * 3,
+        [pltpu.VMEM((w_latent.shape[1], size), BF16), dma((3,))],
+        vmem=6,
+        flops=2 * requests * w_latent.size,
+        nbytes=2 * (w_latent.size + w_output.size + w_value_up.size),
+    )(
+        lengths, normed, latent_gain[None, :], partial[0], in_hbm(w_latent.T),
+        in_hbm(w_value_up), in_hbm(w_output),
+    )
+
+    out_part, out_sent = call(
         functools.partial(finish_kernel, n_tp, requests, lat_size),
-        struct((requests, size), F32),
+        (struct((requests, size), F32), struct((requests, size), BF16)),
         [VMEM] * (n_tp + 4),
-        VMEM,
+        (VMEM, VMEM),
         vmem=4,
         flops=2 * requests * size * w_output.shape[0],
         nbytes=2 * w_output.size + 2 * w_value_up.size,
     )(*parts, q_own, new, value_v, out_v)
-    out_parts = [out_part] + [xored(out_part, "tp", k) for k in range(1, n_tp)]
+    out_parts = [out_part] + [xored(out_sent, "tp", k) for k in range(1, n_tp)]
 
     ffn_row, h_one = call(
         functools.partial(norm_kernel, n_tp),
@@ -748,55 +765,62 @@
     pair = jnp.concatenate([ffn_row, xored(ffn_row, "rep", 1)], axis=0)
     pieces = [pair] + [xored(pair, "rep", 2 * k) for k in range(1, groups)]
 
-    lat_most, rope_most, cache_token = call(
-        functools.partial(cache_kernel, first_span),
-        (struct(lat_pool.shape, BF16), struct(rope_pool.shape, BF16), struct((8, LANES), F32)),
-        [SMEM] * 2 + [VMEM] + [ANY] * 4,
-        (ANY, ANY, VMEM),
+    out_second, lat_most, rope_most = call(
+        functools.partial(cache_kernel, first_span, second_span),
+        (
+            struct((second_span * PAGE + ROWS, lat_size), BF16),
+            struct(lat_pool.shape, BF16),
+            struct(rope_pool.shape, BF16),
+        ),
+        [SMEM] * 2 + [VMEM] * 3 + [ANY] * 5,
+        (VMEM, ANY, ANY),
         [
-            pltpu.VMEM((pages,) + lat_page, BF16),
-            pltpu.VMEM((pages,) + rope_page, BF16),
+            pltpu.VMEM((first_span,) + lat_page, BF16),
+            pltpu.VMEM((per_dev,) + rope_page, BF16),
+            dma((second_span,)),
             dma((2,)),
-            dma((2, pages)),
-            dma((2, pages)),
+            dma((2, per_dev)),
         ],
-        vmem=8,
-        nbytes=2 * pages * page_bytes,
-    )(page_table, move_slot, pair, lat_hbm, rope_hbm, got_first, got_rope)
-
+        vmem=4,
+        nbytes=2 * first_span * page_bytes,
+        aliases={8: 1, 9: 2},
+    )(
+        page_table, move_slot, pair, h_one, new, lat_hbm, got_first, got_rope,
+        lat_most, rope_most,
+    )
     x_all, coef, x_own, out_second = call(
-        functools.partial(order_kernel, groups, requests, cuts[0], second_span),
+        functools.partial(order_kernel, groups, requests),
         (
             struct((everyone, size), BF16),
             struct((everyone, w_router.shape[1]), F32),
             struct((requests, size), BF16),
-            struct((second_span * PAGE + ROWS, lat_size), BF16),
+            struct(out_second.shape, BF16),
         ),
-        [SMEM] * 3 + [VMEM] * 2 + [ANY] + [VMEM] * (groups + 3),
+        [SMEM] + [VMEM] * (groups + 3),
         (VMEM,) * 4,
-        [dma((second_span,))],
         vmem=6,
         flops=4 * everyone * size * everyone,
         nbytes=4 * everyone * size,
-    )(page_table, move_slot, rep_one, route_ids, w_router.T, lat_hbm, *pieces, h_one, new, cache_token)
+        aliases={3 + groups: 3},
+    )(rep_one, route_ids, w_router.T, *pieces, out_second)
     got_second = xored(out_second, "rep", half)
     got_row = got_second[second_span * PAGE :].reshape(1, -1)[:, : size + width]
 
     kept, sent = call(
         functools.partial(expert_kernel, requests, 256, units),
-        (struct((groups * requests, size), F32), struct((groups * requests, size), BF16)),
+        (
+            struct((groups * requests, size), F32),
+            struct((groups * requests, size), BF16),
+        ),
         [SMEM] + [VMEM] * 2 + [ANY] * 3,
         (VMEM, VMEM),
         [pltpu.VMEM((local_experts * units, size), BF16)] * 3
         + [pltpu.VMEM((everyone, size), F32), dma((3, pl.cdiv(local_experts * units, 256)))],
-        vmem=40,
+        vmem=42,
         flops=6 * everyone * expert_gate.size,
         nbytes=6 * expert_gate.size,
     )(
-        rep_one, x_all, coef,
-        in_hbm(gate_t),
-        in_hbm(up_t),
-        in_hbm(expert_down.reshape(-1, size)),
+        rep_one, x_all, coef, in_hbm(gate_t), in_hbm(up_t), in_hbm(expert_down.reshape(-1, size)),
     )
     summed = call(
         functools.partial(pair_kernel, requests),
@@ -807,30 +831,33 @@
         nbytes=8 * everyone * size,
     )(kept, xored(sent, "rep", 1), got_second)
     others = [xored(summed[k], "rep", 2 * k) for k in range(1, groups)]
-    shared_part = call(
-        shared_kernel,
-        struct((requests, size), F32),
-        [VMEM] + [ANY] * 4,
-        VMEM,
+    shared_part, out_third = call(
+        functools.partial(shared_kernel, cuts[1], third_span),
+        (struct((requests, size), F32), struct((third_span * PAGE, lat_size), BF16)),
+        [SMEM, SMEM, VMEM] + [ANY] * 5,
+        (VMEM, VMEM),
         [
             pltpu.VMEM((shared_gate.shape[1], size), BF16),
             pltpu.VMEM((shared_gate.shape[1], size), BF16),
             pltpu.VMEM(shared_down.shape, BF16),
             dma((3,)),
+            dma((third_span,)),
         ],
         vmem=12,
         flops=6 * requests * shared_gate.size,
         nbytes=6 * shared_gate.size,
-    )(x_own, in_hbm(shared_gate.T), in_hbm(shared_up.T), in_hbm(shared_down), summed[0])
-    total, out_third = call(
-        functools.partial(total_kernel, cuts[1], third_span),
-        (struct((requests, size), F32), struct((third_span * PAGE, lat_size), BF16)),
-        [SMEM, SMEM, ANY] + [VMEM] * (groups + 1),
+    )(
+        page_table, move_slot, x_own, in_hbm(shared_gate.T), in_hbm(shared_up.T),
+        in_hbm(shared_down), lat_hbm, summed[0],
+    )
+    total, total_sent = call(
+        total_kernel,
+        (struct((requests, size), F32), struct((requests, size), BF16)),
+        [VMEM] * (groups + 1),
         (VMEM, VMEM),
-        [dma((third_span,))],
         vmem=4,
         nbytes=8 * everyone * size,
-    )(page_table, move_slot, lat_hbm, summed[0], shared_part, *others)
+    )(summed[0], shared_part, *others)
     got_third = xored(out_third, "rep", half)
 
     is_moved = (jnp.arange(requests, dtype=jnp.int32) == move_slot[0])[:, None]
@@ -861,8 +888,8 @@
     )
 
     total_all = total
-    for other in [xored(total, "tp", k) for k in range(1, n_tp)]:
-        total_all = total_all + other
+    for other in [xored(total_sent, "tp", k) for k in range(1, n_tp)]:
+        total_all = total_all + other.astype(F32)
     h_served = jnp.where(is_moved, got_row[:, :size], h_one)
     mixed = (h_served.astype(F32) + total_all).astype(BF16)
 

time: 96.6 us -> 91.2 us (0.944)
  Pallas kernels: 48.5 us -> 45.4 us
  waiting for transfers between devices: 13.7 us -> 11.2 us
    pallas_call x5 -> x6, Pallas kernels: 15.3 us -> 11.6 us  [the longest x1 5.04 us: body(): call(functools.partial(shared_kernel, cuts[1], third_span), (struct((requ...]
    ppermute x24, waiting for transfers between devices: 13.7 us -> 11.2 us  [xored(): return lax.ppermute(value, axis, pairs)]
    pallas_call x1, Pallas kernels: 2.65 us -> 4.34 us  [body(): call(functools.partial(attention_kernel, n_tp, per_dev, requests, lat_siz...]
    pallas_call x1, Pallas kernels: 5.85 us -> 4.66 us  [body(): call(fetch_kernel, (pltpu.VMEM((pages,) + lat_page, BF16), pltpu.VMEM((pa...]
  transfers between devices with their start and end apart: 24 -> 24, of which waited for: 8 -> 8; matrix products, arithmetic and copies ran while one was open for 1% -> 1% of each run, Pallas kernels for 42% -> 45%
where the time goes in v2:
time: 91.2 us; the launch traced here: 90.7 us
  Pallas kernels  45.4 us (50%)
  starting transfers between devices  30.4 us (33%)
  waiting for transfers between devices  11.2 us (12%)
  between operations  1.78 us (2%)
  other arithmetic  1.06 us (1%)
  local copies, waits for them, and re-layouts  0.97 us (1%)
    ppermute x24, starting transfers between devices, xored(): return lax.ppermute(value, axis, pairs)  30.4 us
    pallas_call x1, Pallas kernels, body(): call(functools.partial(expert_kernel, requests, 256, units), (struct((gro...  18.3 us
    ppermute x24, waiting for transfers between devices, xored(): return lax.ppermute(value, axis, pairs)  11.2 us
    pallas_call x1, Pallas kernels, body(): call(functools.partial(shared_kernel, cuts[1], third_span), (struct((requ...  5.04 us
    pallas_call x1, Pallas kernels, body(): call(fetch_kernel, (pltpu.VMEM((pages,) + lat_page, BF16), pltpu.VMEM((pa...  4.66 us
    pallas_call x1, Pallas kernels, body(): call(functools.partial(attention_kernel, n_tp, per_dev, requests, lat_siz...  4.34 us
    pallas_call x1, Pallas kernels, body(): call(token_weights_kernel, (pltpu.VMEM(w_value_up.shape, BF16), pltpu.VME...  3.05 us
    pallas_call x1, Pallas kernels, body(): call(functools.partial(query_kernel, first_span), (struct((rows, lat_size...  2.68 us
  transfers between devices with their start and end apart: 24, of which 8 were waited for; matrix products, arithmetic and copies ran while one was open for 1% of the time, Pallas kernels for 45%

profile of v2, /device:TPU:0, one launch (start us, length us, event | category | flops | bytes accessed | tf_op | source)
XLA Modules:
  0.0 90.7 jit_solution(4651402170140303887)
XLA Ops:
  2.0 2.7 %shard_map.229 = (bf16[16,576]{1,0:T(8,128)(2,1)S(1)}, bf16[4,2048]{1,0:T(4,128)(2,1)S(1)}, bf16[6,128,512]{2,1,0:T(8,128)(2,1)S(1)}, bf16[10,64,128]{2,1,0:T(8,128)(2,1)S(1)}) custom-call(s32[4,10]{1,0:T(4,128)S(1)} %copy-done.1, s32[1]{0:T(128)} %copy.42.slot_in.refs_1_.refs_0_.slot, bf16[4,2048]{1,0:T(4,128)(2,1)} %refs_5_.1, f32[1,2048]{1,0:T(1,128)} %bitcast.35, ...), custom_call_target="tpu_custom_call" | custom-call | flops 12582912 | bytes 3145728 | tf_op jit(solution)/shard_map/pallas_call | solution.py:666
  4.7 3.0 %collective-permute-start.9 = (bf16[6,128,512]{2,1,0:T(8,128)(2,1)S(1)}, bf16[6,128,512]{2,1,0:T(8,128)(2,1)S(1)}, u32[]{:S(2)}, u32[]{:S(2)}) collective-permute-start(bf16[6,128,512]{2,1,0:T(8,128)(2,1)S(1)} %get-tuple-element.54), channel_id=1, source_target_pairs={{0,16},{4,20},{8,24},{12,28},{16,0},{20,4},{24,8},{28,12},{1,17},{... | collective-permute-start | bytes 2359304 | tf_op jit(solution)/shard_map/ppermute | solution.py:31
  7.8 2.0 %collective-permute-start = (bf16[16,576]{1,0:T(8,128)(2,1)S(1)}, bf16[16,576]{1,0:T(8,128)(2,1)S(1)}, u32[]{:S(2)}, u32[]{:S(2)}) collective-permute-start(bf16[16,576]{1,0:T(8,128)(2,1)S(1)} %get-tuple-element.41._.refs_4_), channel_id=1, source_target_pairs={{0,1},{1,0},{2,3},{3,2},{4,5},{5,4},{6,7},{7,6},{8,9},{9,8},{10,11... | collective-permute-start | bytes 55304 | tf_op jit(solution)/shard_map/ppermute | solution.py:31
  9.8 2.6 %collective-permute-start.1 = (bf16[16,576]{1,0:T(8,128)(2,1)S(1)}, bf16[16,576]{1,0:T(8,128)(2,1)S(1)}, u32[]{:S(2)}, u32[]{:S(2)}) collective-permute-start(bf16[16,576]{1,0:T(8,128)(2,1)S(1)} %get-tuple-element.41._.refs_4_), channel_id=1, source_target_pairs={{0,2},{1,3},{2,0},{3,1},{4,6},{5,7},{6,4},{7,5},{8,10},{9,11},{10,... | collective-permute-start | bytes 55304 | tf_op jit(solution)/shard_map/ppermute | solution.py:31
  12.4 4.7 %shard_map.230 = (bf16[40,128,512]{2,1,0:T(8,128)(2,1)S(1)}, bf16[40,64,128]{2,1,0:T(8,128)(2,1)S(1)}, f32[8,128]{1,0:T(8,128)}) custom-call(s32[4,10]{1,0:T(4,128)S(1)} %copy-done.2, bf16[16,576]{1,0:T(8,128)(2,1)S(1)} %get-tuple-element.41._.refs_4_, bf16[40,128,512]{2,1,0:T(8,128)(2,1)} %lat.7, bf16[40,64,128]{2,1,0:T(8,128)(2,1)} %rope.3), custom_call_target="tpu_custom_call" | custom-call | flops 9437184 | bytes 10878976 | tf_op jit(solution)/shard_map/pallas_call | solution.py:697
  17.1 0.9 collective-permute-done.2.refs_7_
  18.0 4.3 %shard_map.231 = (bf16[16,640]{1,0:T(8,128)(2,1)S(1)}, bf16[16,640]{1,0:T(8,128)(2,1)S(1)}, bf16[16,640]{1,0:T(8,128)(2,1)S(1)}, bf16[16,640]{1,0:T(8,128)(2,1)S...) custom-call(s32[4,10]{1,0:T(4,128)S(1)} %copy-done.2, s32[1]{0:T(128)} %copy.42.slot_in.refs_1_.refs_0_.slot, ...), custom_call_target="tpu_custom_call" | custom-call | flops 167772160 | bytes 5898240 | tf_op jit(solution)/shard_map/pallas_call | solution.py:712
  22.4 2.5 %collective-permute-start.4 = (bf16[16,640]{1,0:T(8,128)(2,1)S(1)}, bf16[16,640]{1,0:T(8,128)(2,1)S(1)}, u32[]{:S(2)}, u32[]{:S(2)}) collective-permute-start(bf16[16,640]{1,0:T(8,128)(2,1)S(1)} %get-tuple-element.46), channel_id=1, source_target_pairs={{0,2},{1,3},{2,0},{3,1},{4,6},{5,7},{6,4},{7,5},{8,10},{9,11},{10,... | collective-permute-start | bytes 61448 | tf_op jit(solution)/shard_map/ppermute | solution.py:31
  24.9 1.9 %collective-permute-start.5 = (bf16[16,640]{1,0:T(8,128)(2,1)S(1)}, bf16[16,640]{1,0:T(8,128)(2,1)S(1)}, u32[]{:S(2)}, u32[]{:S(2)}) collective-permute-start(bf16[16,640]{1,0:T(8,128)(2,1)S(1)} %get-tuple-element.47), channel_id=1, source_target_pairs={{0,3},{1,2},{2,1},{3,0},{4,7},{5,6},{6,5},{7,4},{8,11},{9,10},{10,... | collective-permute-start | bytes 61448 | tf_op jit(solution)/shard_map/ppermute | solution.py:31
  26.8 3.1 %shard_map.232 = (bf16[4,512,128]{2,1,0:T(8,128)(2,1)S(1)}, bf16[512,2048]{1,0:T(8,128)(2,1)S(1)}, f32[4,640]{1,0:T(4,128)S(1)}) custom-call(s32[4]{0:T(128)S(1)} %copy-done.6, bf16[4,2048]{1,0:T(4,128)(2,1)S(1)} %get-tuple-element.48.normed, f32[1,512]{1,0:T(1,128)S(1)} %bitcast.26, bf16[16,640]{1,0:T(8,128)(2,1)S(1)} %get-tuple-element.44._.refs_0_, ...), custom_call_target="tpu_custom_call" | custom-call | flops 9437184 | bytes 4980736 | tf_op jit(solution)/shard_map/pallas_call | solution.py:724
  30.5 0.7 shard_map.233
  31.2 2.4 %collective-permute-start.7 = (bf16[4,2048]{1,0:T(4,128)(2,1)S(1)}, bf16[4,2048]{1,0:T(4,128)(2,1)S(1)}, u32[]{:S(2)}, u32[]{:S(2)}) collective-permute-start(bf16[4,2048]{1,0:T(4,128)(2,1)S(1)} %get-tuple-element.53), channel_id=1, source_target_pairs={{0,2},{1,3},{2,0},{3,1},{4,6},{5,7},{6,4},{7,5},{8,10},{9,11},{10,... | collective-permute-start | bytes 49160 | tf_op jit(solution)/shard_map/ppermute | solution.py:31
  33.7 2.0 %collective-permute-start.8 = (bf16[4,2048]{1,0:T(4,128)(2,1)S(1)}, bf16[4,2048]{1,0:T(4,128)(2,1)S(1)}, u32[]{:S(2)}, u32[]{:S(2)}) collective-permute-start(bf16[4,2048]{1,0:T(4,128)(2,1)S(1)} %get-tuple-element.53), channel_id=1, source_target_pairs={{0,3},{1,2},{2,1},{3,0},{4,7},{5,6},{6,5},{7,4},{8,11},{9,10},{10,... | collective-permute-start | bytes 49160 | tf_op jit(solution)/shard_map/ppermute | solution.py:31
  35.9 3.3 %collective-permute-done.8.refs_4_ = bf16[4,2048]{1,0:T(4,128)(2,1)S(1)} collective-permute-done((bf16[4,2048]{1,0:T(4,128)(2,1)S(1)}, bf16[4,2048]{1,0:T(4,128)(2,1)S(1)}, u32[]{:S(2)}, u32[]{:S(2)}) %collective-permute-start.8) | collective-permute-done | bytes 16416 | tf_op jit(solution)/shard_map/ppermute | solution.py:31
  39.4 1.2 %collective-permute-done.11 = bf16[4,2176]{1,0:T(4,128)(2,1)S(1)} collective-permute-done((bf16[4,2176]{1,0:T(4,128)(2,1)S(1)}, bf16[4,2176]{1,0:T(4,128)(2,1)S(1)}, u32[]{:S(2)}, u32[]{:S(2)}) %collective-permute-start.11) | collective-permute-done | bytes 17440 | tf_op jit(solution)/shard_map/ppermute | solution.py:31
  40.6 1.1 %collective-permute-start.12 = (bf16[8,2176]{1,0:T(8,128)(2,1)S(1)}, bf16[8,2176]{1,0:T(8,128)(2,1)S(1)}, u32[]{:S(2)}, u32[]{:S(2)}) collective-permute-start(bf16[8,2176]{1,0:T(8,128)(2,1)S(1)} %pad_maximum_fusion._.refs_0_), channel_id=1, source_target_pairs={{0,8},{4,12},{8,0},{12,4},{16,24},{20,28},{24,16},{28,20},{1,9},{5... | collective-permute-start | bytes 104456 | tf_op jit(solution)/shard_map/ppermute | solution.py:31
  41.7 2.0 %collective-permute-start.13 = (bf16[8,2176]{1,0:T(8,128)(2,1)S(1)}, bf16[8,2176]{1,0:T(8,128)(2,1)S(1)}, u32[]{:S(2)}, u32[]{:S(2)}) collective-permute-start(bf16[8,2176]{1,0:T(8,128)(2,1)S(1)} %pad_maximum_fusion._.refs_0_), channel_id=1, source_target_pairs={{0,16},{4,20},{8,24},{12,28},{16,0},{20,4},{24,8},{28,12},{1,17},{... | collective-permute-start | bytes 104456 | tf_op jit(solution)/shard_map/ppermute | solution.py:31
  44.3 2.2 %shard_map.235 = (bf16[272,512]{1,0:T(8,128)(2,1)S(1)}, bf16[40,128,512]{2,1,0:T(8,128)(2,1)}, bf16[40,64,128]{2,1,0:T(8,128)(2,1)}) custom-call(s32[4,10]{1,0:T(4,128)S(1)} %copy-done.2, s32[1]{0:T(128)} %copy.42.slot_in.refs_1_.refs_0_.slot, bf16[8,2176]{1,0:T(8,128)(2,1)S(1)} %pad_maximum_fusion._.refs_0_, ...), custom_call_target="tpu_custom_call", output_to_operand_aliasing={{1}: (8, {}), {2}: (9, {})} | custom-call | bytes 1769472 | tf_op jit(solution)/shard_map/pallas_call | solution.py:768
  46.5 2.0 %collective-permute-done.14.refs_3_ = bf16[8,2176]{1,0:T(8,128)(2,1)S(1)} collective-permute-done((bf16[8,2176]{1,0:T(8,128)(2,1)S(1)}, bf16[8,2176]{1,0:T(8,128)(2,1)S(1)}, u32[]{:S(2)}, u32[]{:S(2)}) %collective-permute-start.14) | collective-permute-done | bytes 34848 | tf_op jit(solution)/shard_map/ppermute | solution.py:31
  49.2 18.3 %shard_map.237 = (f32[16,2048]{1,0:T(8,128)S(1)}, bf16[16,2048]{1,0:T(8,128)(2,1)S(1)}) custom-call(s32[1]{0:T(128)} %bitcast.1.rank, bf16[32,2048]{1,0:T(8,128)(2,1)S(1)} %get-tuple-element.62.x, f32[32,64]{1,0:T(8,128)S(1)} %get-tuple-element.63.coef, bf16[2816,2048]{1,0:T(8,128)(2,1)} %bitcast.27, bf16[2816,2048]{1,0:T(8,128)(2,1)} %bitcast.28, ...), custom_call_target="tpu_custom_call" | custom-call | flops 1107296256 | bytes 34603008 | tf_op jit(solution)/shard_map/pallas_call | solution.py:809
  67.8 1.0 %collective-permute-done.16.got = bf16[16,2048]{1,0:T(8,128)(2,1)S(1)} collective-permute-done((bf16[16,2048]{1,0:T(8,128)(2,1)S(1)}, bf16[16,2048]{1,0:T(8,128)(2,1)S(1)}, u32[]{:S(2)}, u32[]{:S(2)}) %collective-permute-start.16) | collective-permute-done | bytes 65568 | tf_op jit(solution)/shard_map/ppermute | solution.py:31
  68.9 1.0 %collective-permute-start.17 = (bf16[4,2048]{1,0:T(4,128)(2,1)S(1)}, bf16[4,2048]{1,0:T(4,128)(2,1)S(1)}, u32[]{:S(2)}, u32[]{:S(2)}) collective-permute-start(bf16[4,2048]{1,0:T(4,128)(2,1)S(1)} %get-tuple-element.69), channel_id=1, source_target_pairs={{0,8},{4,12},{8,0},{12,4},{16,24},{20,28},{24,16},{28,20},{1,9},{5... | collective-permute-start | bytes 49160 | tf_op jit(solution)/shard_map/ppermute | solution.py:31
  69.9 1.5 %collective-permute-start.18 = (bf16[4,2048]{1,0:T(4,128)(2,1)S(1)}, bf16[4,2048]{1,0:T(4,128)(2,1)S(1)}, u32[]{:S(2)}, u32[]{:S(2)}) collective-permute-start(bf16[4,2048]{1,0:T(4,128)(2,1)S(1)} %get-tuple-element.70), channel_id=1, source_target_pairs={{0,16},{4,20},{8,24},{12,28},{16,0},{20,4},{24,8},{28,12},{1,17},{... | collective-permute-start | bytes 49160 | tf_op jit(solution)/shard_map/ppermute | solution.py:31
  71.4 1.0 %collective-permute-start.19 = (bf16[4,2048]{1,0:T(4,128)(2,1)S(1)}, bf16[4,2048]{1,0:T(4,128)(2,1)S(1)}, u32[]{:S(2)}, u32[]{:S(2)}) collective-permute-start(bf16[4,2048]{1,0:T(4,128)(2,1)S(1)} %get-tuple-element.71), channel_id=1, source_target_pairs={{0,24},{4,28},{8,16},{12,20},{16,8},{20,12},{24,0},{28,4},{1,25},{... | collective-permute-start | bytes 49160 | tf_op jit(solution)/shard_map/ppermute | solution.py:31
  72.5 5.0 %shard_map.239 = (f32[4,2048]{1,0:T(4,128)S(1)}, bf16[256,512]{1,0:T(8,128)(2,1)S(1)}) custom-call(s32[4,10]{1,0:T(4,128)S(1)} %copy-done.2, s32[1]{0:T(128)} %copy.42.slot_in.refs_1_.refs_0_.slot, bf16[4,2048]{1,0:T(4,128)(2,1)S(1)} %get-tuple-element.67.x, bf16[704,2048]{1,0:T(8,128)(2,1)} %bitcast.30, bf16[704,2048]{1,0:T(8,128)(2,1)} %bitcast.31, ...), custom_call_target="tpu_custom_call" | custom-call | flops 34603008 | bytes 8650752 | tf_op jit(solution)/shard_map/pallas_call | solution.py:834
  77.6 3.0 %collective-permute-start.21 = (bf16[4,2048]{1,0:T(4,128)(2,1)S(1)}, bf16[4,2048]{1,0:T(4,128)(2,1)S(1)}, u32[]{:S(2)}, u32[]{:S(2)}) collective-permute-start(bf16[4,2048]{1,0:T(4,128)(2,1)S(1)} %get-tuple-element.73), channel_id=1, source_target_pairs={{0,2},{1,3},{2,0},{3,1},{4,6},{5,7},{6,4},{7,5},{8,10},{9,11},{10,... | collective-permute-start | bytes 49160 | tf_op jit(solution)/shard_map/ppermute | solution.py:31
  80.6 1.4 %collective-permute-start.22 = (bf16[4,2048]{1,0:T(4,128)(2,1)S(1)}, bf16[4,2048]{1,0:T(4,128)(2,1)S(1)}, u32[]{:S(2)}, u32[]{:S(2)}) collective-permute-start(bf16[4,2048]{1,0:T(4,128)(2,1)S(1)} %get-tuple-element.73), channel_id=1, source_target_pairs={{0,3},{1,2},{2,1},{3,0},{4,7},{5,6},{6,5},{7,4},{8,11},{9,10},{10,... | collective-permute-start | bytes 49160 | tf_op jit(solution)/shard_map/ppermute | solution.py:31
  82.3 2.0 %collective-permute-start.23 = (bf16[256,512]{1,0:T(8,128)(2,1)S(1)}, bf16[256,512]{1,0:T(8,128)(2,1)S(1)}, u32[]{:S(2)}, u32[]{:S(2)}) collective-permute-start(bf16[256,512]{1,0:T(8,128)(2,1)S(1)} %get-tuple-element.74), channel_id=1, source_target_pairs={{0,16},{4,20},{8,24},{12,28},{16,0},{20,4},{24,8},{28,12},{1,17},{... | collective-permute-start | bytes 786440 | tf_op jit(solution)/shard_map/ppermute | solution.py:31
  84.3 2.4 %shard_map.241 = (bf16[40,128,512]{2,1,0:T(8,128)(2,1)}, bf16[40,64,128]{2,1,0:T(8,128)(2,1)}) custom-call(s32[4,10]{1,0:T(4,128)S(1)} %copy-done.2, s32[1]{0:T(128)} %copy.42.slot_in.refs_1_.refs_0_.slot, s32[4]{0:T(128)S(1)} %add_reduce_fusion.lengths, s32[1]{0:T(128)} %bitcast.3.refs_3_.rank, ...), custom_call_target="tpu_custom_call", output_to_operand_aliasing={{0}: (8, {}), {1}: (9, {})} | custom-call | bytes 589824 | tf_op jit(solution)/shard_map/pallas_call | solution.py:869
  86.7 0.7 add_convert_fusion
  87.4 1.9 %collective-permute-done.23.got = bf16[256,512]{1,0:T(8,128)(2,1)S(1)} collective-permute-done((bf16[256,512]{1,0:T(8,128)(2,1)S(1)}, bf16[256,512]{1,0:T(8,128)(2,1)S(1)}, u32[]{:S(2)}, u32[]{:S(2)}) %collective-permute-start.23) | collective-permute-done | bytes 262176 | tf_op jit(solution)/shard_map/ppermute | solution.py:31
  89.2 1.3 %shard_map.242 = bf16[40,128,512]{2,1,0:T(8,128)(2,1)} custom-call(s32[4,10]{1,0:T(4,128)S(1)} %copy-done.2, s32[1]{0:T(128)} %copy.42.slot_in.refs_1_.refs_0_.slot, s32[4]{0:T(128)S(1)} %add_reduce_fusion.lengths, s32[1]{0:T(128)} %bitcast.3.refs_3_.rank, f32[4,512]{1,0:T(4,128)S(1)} %slice.39.new_lat, ...), custom_call_target="tpu_custom_call", output_to_operand_aliasing={{}: (6, {})} | custom-call | bytes 589824 | tf_op jit(solution)/shard_map/pallas_call | solution.py:896
  (60 shorter events, 4.0 us)
Async XLA Ops:
  0.6 11.8 %copy-start.2 = (s32[4,10]{1,0:T(4,128)S(1)}, s32[4,10]{1,0:T(4,128)}, u32[]{:S(2)}) copy-start(s32[4,10]{1,0:T(4,128)} %table.9) | copy-start | bytes 484
  1.3 0.7 copy-start.1
  4.7 13.3 %copy-start.6 = (s32[4]{0:T(128)S(1)}, s32[4]{0:T(128)}, u32[]{:S(2)}) copy-start(s32[4]{0:T(128)} %lengths.1) | copy-start | bytes 52
  4.7 34.5 %collective-permute-start.9 = (bf16[6,128,512]{2,1,0:T(8,128)(2,1)S(1)}, bf16[6,128,512]{2,1,0:T(8,128)(2,1)S(1)}, u32[]{:S(2)}, u32[]{:S(2)}) collective-permute-start(bf16[6,128,512]{2,1,0:T(8,128)(2,1)S(1)} %get-tuple-element.54), channel_id=1, source_target_pairs={{0,16},{4,20},{8,24},{12,28},{16,0},{20,4},{24,8},{28,12},{1,17},{... | collective-permute-start | bytes 2359304 | tf_op jit(solution)/shard_map/ppermute | solution.py:31
  7.7 31.5 %collective-permute-start.10 = (bf16[10,64,128]{2,1,0:T(8,128)(2,1)S(1)}, bf16[10,64,128]{2,1,0:T(8,128)(2,1)S(1)}, u32[]{:S(2)}, u32[]{:S(2)}) collective-permute-start(bf16[10,64,128]{2,1,0:T(8,128)(2,1)S(1)} %get-tuple-element.55), channel_id=1, source_target_pairs={{0,16},{4,20},{8,24},{12,28},{16,0},{20,4},{24,8},{28,12},{1,17},{... | collective-permute-start | bytes 491528 | tf_op jit(solution)/shard_map/ppermute | solution.py:31
  7.8 9.3 %collective-permute-start = (bf16[16,576]{1,0:T(8,128)(2,1)S(1)}, bf16[16,576]{1,0:T(8,128)(2,1)S(1)}, u32[]{:S(2)}, u32[]{:S(2)}) collective-permute-start(bf16[16,576]{1,0:T(8,128)(2,1)S(1)} %get-tuple-element.41._.refs_4_), channel_id=1, source_target_pairs={{0,1},{1,0},{2,3},{3,2},{4,5},{5,4},{6,7},{7,6},{8,9},{9,8},{10,11... | collective-permute-start | bytes 55304 | tf_op jit(solution)/shard_map/ppermute | solution.py:31
  9.8 7.3 %collective-permute-start.1 = (bf16[16,576]{1,0:T(8,128)(2,1)S(1)}, bf16[16,576]{1,0:T(8,128)(2,1)S(1)}, u32[]{:S(2)}, u32[]{:S(2)}) collective-permute-start(bf16[16,576]{1,0:T(8,128)(2,1)S(1)} %get-tuple-element.41._.refs_4_), channel_id=1, source_target_pairs={{0,2},{1,3},{2,0},{3,1},{4,6},{5,7},{6,4},{7,5},{8,10},{9,11},{10,... | collective-permute-start | bytes 55304 | tf_op jit(solution)/shard_map/ppermute | solution.py:31
  12.4 5.6 %collective-permute-start.2 = (bf16[16,576]{1,0:T(8,128)(2,1)S(1)}, bf16[16,576]{1,0:T(8,128)(2,1)S(1)}, u32[]{:S(2)}, u32[]{:S(2)}) collective-permute-start(bf16[16,576]{1,0:T(8,128)(2,1)S(1)} %get-tuple-element.41._.refs_4_), channel_id=1, source_target_pairs={{0,3},{1,2},{2,1},{3,0},{4,7},{5,6},{6,5},{7,4},{8,11},{9,10},{10,... | collective-permute-start | bytes 55304 | tf_op jit(solution)/shard_map/ppermute | solution.py:31
  12.4 14.4 %copy-start.5 = (f32[512]{0:T(512)S(1)}, f32[512]{0:T(512)}, u32[]{:S(2)}) copy-start(f32[512]{0:T(512)} %param.31) | copy-start | bytes 6148
  22.3 16.9 %copy-start.3 = (bf16[4,2048]{1,0:T(4,128)(2,1)S(1)}, bf16[4,2048]{1,0:T(4,128)(2,1)}, u32[]{:S(2)}) copy-start(bf16[4,2048]{1,0:T(4,128)(2,1)} %refs_5_.1) | copy-start | bytes 49156
  22.3 16.9 %copy-start.4 = (f32[2048]{0:T(1024)S(1)}, f32[2048]{0:T(1024)}, u32[]{:S(2)}) copy-start(f32[2048]{0:T(1024)} %param.35) | copy-start | bytes 24580
  22.3 21.8 %copy-start.7 = (s32[32,6]{0,1:T(8,128)S(1)}, s32[32,6]{0,1:T(8,128)}, u32[]{:S(2)}) copy-start(s32[32,6]{0,1:T(8,128)} %param.37) | copy-start | bytes 2308
  22.4 7.5 %collective-permute-start.3 = (bf16[16,640]{1,0:T(8,128)(2,1)S(1)}, bf16[16,640]{1,0:T(8,128)(2,1)S(1)}, u32[]{:S(2)}, u32[]{:S(2)}) collective-permute-start(bf16[16,640]{1,0:T(8,128)(2,1)S(1)} %get-tuple-element.45), channel_id=1, source_target_pairs={{0,1},{1,0},{2,3},{3,2},{4,5},{5,4},{6,7},{7,6},{8,9},{9,8},{10,11... | collective-permute-start | bytes 61448 | tf_op jit(solution)/shard_map/ppermute | solution.py:31
  22.4 7.4 %collective-permute-start.4 = (bf16[16,640]{1,0:T(8,128)(2,1)S(1)}, bf16[16,640]{1,0:T(8,128)(2,1)S(1)}, u32[]{:S(2)}, u32[]{:S(2)}) collective-permute-start(bf16[16,640]{1,0:T(8,128)(2,1)S(1)} %get-tuple-element.46), channel_id=1, source_target_pairs={{0,2},{1,3},{2,0},{3,1},{4,6},{5,7},{6,4},{7,5},{8,10},{9,11},{10,... | collective-permute-start | bytes 61448 | tf_op jit(solution)/shard_map/ppermute | solution.py:31
  24.9 5.6 %collective-permute-start.5 = (bf16[16,640]{1,0:T(8,128)(2,1)S(1)}, bf16[16,640]{1,0:T(8,128)(2,1)S(1)}, u32[]{:S(2)}, u32[]{:S(2)}) collective-permute-start(bf16[16,640]{1,0:T(8,128)(2,1)S(1)} %get-tuple-element.47), channel_id=1, source_target_pairs={{0,3},{1,2},{2,1},{3,0},{4,7},{5,6},{6,5},{7,4},{8,11},{9,10},{10,... | collective-permute-start | bytes 61448 | tf_op jit(solution)/shard_map/ppermute | solution.py:31
  31.2 4.4 %collective-permute-start.6 = (bf16[4,2048]{1,0:T(4,128)(2,1)S(1)}, bf16[4,2048]{1,0:T(4,128)(2,1)S(1)}, u32[]{:S(2)}, u32[]{:S(2)}) collective-permute-start(bf16[4,2048]{1,0:T(4,128)(2,1)S(1)} %get-tuple-element.53), channel_id=1, source_target_pairs={{0,1},{1,0},{2,3},{3,2},{4,5},{5,4},{6,7},{7,6},{8,9},{9,8},{10,11... | collective-permute-start | bytes 49160 | tf_op jit(solution)/shard_map/ppermute | solution.py:31
  31.2 4.7 %collective-permute-start.7 = (bf16[4,2048]{1,0:T(4,128)(2,1)S(1)}, bf16[4,2048]{1,0:T(4,128)(2,1)S(1)}, u32[]{:S(2)}, u32[]{:S(2)}) collective-permute-start(bf16[4,2048]{1,0:T(4,128)(2,1)S(1)} %get-tuple-element.53), channel_id=1, source_target_pairs={{0,2},{1,3},{2,0},{3,1},{4,6},{5,7},{6,4},{7,5},{8,10},{9,11},{10,... | collective-permute-start | bytes 49160 | tf_op jit(solution)/shard_map/ppermute | solution.py:31
  33.7 5.5 %collective-permute-start.8 = (bf16[4,2048]{1,0:T(4,128)(2,1)S(1)}, bf16[4,2048]{1,0:T(4,128)(2,1)S(1)}, u32[]{:S(2)}, u32[]{:S(2)}) collective-permute-start(bf16[4,2048]{1,0:T(4,128)(2,1)S(1)} %get-tuple-element.53), channel_id=1, source_target_pairs={{0,3},{1,2},{2,1},{3,0},{4,7},{5,6},{6,5},{7,4},{8,11},{9,10},{10,... | collective-permute-start | bytes 49160 | tf_op jit(solution)/shard_map/ppermute | solution.py:31
  39.3 1.3 %collective-permute-start.11 = (bf16[4,2176]{1,0:T(4,128)(2,1)S(1)}, bf16[4,2176]{1,0:T(4,128)(2,1)S(1)}, u32[]{:S(2)}, u32[]{:S(2)}) collective-permute-start(bf16[4,2176]{1,0:T(4,128)(2,1)S(1)} %get-tuple-element.56), channel_id=1, source_target_pairs={{0,4},{4,0},{8,12},{12,8},{16,20},{20,16},{24,28},{28,24},{1,5},{5... | collective-permute-start | bytes 52232 | tf_op jit(solution)/shard_map/ppermute | solution.py:31
  40.6 5.9 %collective-permute-start.12 = (bf16[8,2176]{1,0:T(8,128)(2,1)S(1)}, bf16[8,2176]{1,0:T(8,128)(2,1)S(1)}, u32[]{:S(2)}, u32[]{:S(2)}) collective-permute-start(bf16[8,2176]{1,0:T(8,128)(2,1)S(1)} %pad_maximum_fusion._.refs_0_), channel_id=1, source_target_pairs={{0,8},{4,12},{8,0},{12,4},{16,24},{20,28},{24,16},{28,20},{1,9},{5... | collective-permute-start | bytes 104456 | tf_op jit(solution)/shard_map/ppermute | solution.py:31
  41.7 4.8 %collective-permute-start.13 = (bf16[8,2176]{1,0:T(8,128)(2,1)S(1)}, bf16[8,2176]{1,0:T(8,128)(2,1)S(1)}, u32[]{:S(2)}, u32[]{:S(2)}) collective-permute-start(bf16[8,2176]{1,0:T(8,128)(2,1)S(1)} %pad_maximum_fusion._.refs_0_), channel_id=1, source_target_pairs={{0,16},{4,20},{8,24},{12,28},{16,0},{20,4},{24,8},{28,12},{1,17},{... | collective-permute-start | bytes 104456 | tf_op jit(solution)/shard_map/ppermute | solution.py:31
  43.7 4.8 %collective-permute-start.14 = (bf16[8,2176]{1,0:T(8,128)(2,1)S(1)}, bf16[8,2176]{1,0:T(8,128)(2,1)S(1)}, u32[]{:S(2)}, u32[]{:S(2)}) collective-permute-start(bf16[8,2176]{1,0:T(8,128)(2,1)S(1)} %pad_maximum_fusion._.refs_0_), channel_id=1, source_target_pairs={{0,24},{4,28},{8,16},{12,20},{16,8},{20,12},{24,0},{28,4},{1,25},{... | collective-permute-start | bytes 104456 | tf_op jit(solution)/shard_map/ppermute | solution.py:31
  44.3 4.3 %copy-start = (bf16[2048,64]{0,1:T(8,128)(2,1)S(1)}, bf16[2048,64]{0,1:T(8,128)(2,1)}, u32[]{:S(2)}) copy-start(bf16[2048,64]{0,1:T(8,128)(2,1)} %param.36) | copy-start | bytes 786436
  49.1 18.5 %collective-permute-start.15 = (bf16[272,512]{1,0:T(8,128)(2,1)S(1)}, bf16[272,512]{1,0:T(8,128)(2,1)S(1)}, u32[]{:S(2)}, u32[]{:S(2)}) collective-permute-start(bf16[272,512]{1,0:T(8,128)(2,1)S(1)} %get-tuple-element.61), channel_id=1, source_target_pairs={{0,16},{4,20},{8,24},{12,28},{16,0},{20,4},{24,8},{28,12},{1,17},{... | collective-permute-start | bytes 835592 | tf_op jit(solution)/shard_map/ppermute | solution.py:31
  67.5 1.3 %collective-permute-start.16 = (bf16[16,2048]{1,0:T(8,128)(2,1)S(1)}, bf16[16,2048]{1,0:T(8,128)(2,1)S(1)}, u32[]{:S(2)}, u32[]{:S(2)}) collective-permute-start(bf16[16,2048]{1,0:T(8,128)(2,1)S(1)} %get-tuple-element.65), channel_id=1, source_target_pairs={{0,4},{4,0},{8,12},{12,8},{16,20},{20,16},{24,28},{28,24},{1,5},{5... | collective-permute-start | bytes 196616 | tf_op jit(solution)/shard_map/ppermute | solution.py:31
  68.9 8.6 %collective-permute-start.17 = (bf16[4,2048]{1,0:T(4,128)(2,1)S(1)}, bf16[4,2048]{1,0:T(4,128)(2,1)S(1)}, u32[]{:S(2)}, u32[]{:S(2)}) collective-permute-start(bf16[4,2048]{1,0:T(4,128)(2,1)S(1)} %get-tuple-element.69), channel_id=1, source_target_pairs={{0,8},{4,12},{8,0},{12,4},{16,24},{20,28},{24,16},{28,20},{1,9},{5... | collective-permute-start | bytes 49160 | tf_op jit(solution)/shard_map/ppermute | solution.py:31
  69.9 7.6 %collective-permute-start.18 = (bf16[4,2048]{1,0:T(4,128)(2,1)S(1)}, bf16[4,2048]{1,0:T(4,128)(2,1)S(1)}, u32[]{:S(2)}, u32[]{:S(2)}) collective-permute-start(bf16[4,2048]{1,0:T(4,128)(2,1)S(1)} %get-tuple-element.70), channel_id=1, source_target_pairs={{0,16},{4,20},{8,24},{12,28},{16,0},{20,4},{24,8},{28,12},{1,17},{... | collective-permute-start | bytes 49160 | tf_op jit(solution)/shard_map/ppermute | solution.py:31
  71.4 6.1 %collective-permute-start.19 = (bf16[4,2048]{1,0:T(4,128)(2,1)S(1)}, bf16[4,2048]{1,0:T(4,128)(2,1)S(1)}, u32[]{:S(2)}, u32[]{:S(2)}) collective-permute-start(bf16[4,2048]{1,0:T(4,128)(2,1)S(1)} %get-tuple-element.71), channel_id=1, source_target_pairs={{0,24},{4,28},{8,16},{12,20},{16,8},{20,12},{24,0},{28,4},{1,25},{... | collective-permute-start | bytes 49160 | tf_op jit(solution)/shard_map/ppermute | solution.py:31
  77.6 9.1 %collective-permute-start.20 = (bf16[4,2048]{1,0:T(4,128)(2,1)S(1)}, bf16[4,2048]{1,0:T(4,128)(2,1)S(1)}, u32[]{:S(2)}, u32[]{:S(2)}) collective-permute-start(bf16[4,2048]{1,0:T(4,128)(2,1)S(1)} %get-tuple-element.73), channel_id=1, source_target_pairs={{0,1},{1,0},{2,3},{3,2},{4,5},{5,4},{6,7},{7,6},{8,9},{9,8},{10,11... | collective-permute-start | bytes 49160 | tf_op jit(solution)/shard_map/ppermute | solution.py:31
  77.6 9.0 %collective-permute-start.21 = (bf16[4,2048]{1,0:T(4,128)(2,1)S(1)}, bf16[4,2048]{1,0:T(4,128)(2,1)S(1)}, u32[]{:S(2)}, u32[]{:S(2)}) collective-permute-start(bf16[4,2048]{1,0:T(4,128)(2,1)S(1)} %get-tuple-element.73), channel_id=1, source_target_pairs={{0,2},{1,3},{2,0},{3,1},{4,6},{5,7},{6,4},{7,5},{8,10},{9,11},{10,... | collective-permute-start | bytes 49160 | tf_op jit(solution)/shard_map/ppermute | solution.py:31
  80.6 6.1 %collective-permute-start.22 = (bf16[4,2048]{1,0:T(4,128)(2,1)S(1)}, bf16[4,2048]{1,0:T(4,128)(2,1)S(1)}, u32[]{:S(2)}, u32[]{:S(2)}) collective-permute-start(bf16[4,2048]{1,0:T(4,128)(2,1)S(1)} %get-tuple-element.73), channel_id=1, source_target_pairs={{0,3},{1,2},{2,1},{3,0},{4,7},{5,6},{6,5},{7,4},{8,11},{9,10},{10,... | collective-permute-start | bytes 49160 | tf_op jit(solution)/shard_map/ppermute | solution.py:31
  82.3 6.9 %collective-permute-start.23 = (bf16[256,512]{1,0:T(8,128)(2,1)S(1)}, bf16[256,512]{1,0:T(8,128)(2,1)S(1)}, u32[]{:S(2)}, u32[]{:S(2)}) collective-permute-start(bf16[256,512]{1,0:T(8,128)(2,1)S(1)} %get-tuple-element.74), channel_id=1, source_target_pairs={{0,16},{4,20},{8,24},{12,28},{16,0},{20,4},{24,8},{28,12},{1,17},{... | collective-permute-start | bytes 786440 | tf_op jit(solution)/shard_map/ppermute | solution.py:31

commit v3 on v2

--- a/solution.py
+++ b/solution.py
@@ -327,7 +327,7 @@
 
 def order_kernel(groups, requests, rank, route_ids, router, *refs):
     pieces = refs[:groups]
-    x_out, coef_out, own_out, _ = refs[groups + 1 :]
+    x_out, coef_out, _ = refs[groups + 1 :]
     size = router.shape[1]
     wide = jnp.concatenate([p[...].astype(F32) for p in pieces], axis=0)
     rows = wide.shape[0]
@@ -342,9 +342,7 @@
     )
     column = lax.broadcasted_iota(jnp.int32, (rows, rows), 1)
     picks = (column == source).astype(F32).astype(BF16)
-    x = jnp.dot(picks, wide[:, :size].astype(BF16), preferred_element_type=F32)
-    own_out[...] = x[:requests, :].astype(BF16)
-    x = x.astype(BF16)
+    x = jnp.dot(picks, wide[:, :size].astype(BF16), preferred_element_type=F32).astype(BF16)
     x_out[...] = x
     gates = jax.nn.sigmoid(lax.dot_general(x, router[...], NT, preferred_element_type=F32))
     home = (place ^ rank[0]) * requests + row % requests
@@ -415,7 +413,8 @@
 
 
 def shared_kernel(
-    first, count, table, slot, x, gate, up, down, lat, _, out, lat_out, gate_v, up_v, down_v, sems, page_sems,
+    first, count, table, slot, rows, h_one, new, _, gate, up, down, lat,
+    out, next_out, gate_v, up_v, down_v, sems, page_sems,
 ):
     copies = [
         pltpu.make_async_copy(gate, gate_v, sems.at[0]),
@@ -424,21 +423,32 @@
     ]
     for copy in copies:
         copy.start()
-    pages = copy_pages(table, slot, lat, lat_out, page_sems, first, count)
+    pages = copy_pages(table, slot, lat, next_out, page_sems, first, count)
+    x = rows[:, : gate.shape[1]]
     copies[0].wait()
-    gate_val = lax.dot_general(x[...], gate_v[...], NT, preferred_element_type=F32)
+    gate_val = lax.dot_general(x, gate_v[...], NT, preferred_element_type=F32)
     copies[1].wait()
-    up_val = lax.dot_general(x[...], up_v[...], NT, preferred_element_type=F32)
+    up_val = lax.dot_general(x, up_v[...], NT, preferred_element_type=F32)
     hid = (silu(gate_val) * up_val).astype(BF16)
     copies[2].wait()
+    shared = jnp.dot(hid, down_v[...], preferred_element_type=F32)
+    out[...] = shared
+    every = jnp.concatenate([h_one[...].astype(F32), new[...], shared], axis=1)
+    row = lax.broadcasted_iota(jnp.int32, every.shape, 0)
+    every = jnp.sum(jnp.where(row == slot[0], every, 0.0), axis=0, keepdims=True)
+    lat_size = next_out.shape[1]
+    lines = [every[:, b : b + lat_size] for b in range(0, every.shape[1], lat_size)]
+    lines[-1] = jnp.pad(lines[-1], ((0, 0), (0, lat_size - lines[-1].shape[1])))
+    lines.append(jnp.zeros((ROWS - len(lines), lat_size), F32))
+    next_out[count * PAGE :, :] = jnp.concatenate(lines, axis=0).astype(BF16)
     for copy in pages:
         copy.wait()
-    out[...] = jnp.dot(hid, down_v[...], preferred_element_type=F32)
-
-
-def total_kernel(own, shared, *refs):
+
+
+def total_kernel(slot, got, own, shared, _, *refs):
     others, (total, sent) = refs[:-2], refs[-2:]
-    value = own[...] + shared[...]
+    row = lax.broadcasted_iota(jnp.int32, own.shape, 0)
+    value = own[...] + jnp.where(row == slot[0], got[...].astype(F32), shared[...])
     for other in others:
         value += other[...].astype(F32)
     total[...] = value
@@ -455,36 +465,29 @@
 
 
 def cache_kernel(
-    first, count, table, slot, _, h_one, new, lat, got_lat, got_rope, lat_in, rope_in,
-    next_out, lat_out, rope_out, lat_v, rope_v, page_sems, got_sems, sems,
+    first, table, slot, _, got_lat, got_rope, lat_in, rope_in,
+    lat_out, rope_out, token, lat_v, rope_v, got_sems, sems,
 ):
     del lat_in, rope_in
     per_dev = table.shape[1]
     moved = slot[0]
+    token[...] = jnp.zeros_like(token)
     fetches = [
-        pltpu.make_async_copy(got_lat, lat_v, got_sems.at[0]),
-        pltpu.make_async_copy(got_rope, rope_v, got_sems.at[1]),
+        pltpu.make_async_copy(got_rope, rope_v, got_sems.at[0]),
+        pltpu.make_async_copy(got_lat, lat_v, got_sems.at[1]),
     ]
     for copy in fetches:
         copy.start()
-    copies = copy_pages(table, slot, lat, next_out, page_sems, first, count)
-    both = jnp.concatenate([h_one[...].astype(F32), new[...]], axis=1)
-    row = lax.broadcasted_iota(jnp.int32, both.shape, 0)
-    both = jnp.sum(jnp.where(row == moved, both, 0.0), axis=0, keepdims=True)
-    lat_size = next_out.shape[1]
-    lines = [both[:, b : b + lat_size] for b in range(0, both.shape[1], lat_size)]
-    lines[-1] = jnp.pad(lines[-1], ((0, 0), (0, lat_size - lines[-1].shape[1])))
-    lines.append(jnp.zeros((ROWS - len(lines), lat_size), F32))
-    next_out[count * PAGE :, :] = jnp.concatenate(lines, axis=0).astype(BF16)
     for copy in fetches:
         copy.wait()
+    copies = []
     for j in range(per_dev):
         page = table[moved, j]
         if j < first:
             copies.append(pltpu.make_async_copy(lat_v.at[j], lat_out.at[page], sems.at[0, j]))
-            copies[-1].start()
         copies.append(pltpu.make_async_copy(rope_v.at[j], rope_out.at[page], sems.at[1, j]))
-        copies[-1].start()
+    for copy in copies:
+        copy.start()
     for copy in copies:
         copy.wait()
 
@@ -582,37 +585,6 @@
         def _():
             lat_write(r).wait()
     for copy in pages:
-        copy.wait()
-
-
-def last_kernel(first, table, slot, lengths, rank, new_lat, got, _, lat_out, pages, in_sem, sems):
-    per_dev = table.shape[1]
-    moved = slot[0]
-    count = per_dev - first
-    fetch = pltpu.make_async_copy(got, pages, in_sem.at[0])
-    fetch.start()
-    fetch.wait()
-    owned, local, _, inside, group = token_spot(moved, table, lengths, rank)
-
-    @pl.when(owned & (local >= first))
-    def _():
-        index = jnp.maximum(local - first, 0)
-        piece = pl.ds(pl.multiple_of(index * PAGE + group, 16), 16)
-        tile = pages[piece, :].astype(F32)
-        row = lax.broadcasted_iota(jnp.int32, tile.shape, 0)
-        pages[piece, :] = jnp.where(
-            row == inside - group, new_lat[pl.ds(moved, 1), :], tile
-        ).astype(BF16)
-
-    copies = [
-        pltpu.make_async_copy(
-            pages.at[pl.ds(j * PAGE, PAGE)], lat_out.at[table[moved, first + j]], sems.at[j]
-        )
-        for j in range(count)
-    ]
-    for copy in copies:
-        copy.start()
-    for copy in copies:
         copy.wait()
 
 
@@ -655,8 +627,8 @@
     rep_one = lax.axis_index("rep").astype(jnp.int32)[None]
     page_bytes = PAGE * (lat_size + ROPE) * 2
     dma = pltpu.SemaphoreType.DMA
-    cuts = (per_dev * 6 // 10, per_dev * 8 // 10)
-    first_span, second_span, third_span = cuts[0], cuts[1] - cuts[0], per_dev - cuts[1]
+    first_span = per_dev * 6 // 10
+    second_span = per_dev - first_span
     lat_page = lat_pool.shape[1:]
     rope_page = rope_pool.shape[1:]
     lat_hbm, rope_hbm = in_hbm(lat_pool), in_hbm(rope_pool)
@@ -765,49 +737,47 @@
     pair = jnp.concatenate([ffn_row, xored(ffn_row, "rep", 1)], axis=0)
     pieces = [pair] + [xored(pair, "rep", 2 * k) for k in range(1, groups)]
 
-    out_second, lat_most, rope_most = call(
-        functools.partial(cache_kernel, first_span, second_span),
+    shared_part, out_second = call(
+        functools.partial(shared_kernel, first_span, second_span),
         (
+            struct((requests, size), F32),
             struct((second_span * PAGE + ROWS, lat_size), BF16),
-            struct(lat_pool.shape, BF16),
-            struct(rope_pool.shape, BF16),
         ),
-        [SMEM] * 2 + [VMEM] * 3 + [ANY] * 5,
-        (VMEM, ANY, ANY),
+        [SMEM, SMEM] + [VMEM] * 4 + [ANY] * 4,
+        (VMEM, VMEM),
         [
-            pltpu.VMEM((first_span,) + lat_page, BF16),
-            pltpu.VMEM((per_dev,) + rope_page, BF16),
+            pltpu.VMEM((shared_gate.shape[1], size), BF16),
+            pltpu.VMEM((shared_gate.shape[1], size), BF16),
+            pltpu.VMEM(shared_down.shape, BF16),
+            dma((3,)),
             dma((second_span,)),
-            dma((2,)),
-            dma((2, per_dev)),
         ],
-        vmem=4,
-        nbytes=2 * first_span * page_bytes,
-        aliases={8: 1, 9: 2},
+        vmem=12,
+        flops=6 * requests * shared_gate.size,
+        nbytes=6 * shared_gate.size,
     )(
-        page_table, move_slot, pair, h_one, new, lat_hbm, got_first, got_rope,
-        lat_most, rope_most,
+        page_table, move_slot, ffn_row, h_one, new, pair, in_hbm(shared_gate.T),
+        in_hbm(shared_up.T), in_hbm(shared_down), lat_hbm,
     )
-    x_all, coef, x_own, out_second = call(
+    x_all, coef, out_second = call(
         functools.partial(order_kernel, groups, requests),
         (
             struct((everyone, size), BF16),
             struct((everyone, w_router.shape[1]), F32),
-            struct((requests, size), BF16),
             struct(out_second.shape, BF16),
         ),
         [SMEM] + [VMEM] * (groups + 3),
-        (VMEM,) * 4,
+        (VMEM,) * 3,
         vmem=6,
         flops=4 * everyone * size * everyone,
         nbytes=4 * everyone * size,
-        aliases={3 + groups: 3},
+        aliases={3 + groups: 2},
     )(rep_one, route_ids, w_router.T, *pieces, out_second)
     got_second = xored(out_second, "rep", half)
-    got_row = got_second[second_span * PAGE :].reshape(1, -1)[:, : size + width]
+    got_row = got_second[second_span * PAGE :].reshape(1, -1)[:, : size + width + size]
 
     kept, sent = call(
-        functools.partial(expert_kernel, requests, 256, units),
+        functools.partial(expert_kernel, requests, 512, units),
         (
             struct((groups * requests, size), F32),
             struct((groups * requests, size), BF16),
@@ -815,7 +785,7 @@
         [SMEM] + [VMEM] * 2 + [ANY] * 3,
         (VMEM, VMEM),
         [pltpu.VMEM((local_experts * units, size), BF16)] * 3
-        + [pltpu.VMEM((everyone, size), F32), dma((3, pl.cdiv(local_experts * units, 256)))],
+        + [pltpu.VMEM((everyone, size), F32), dma((3, pl.cdiv(local_experts * units, 512)))],
         vmem=42,
         flops=6 * everyone * expert_gate.size,
         nbytes=6 * expert_gate.size,
@@ -831,43 +801,38 @@
         nbytes=8 * everyone * size,
     )(kept, xored(sent, "rep", 1), got_second)
     others = [xored(summed[k], "rep", 2 * k) for k in range(1, groups)]
-    shared_part, out_third = call(
-        functools.partial(shared_kernel, cuts[1], third_span),
-        (struct((requests, size), F32), struct((third_span * PAGE, lat_size), BF16)),
-        [SMEM, SMEM, VMEM] + [ANY] * 5,
-        (VMEM, VMEM),
+    lat_most, rope_most, cache_token = call(
+        functools.partial(cache_kernel, first_span),
+        (struct(lat_pool.shape, BF16), struct(rope_pool.shape, BF16), struct((8, LANES), F32)),
+        [SMEM] * 2 + [VMEM] + [ANY] * 4,
+        (ANY, ANY, VMEM),
         [
-            pltpu.VMEM((shared_gate.shape[1], size), BF16),
-            pltpu.VMEM((shared_gate.shape[1], size), BF16),
-            pltpu.VMEM(shared_down.shape, BF16),
-            dma((3,)),
-            dma((third_span,)),
+            pltpu.VMEM((first_span,) + lat_page, BF16),
+            pltpu.VMEM((per_dev,) + rope_page, BF16),
+            dma((2,)),
+            dma((2, per_dev)),
         ],
-        vmem=12,
-        flops=6 * requests * shared_gate.size,
-        nbytes=6 * shared_gate.size,
-    )(
-        page_table, move_slot, x_own, in_hbm(shared_gate.T), in_hbm(shared_up.T),
-        in_hbm(shared_down), lat_hbm, summed[0],
-    )
+        vmem=4,
+        nbytes=2 * first_span * page_bytes,
+        aliases={5: 0, 6: 1},
+    )(page_table, move_slot, summed[0], got_first, got_rope, lat_most, rope_most)
     total, total_sent = call(
         total_kernel,
         (struct((requests, size), F32), struct((requests, size), BF16)),
-        [VMEM] * (groups + 1),
+        [SMEM] + [VMEM] * (groups + 3),
         (VMEM, VMEM),
         vmem=4,
         nbytes=8 * everyone * size,
-    )(summed[0], shared_part, *others)
-    got_third = xored(out_third, "rep", half)
+    )(move_slot, got_row[:, size + width :], summed[0], shared_part, cache_token, *others)
 
     is_moved = (jnp.arange(requests, dtype=jnp.int32) == move_slot[0])[:, None]
-    new_served = jnp.where(is_moved, got_row[:, size:].astype(F32), new)
+    new_served = jnp.where(is_moved, got_row[:, size : size + width].astype(F32), new)
     marks = new_served[:, lat_size + ROPE : lat_size + ROPE + 2].astype(jnp.int32)
     len_served = marks[:, 0] * PAGE + marks[:, 1]
     lat_new = new_served[:, :lat_size]
     rope_new = new_served[:, lat_size : lat_size + ROPE].T
-    lat_most, rope_cache = call(
-        functools.partial(token_kernel, cuts[0], cuts[1]),
+    lat_cache, rope_cache = call(
+        functools.partial(token_kernel, first_span, per_dev),
         (struct(lat_pool.shape, BF16), struct(rope_pool.shape, BF16)),
         [SMEM] * 4 + [VMEM] * 2 + [ANY, VMEM] + [ANY] * 2,
         (ANY, ANY),
@@ -892,17 +857,6 @@
         total_all = total_all + other.astype(F32)
     h_served = jnp.where(is_moved, got_row[:, :size], h_one)
     mixed = (h_served.astype(F32) + total_all).astype(BF16)
-
-    lat_cache = call(
-        functools.partial(last_kernel, cuts[1]),
-        struct(lat_pool.shape, BF16),
-        [SMEM] * 4 + [VMEM] + [ANY] * 2,
-        ANY,
-        [pltpu.VMEM((third_span * PAGE, lat_size), BF16), dma((1,)), dma((third_span,))],
-        vmem=2,
-        nbytes=2 * third_span * page_bytes,
-        aliases={6: 0},
-    )(page_table, move_slot, len_served, tp_one, lat_new, got_third, lat_most)
     return (mixed, lat_cache, rope_cache)
 
 

time: 91.2 us -> 80.1 us (0.88)
  Pallas kernels: 45.4 us -> 38.4 us
  waiting for transfers between devices: 11.2 us -> 8.51 us
  starting transfers between devices: 30.4 us -> 29.1 us
    pallas_call x5 -> x4, Pallas kernels: 29.2 us -> 21.8 us  [the longest x1 12.6 us: body(): call(functools.partial(expert_kernel, requests, 512, units), (struct((gro...]
    ppermute x24 -> x23, waiting for transfers between devices: 11.2 us -> 8.51 us  [xored(): return lax.ppermute(value, axis, pairs)]
    ppermute x24 -> x23, starting transfers between devices: 30.4 us -> 29.1 us  [xored(): return lax.ppermute(value, axis, pairs)]
  transfers between devices with their start and end apart: 24 -> 23, of which waited for: 8 -> 8; matrix products, arithmetic and copies ran while one was open for 1% -> 1% of each run, Pallas kernels for 45% -> 44%
where the time goes in v3:
time: 80.1 us; the launch traced here: 79.7 us
  Pallas kernels  38.4 us (48%)
  starting transfers between devices  29.1 us (36%)
  waiting for transfers between devices  8.51 us (11%)
  between operations  1.63 us (2%)
  local copies, waits for them, and re-layouts  1.17 us (1%)
  other arithmetic  0.88 us (1%)
    ppermute x23, starting transfers between devices, xored(): return lax.ppermute(value, axis, pairs)  29.1 us
    pallas_call x1, Pallas kernels, body(): call(functools.partial(expert_kernel, requests, 512, units), (struct((gro...  12.6 us
    ppermute x23, waiting for transfers between devices, xored(): return lax.ppermute(value, axis, pairs)  8.51 us
    pallas_call x1, Pallas kernels, body(): call(functools.partial(shared_kernel, first_span, second_span), (struct((...  5.08 us
    pallas_call x1, Pallas kernels, body(): call(functools.partial(attention_kernel, n_tp, per_dev, requests, lat_siz...  4.8 us
    pallas_call x1, Pallas kernels, body(): call(fetch_kernel, (pltpu.VMEM((pages,) + lat_page, BF16), pltpu.VMEM((pa...  4.66 us
    pallas_call x1, Pallas kernels, body(): call(token_weights_kernel, (pltpu.VMEM(w_value_up.shape, BF16), pltpu.VME...  3.05 us
    pallas_call x1, Pallas kernels, body(): call(functools.partial(query_kernel, first_span), (struct((rows, lat_size...  2.68 us
  transfers between devices with their start and end apart: 23, of which 8 were waited for; matrix products, arithmetic and copies ran while one was open for 1% of the time, Pallas kernels for 44%

profile of v3, /device:TPU:0, one launch (start us, length us, event | category | flops | bytes accessed | tf_op | source)
XLA Modules:
  0.0 79.7 jit_solution(12764646784254404982)
XLA Ops:
  1.3 0.7 copy-done.1
  2.0 2.7 %shard_map.229 = (bf16[16,576]{1,0:T(8,128)(2,1)S(1)}, bf16[4,2048]{1,0:T(4,128)(2,1)S(1)}, bf16[6,128,512]{2,1,0:T(8,128)(2,1)S(1)}, bf16[10,64,128]{2,1,0:T(8,128)(2,1)S(1)}) custom-call(s32[4,10]{1,0:T(4,128)S(1)} %copy-done.1, s32[1]{0:T(128)} %copy.40.slot_in.refs_1_.refs_0_.slot, bf16[4,2048]{1,0:T(4,128)(2,1)} %refs_5_.1, f32[1,2048]{1,0:T(1,128)} %bitcast.37, ...), custom_call_target="tpu_custom_call" | custom-call | flops 12582912 | bytes 3145728 | tf_op jit(solution)/shard_map/pallas_call | solution.py:638
  4.7 3.0 %collective-permute-start.9 = (bf16[6,128,512]{2,1,0:T(8,128)(2,1)S(1)}, bf16[6,128,512]{2,1,0:T(8,128)(2,1)S(1)}, u32[]{:S(2)}, u32[]{:S(2)}) collective-permute-start(bf16[6,128,512]{2,1,0:T(8,128)(2,1)S(1)} %get-tuple-element.53), channel_id=1, source_target_pairs={{0,16},{4,20},{8,24},{12,28},{16,0},{20,4},{24,8},{28,12},{1,17},{... | collective-permute-start | bytes 2359304 | tf_op jit(solution)/shard_map/ppermute | solution.py:31
  7.8 2.0 %collective-permute-start = (bf16[16,576]{1,0:T(8,128)(2,1)S(1)}, bf16[16,576]{1,0:T(8,128)(2,1)S(1)}, u32[]{:S(2)}, u32[]{:S(2)}) collective-permute-start(bf16[16,576]{1,0:T(8,128)(2,1)S(1)} %get-tuple-element.40._.refs_4_), channel_id=1, source_target_pairs={{0,1},{1,0},{2,3},{3,2},{4,5},{5,4},{6,7},{7,6},{8,9},{9,8},{10,11... | collective-permute-start | bytes 55304 | tf_op jit(solution)/shard_map/ppermute | solution.py:31
  9.8 2.6 %collective-permute-start.1 = (bf16[16,576]{1,0:T(8,128)(2,1)S(1)}, bf16[16,576]{1,0:T(8,128)(2,1)S(1)}, u32[]{:S(2)}, u32[]{:S(2)}) collective-permute-start(bf16[16,576]{1,0:T(8,128)(2,1)S(1)} %get-tuple-element.40._.refs_4_), channel_id=1, source_target_pairs={{0,2},{1,3},{2,0},{3,1},{4,6},{5,7},{6,4},{7,5},{8,10},{9,11},{10,... | collective-permute-start | bytes 55304 | tf_op jit(solution)/shard_map/ppermute | solution.py:31
  12.4 4.7 %shard_map.230 = (bf16[40,128,512]{2,1,0:T(8,128)(2,1)S(1)}, bf16[40,64,128]{2,1,0:T(8,128)(2,1)S(1)}, f32[8,128]{1,0:T(8,128)}) custom-call(s32[4,10]{1,0:T(4,128)S(1)} %copy-done.2, bf16[16,576]{1,0:T(8,128)(2,1)S(1)} %get-tuple-element.40._.refs_4_, bf16[40,128,512]{2,1,0:T(8,128)(2,1)} %lat.5, bf16[40,64,128]{2,1,0:T(8,128)(2,1)} %rope.3), custom_call_target="tpu_custom_call" | custom-call | flops 9437184 | bytes 10878976 | tf_op jit(solution)/shard_map/pallas_call | solution.py:669
  17.1 0.9 %collective-permute-done.2.refs_7_ = bf16[16,576]{1,0:T(8,128)(2,1)S(1)} collective-permute-done((bf16[16,576]{1,0:T(8,128)(2,1)S(1)}, bf16[16,576]{1,0:T(8,128)(2,1)S(1)}, u32[]{:S(2)}, u32[]{:S(2)}) %collective-permute-start.2) | collective-permute-done | bytes 18464 | tf_op jit(solution)/shard_map/ppermute | solution.py:31
  18.0 4.8 %shard_map.231 = (bf16[16,640]{1,0:T(8,128)(2,1)S(1)}, bf16[16,640]{1,0:T(8,128)(2,1)S(1)}, bf16[16,640]{1,0:T(8,128)(2,1)S(1)}, bf16[16,640]{1,0:T(8,128)(2,1)S...) custom-call(s32[4,10]{1,0:T(4,128)S(1)} %copy-done.2, s32[1]{0:T(128)} %copy.40.slot_in.refs_1_.refs_0_.slot, ...), custom_call_target="tpu_custom_call" | custom-call | flops 167772160 | bytes 5898240 | tf_op jit(solution)/shard_map/pallas_call | solution.py:684
  22.9 2.1 %collective-permute-start.4 = (bf16[16,640]{1,0:T(8,128)(2,1)S(1)}, bf16[16,640]{1,0:T(8,128)(2,1)S(1)}, u32[]{:S(2)}, u32[]{:S(2)}) collective-permute-start(bf16[16,640]{1,0:T(8,128)(2,1)S(1)} %get-tuple-element.45), channel_id=1, source_target_pairs={{0,2},{1,3},{2,0},{3,1},{4,6},{5,7},{6,4},{7,5},{8,10},{9,11},{10,... | collective-permute-start | bytes 61448 | tf_op jit(solution)/shard_map/ppermute | solution.py:31
  25.0 2.3 %collective-permute-start.5 = (bf16[16,640]{1,0:T(8,128)(2,1)S(1)}, bf16[16,640]{1,0:T(8,128)(2,1)S(1)}, u32[]{:S(2)}, u32[]{:S(2)}) collective-permute-start(bf16[16,640]{1,0:T(8,128)(2,1)S(1)} %get-tuple-element.46), channel_id=1, source_target_pairs={{0,3},{1,2},{2,1},{3,0},{4,7},{5,6},{6,5},{7,4},{8,11},{9,10},{10,... | collective-permute-start | bytes 61448 | tf_op jit(solution)/shard_map/ppermute | solution.py:31
  27.3 3.1 %shard_map.232 = (bf16[4,512,128]{2,1,0:T(8,128)(2,1)S(1)}, bf16[512,2048]{1,0:T(8,128)(2,1)S(1)}, f32[4,640]{1,0:T(4,128)S(1)}) custom-call(s32[4]{0:T(128)S(1)} %copy-done.6, bf16[4,2048]{1,0:T(4,128)(2,1)S(1)} %get-tuple-element.47.normed, f32[1,512]{1,0:T(1,128)S(1)} %bitcast.28, bf16[16,640]{1,0:T(8,128)(2,1)S(1)} %get-tuple-element.43._.refs_0_, ...), custom_call_target="tpu_custom_call" | custom-call | flops 9437184 | bytes 4980736 | tf_op jit(solution)/shard_map/pallas_call | solution.py:696
  30.5 0.7 shard_map.233
  31.2 3.1 %collective-permute-start.7 = (bf16[4,2048]{1,0:T(4,128)(2,1)S(1)}, bf16[4,2048]{1,0:T(4,128)(2,1)S(1)}, u32[]{:S(2)}, u32[]{:S(2)}) collective-permute-start(bf16[4,2048]{1,0:T(4,128)(2,1)S(1)} %get-tuple-element.52), channel_id=1, source_target_pairs={{0,2},{1,3},{2,0},{3,1},{4,6},{5,7},{6,4},{7,5},{8,10},{9,11},{10,... | collective-permute-start | bytes 49160 | tf_op jit(solution)/shard_map/ppermute | solution.py:31
  34.3 1.3 %collective-permute-start.8 = (bf16[4,2048]{1,0:T(4,128)(2,1)S(1)}, bf16[4,2048]{1,0:T(4,128)(2,1)S(1)}, u32[]{:S(2)}, u32[]{:S(2)}) collective-permute-start(bf16[4,2048]{1,0:T(4,128)(2,1)S(1)} %get-tuple-element.52), channel_id=1, source_target_pairs={{0,3},{1,2},{2,1},{3,0},{4,7},{5,6},{6,5},{7,4},{8,11},{9,10},{10,... | collective-permute-start | bytes 49160 | tf_op jit(solution)/shard_map/ppermute | solution.py:31
  36.1 3.8 %collective-permute-done.8.refs_4_ = bf16[4,2048]{1,0:T(4,128)(2,1)S(1)} collective-permute-done((bf16[4,2048]{1,0:T(4,128)(2,1)S(1)}, bf16[4,2048]{1,0:T(4,128)(2,1)S(1)}, u32[]{:S(2)}, u32[]{:S(2)}) %collective-permute-start.8) | collective-permute-done | bytes 16416 | tf_op jit(solution)/shard_map/ppermute | solution.py:31
  40.1 1.2 %collective-permute-done.11 = bf16[4,2176]{1,0:T(4,128)(2,1)S(1)} collective-permute-done((bf16[4,2176]{1,0:T(4,128)(2,1)S(1)}, bf16[4,2176]{1,0:T(4,128)(2,1)S(1)}, u32[]{:S(2)}, u32[]{:S(2)}) %collective-permute-start.11) | collective-permute-done | bytes 17440 | tf_op jit(solution)/shard_map/ppermute | solution.py:31
  41.7 1.5 %collective-permute-start.13 = (bf16[8,2176]{1,0:T(8,128)(2,1)S(1)}, bf16[8,2176]{1,0:T(8,128)(2,1)S(1)}, u32[]{:S(2)}, u32[]{:S(2)}) collective-permute-start(bf16[8,2176]{1,0:T(8,128)(2,1)S(1)} %pad_maximum_fusion._.refs_0_), channel_id=1, source_target_pairs={{0,16},{4,20},{8,24},{12,28},{16,0},{20,4},{24,8},{28,12},{1,17},{... | collective-permute-start | bytes 104456 | tf_op jit(solution)/shard_map/ppermute | solution.py:31
  43.3 1.6 %collective-permute-start.14 = (bf16[8,2176]{1,0:T(8,128)(2,1)S(1)}, bf16[8,2176]{1,0:T(8,128)(2,1)S(1)}, u32[]{:S(2)}, u32[]{:S(2)}) collective-permute-start(bf16[8,2176]{1,0:T(8,128)(2,1)S(1)} %pad_maximum_fusion._.refs_0_), channel_id=1, source_target_pairs={{0,24},{4,28},{8,16},{12,20},{16,8},{20,12},{24,0},{28,4},{1,25},{... | collective-permute-start | bytes 104456 | tf_op jit(solution)/shard_map/ppermute | solution.py:31
  45.0 5.1 %shard_map.235 = (f32[4,2048]{1,0:T(4,128)S(1)}, bf16[528,512]{1,0:T(8,128)(2,1)S(1)}) custom-call(s32[4,10]{1,0:T(4,128)S(1)} %copy-done.2, s32[1]{0:T(128)} %copy.40.slot_in.refs_1_.refs_0_.slot, bf16[4,2176]{1,0:T(4,128)(2,1)S(1)} %get-tuple-element.55.rows, bf16[4,2048]{1,0:T(4,128)(2,1)S(1)} %get-tuple-element.56.h_one, ...), custom_call_target="tpu_custom_call" | custom-call | flops 34603008 | bytes 8650752 | tf_op jit(solution)/shard_map/pallas_call | solution.py:740
  50.1 0.6 shard_map.236
  50.7 0.9 %collective-permute-start.15 = (bf16[528,512]{1,0:T(8,128)(2,1)S(1)}, bf16[528,512]{1,0:T(8,128)(2,1)S(1)}, u32[]{:S(2)}, u32[]{:S(2)}) collective-permute-start(bf16[528,512]{1,0:T(8,128)(2,1)S(1)} %get-tuple-element.58), channel_id=1, source_target_pairs={{0,16},{4,20},{8,24},{12,28},{16,0},{20,4},{24,8},{28,12},{1,17},{... | collective-permute-start | bytes 1622024 | tf_op jit(solution)/shard_map/ppermute | solution.py:31
  51.7 12.6 %shard_map.237 = (f32[16,2048]{1,0:T(8,128)S(1)}, bf16[16,2048]{1,0:T(8,128)(2,1)S(1)}) custom-call(s32[1]{0:T(128)} %bitcast.1.rank, bf16[32,2048]{1,0:T(8,128)(2,1)S(1)} %get-tuple-element.59.x, f32[32,64]{1,0:T(8,128)S(1)} %get-tuple-element.60.coef, bf16[2816,2048]{1,0:T(8,128)(2,1)} %bitcast.29, bf16[2816,2048]{1,0:T(8,128)(2,1)} %bitcast.30, ...), custom_call_target="tpu_custom_call" | custom-call | flops 1107296256 | bytes 34603008 | tf_op jit(solution)/shard_map/pallas_call | solution.py:779
  64.5 1.1 %collective-permute-done.16.got = bf16[16,2048]{1,0:T(8,128)(2,1)S(1)} collective-permute-done((bf16[16,2048]{1,0:T(8,128)(2,1)S(1)}, bf16[16,2048]{1,0:T(8,128)(2,1)S(1)}, u32[]{:S(2)}, u32[]{:S(2)}) %collective-permute-start.16) | collective-permute-done | bytes 65568 | tf_op jit(solution)/shard_map/ppermute | solution.py:31
  65.7 1.1 %collective-permute-start.17 = (bf16[4,2048]{1,0:T(4,128)(2,1)S(1)}, bf16[4,2048]{1,0:T(4,128)(2,1)S(1)}, u32[]{:S(2)}, u32[]{:S(2)}) collective-permute-start(bf16[4,2048]{1,0:T(4,128)(2,1)S(1)} %get-tuple-element.68), channel_id=1, source_target_pairs={{0,8},{4,12},{8,0},{12,4},{16,24},{20,28},{24,16},{28,20},{1,9},{5... | collective-permute-start | bytes 49160 | tf_op jit(solution)/shard_map/ppermute | solution.py:31
  66.8 0.5 collective-permute-start.18
  67.3 1.9 %collective-permute-start.19 = (bf16[4,2048]{1,0:T(4,128)(2,1)S(1)}, bf16[4,2048]{1,0:T(4,128)(2,1)S(1)}, u32[]{:S(2)}, u32[]{:S(2)}) collective-permute-start(bf16[4,2048]{1,0:T(4,128)(2,1)S(1)} %get-tuple-element.70), channel_id=1, source_target_pairs={{0,24},{4,28},{8,16},{12,20},{16,8},{20,12},{24,0},{28,4},{1,25},{... | collective-permute-start | bytes 49160 | tf_op jit(solution)/shard_map/ppermute | solution.py:31
  69.4 1.9 %shard_map.239 = (bf16[40,128,512]{2,1,0:T(8,128)(2,1)}, bf16[40,64,128]{2,1,0:T(8,128)(2,1)}, f32[8,128]{1,0:T(8,128)S(1)}) custom-call(s32[4,10]{1,0:T(4,128)S(1)} %copy-done.2, s32[1]{0:T(128)} %copy.40.slot_in.refs_1_.refs_0_.slot, f32[4,2048]{1,0:T(4,128)S(1)} %get-tuple-element.63._.own, ...), custom_call_target="tpu_custom_call", output_to_operand_aliasing={{0}: (5, {}), {1}: (6, {})} | custom-call | bytes 1769472 | tf_op jit(solution)/shard_map/pallas_call | solution.py:804
  71.4 0.5 collective-permute-done.19.refs_2_
  71.9 2.5 %collective-permute-start.22 = (bf16[4,2048]{1,0:T(4,128)(2,1)S(1)}, bf16[4,2048]{1,0:T(4,128)(2,1)S(1)}, u32[]{:S(2)}, u32[]{:S(2)}) collective-permute-start(bf16[4,2048]{1,0:T(4,128)(2,1)S(1)} %get-tuple-element.72), channel_id=1, source_target_pairs={{0,3},{1,2},{2,1},{3,0},{4,7},{5,6},{6,5},{7,4},{8,11},{9,10},{10,... | collective-permute-start | bytes 49160 | tf_op jit(solution)/shard_map/ppermute | solution.py:31
  74.4 2.0 %collective-permute-start.20 = (bf16[4,2048]{1,0:T(4,128)(2,1)S(1)}, bf16[4,2048]{1,0:T(4,128)(2,1)S(1)}, u32[]{:S(2)}, u32[]{:S(2)}) collective-permute-start(bf16[4,2048]{1,0:T(4,128)(2,1)S(1)} %get-tuple-element.72), channel_id=1, source_target_pairs={{0,1},{1,0},{2,3},{3,2},{4,5},{5,4},{6,7},{7,6},{8,9},{9,8},{10,11... | collective-permute-start | bytes 49160 | tf_op jit(solution)/shard_map/ppermute | solution.py:31
  76.5 2.2 %shard_map.241 = (bf16[40,128,512]{2,1,0:T(8,128)(2,1)}, bf16[40,64,128]{2,1,0:T(8,128)(2,1)}) custom-call(s32[4,10]{1,0:T(4,128)S(1)} %copy-done.2, s32[1]{0:T(128)} %copy.40.slot_in.refs_1_.refs_0_.slot, s32[4]{0:T(128)S(1)} %add_bitcast_fusion.lengths, s32[1]{0:T(128)} %bitcast.3.refs_3_.rank, ...), custom_call_target="tpu_custom_call", output_to_operand_aliasing={{0}: (8, {}), {1}: (9, {})} | custom-call | bytes 1179648 | tf_op jit(solution)/shard_map/pallas_call | solution.py:834
  79.0 0.7 add_convert_fusion
  (58 shorter events, 2.5 us)
Async XLA Ops:
  0.6 11.8 %copy-start.2 = (s32[4,10]{1,0:T(4,128)S(1)}, s32[4,10]{1,0:T(4,128)}, u32[]{:S(2)}) copy-start(s32[4,10]{1,0:T(4,128)} %table.7) | copy-start | bytes 484
  1.3 0.7 copy-start.1
  4.7 13.3 %copy-start.6 = (s32[4]{0:T(128)S(1)}, s32[4]{0:T(128)}, u32[]{:S(2)}) copy-start(s32[4]{0:T(128)} %lengths.1) | copy-start | bytes 52
  4.7 35.2 %collective-permute-start.9 = (bf16[6,128,512]{2,1,0:T(8,128)(2,1)S(1)}, bf16[6,128,512]{2,1,0:T(8,128)(2,1)S(1)}, u32[]{:S(2)}, u32[]{:S(2)}) collective-permute-start(bf16[6,128,512]{2,1,0:T(8,128)(2,1)S(1)} %get-tuple-element.53), channel_id=1, source_target_pairs={{0,16},{4,20},{8,24},{12,28},{16,0},{20,4},{24,8},{28,12},{1,17},{... | collective-permute-start | bytes 2359304 | tf_op jit(solution)/shard_map/ppermute | solution.py:31
  7.7 32.2 %collective-permute-start.10 = (bf16[10,64,128]{2,1,0:T(8,128)(2,1)S(1)}, bf16[10,64,128]{2,1,0:T(8,128)(2,1)S(1)}, u32[]{:S(2)}, u32[]{:S(2)}) collective-permute-start(bf16[10,64,128]{2,1,0:T(8,128)(2,1)S(1)} %get-tuple-element.54), channel_id=1, source_target_pairs={{0,16},{4,20},{8,24},{12,28},{16,0},{20,4},{24,8},{28,12},{1,17},{... | collective-permute-start | bytes 491528 | tf_op jit(solution)/shard_map/ppermute | solution.py:31
  7.8 9.3 %collective-permute-start = (bf16[16,576]{1,0:T(8,128)(2,1)S(1)}, bf16[16,576]{1,0:T(8,128)(2,1)S(1)}, u32[]{:S(2)}, u32[]{:S(2)}) collective-permute-start(bf16[16,576]{1,0:T(8,128)(2,1)S(1)} %get-tuple-element.40._.refs_4_), channel_id=1, source_target_pairs={{0,1},{1,0},{2,3},{3,2},{4,5},{5,4},{6,7},{7,6},{8,9},{9,8},{10,11... | collective-permute-start | bytes 55304 | tf_op jit(solution)/shard_map/ppermute | solution.py:31
  9.8 7.3 %collective-permute-start.1 = (bf16[16,576]{1,0:T(8,128)(2,1)S(1)}, bf16[16,576]{1,0:T(8,128)(2,1)S(1)}, u32[]{:S(2)}, u32[]{:S(2)}) collective-permute-start(bf16[16,576]{1,0:T(8,128)(2,1)S(1)} %get-tuple-element.40._.refs_4_), channel_id=1, source_target_pairs={{0,2},{1,3},{2,0},{3,1},{4,6},{5,7},{6,4},{7,5},{8,10},{9,11},{10,... | collective-permute-start | bytes 55304 | tf_op jit(solution)/shard_map/ppermute | solution.py:31
  12.4 5.6 %collective-permute-start.2 = (bf16[16,576]{1,0:T(8,128)(2,1)S(1)}, bf16[16,576]{1,0:T(8,128)(2,1)S(1)}, u32[]{:S(2)}, u32[]{:S(2)}) collective-permute-start(bf16[16,576]{1,0:T(8,128)(2,1)S(1)} %get-tuple-element.40._.refs_4_), channel_id=1, source_target_pairs={{0,3},{1,2},{2,1},{3,0},{4,7},{5,6},{6,5},{7,4},{8,11},{9,10},{10,... | collective-permute-start | bytes 55304 | tf_op jit(solution)/shard_map/ppermute | solution.py:31
  12.4 14.9 %copy-start.5 = (f32[512]{0:T(512)S(1)}, f32[512]{0:T(512)}, u32[]{:S(2)}) copy-start(f32[512]{0:T(512)} %param.31) | copy-start | bytes 6148
  22.8 17.1 %copy-start.3 = (bf16[4,2048]{1,0:T(4,128)(2,1)S(1)}, bf16[4,2048]{1,0:T(4,128)(2,1)}, u32[]{:S(2)}) copy-start(bf16[4,2048]{1,0:T(4,128)(2,1)} %refs_5_.1) | copy-start | bytes 49156
  22.8 17.1 %copy-start.4 = (f32[2048]{0:T(1024)S(1)}, f32[2048]{0:T(1024)}, u32[]{:S(2)}) copy-start(f32[2048]{0:T(1024)} %param.35) | copy-start | bytes 24580
  22.8 22.1 %copy-start.7 = (s32[32,6]{0,1:T(8,128)S(1)}, s32[32,6]{0,1:T(8,128)}, u32[]{:S(2)}) copy-start(s32[32,6]{0,1:T(8,128)} %param.37) | copy-start | bytes 2308
  22.8 7.5 %collective-permute-start.3 = (bf16[16,640]{1,0:T(8,128)(2,1)S(1)}, bf16[16,640]{1,0:T(8,128)(2,1)S(1)}, u32[]{:S(2)}, u32[]{:S(2)}) collective-permute-start(bf16[16,640]{1,0:T(8,128)(2,1)S(1)} %get-tuple-element.44), channel_id=1, source_target_pairs={{0,1},{1,0},{2,3},{3,2},{4,5},{5,4},{6,7},{7,6},{8,9},{9,8},{10,11... | collective-permute-start | bytes 61448 | tf_op jit(solution)/shard_map/ppermute | solution.py:31
  22.9 7.4 %collective-permute-start.4 = (bf16[16,640]{1,0:T(8,128)(2,1)S(1)}, bf16[16,640]{1,0:T(8,128)(2,1)S(1)}, u32[]{:S(2)}, u32[]{:S(2)}) collective-permute-start(bf16[16,640]{1,0:T(8,128)(2,1)S(1)} %get-tuple-element.45), channel_id=1, source_target_pairs={{0,2},{1,3},{2,0},{3,1},{4,6},{5,7},{6,4},{7,5},{8,10},{9,11},{10,... | collective-permute-start | bytes 61448 | tf_op jit(solution)/shard_map/ppermute | solution.py:31
  25.0 5.6 %collective-permute-start.5 = (bf16[16,640]{1,0:T(8,128)(2,1)S(1)}, bf16[16,640]{1,0:T(8,128)(2,1)S(1)}, u32[]{:S(2)}, u32[]{:S(2)}) collective-permute-start(bf16[16,640]{1,0:T(8,128)(2,1)S(1)} %get-tuple-element.46), channel_id=1, source_target_pairs={{0,3},{1,2},{2,1},{3,0},{4,7},{5,6},{6,5},{7,4},{8,11},{9,10},{10,... | collective-permute-start | bytes 61448 | tf_op jit(solution)/shard_map/ppermute | solution.py:31
  31.2 4.4 %collective-permute-start.6 = (bf16[4,2048]{1,0:T(4,128)(2,1)S(1)}, bf16[4,2048]{1,0:T(4,128)(2,1)S(1)}, u32[]{:S(2)}, u32[]{:S(2)}) collective-permute-start(bf16[4,2048]{1,0:T(4,128)(2,1)S(1)} %get-tuple-element.52), channel_id=1, source_target_pairs={{0,1},{1,0},{2,3},{3,2},{4,5},{5,4},{6,7},{7,6},{8,9},{9,8},{10,11... | collective-permute-start | bytes 49160 | tf_op jit(solution)/shard_map/ppermute | solution.py:31
  31.2 4.8 %collective-permute-start.7 = (bf16[4,2048]{1,0:T(4,128)(2,1)S(1)}, bf16[4,2048]{1,0:T(4,128)(2,1)S(1)}, u32[]{:S(2)}, u32[]{:S(2)}) collective-permute-start(bf16[4,2048]{1,0:T(4,128)(2,1)S(1)} %get-tuple-element.52), channel_id=1, source_target_pairs={{0,2},{1,3},{2,0},{3,1},{4,6},{5,7},{6,4},{7,5},{8,10},{9,11},{10,... | collective-permute-start | bytes 49160 | tf_op jit(solution)/shard_map/ppermute | solution.py:31
  34.3 5.5 %collective-permute-start.8 = (bf16[4,2048]{1,0:T(4,128)(2,1)S(1)}, bf16[4,2048]{1,0:T(4,128)(2,1)S(1)}, u32[]{:S(2)}, u32[]{:S(2)}) collective-permute-start(bf16[4,2048]{1,0:T(4,128)(2,1)S(1)} %get-tuple-element.52), channel_id=1, source_target_pairs={{0,3},{1,2},{2,1},{3,0},{4,7},{5,6},{6,5},{7,4},{8,11},{9,10},{10,... | collective-permute-start | bytes 49160 | tf_op jit(solution)/shard_map/ppermute | solution.py:31
  40.0 1.3 %collective-permute-start.11 = (bf16[4,2176]{1,0:T(4,128)(2,1)S(1)}, bf16[4,2176]{1,0:T(4,128)(2,1)S(1)}, u32[]{:S(2)}, u32[]{:S(2)}) collective-permute-start(bf16[4,2176]{1,0:T(4,128)(2,1)S(1)} %get-tuple-element.55.rows), channel_id=1, source_target_pairs={{0,4},{4,0},{8,12},{12,8},{16,20},{20,16},{24,28},{28,24},{1,5},{5... | collective-permute-start | bytes 52232 | tf_op jit(solution)/shard_map/ppermute | solution.py:31
  41.3 8.7 %collective-permute-start.12 = (bf16[8,2176]{1,0:T(8,128)(2,1)S(1)}, bf16[8,2176]{1,0:T(8,128)(2,1)S(1)}, u32[]{:S(2)}, u32[]{:S(2)}) collective-permute-start(bf16[8,2176]{1,0:T(8,128)(2,1)S(1)} %pad_maximum_fusion._.refs_0_), channel_id=1, source_target_pairs={{0,8},{4,12},{8,0},{12,4},{16,24},{20,28},{24,16},{28,20},{1,9},{5... | collective-permute-start | bytes 104456 | tf_op jit(solution)/shard_map/ppermute | solution.py:31
  41.7 8.3 %collective-permute-start.13 = (bf16[8,2176]{1,0:T(8,128)(2,1)S(1)}, bf16[8,2176]{1,0:T(8,128)(2,1)S(1)}, u32[]{:S(2)}, u32[]{:S(2)}) collective-permute-start(bf16[8,2176]{1,0:T(8,128)(2,1)S(1)} %pad_maximum_fusion._.refs_0_), channel_id=1, source_target_pairs={{0,16},{4,20},{8,24},{12,28},{16,0},{20,4},{24,8},{28,12},{1,17},{... | collective-permute-start | bytes 104456 | tf_op jit(solution)/shard_map/ppermute | solution.py:31
  43.3 6.8 %collective-permute-start.14 = (bf16[8,2176]{1,0:T(8,128)(2,1)S(1)}, bf16[8,2176]{1,0:T(8,128)(2,1)S(1)}, u32[]{:S(2)}, u32[]{:S(2)}) collective-permute-start(bf16[8,2176]{1,0:T(8,128)(2,1)S(1)} %pad_maximum_fusion._.refs_0_), channel_id=1, source_target_pairs={{0,24},{4,28},{8,16},{12,20},{16,8},{20,12},{24,0},{28,4},{1,25},{... | collective-permute-start | bytes 104456 | tf_op jit(solution)/shard_map/ppermute | solution.py:31
  45.0 5.1 %copy-start = (bf16[2048,64]{0,1:T(8,128)(2,1)S(1)}, bf16[2048,64]{0,1:T(8,128)(2,1)}, u32[]{:S(2)}) copy-start(bf16[2048,64]{0,1:T(8,128)(2,1)} %param.36) | copy-start | bytes 786436
  50.7 13.7 %collective-permute-start.15 = (bf16[528,512]{1,0:T(8,128)(2,1)S(1)}, bf16[528,512]{1,0:T(8,128)(2,1)S(1)}, u32[]{:S(2)}, u32[]{:S(2)}) collective-permute-start(bf16[528,512]{1,0:T(8,128)(2,1)S(1)} %get-tuple-element.58), channel_id=1, source_target_pairs={{0,16},{4,20},{8,24},{12,28},{16,0},{20,4},{24,8},{28,12},{1,17},{... | collective-permute-start | bytes 1622024 | tf_op jit(solution)/shard_map/ppermute | solution.py:31
  64.3 1.3 %collective-permute-start.16 = (bf16[16,2048]{1,0:T(8,128)(2,1)S(1)}, bf16[16,2048]{1,0:T(8,128)(2,1)S(1)}, u32[]{:S(2)}, u32[]{:S(2)}) collective-permute-start(bf16[16,2048]{1,0:T(8,128)(2,1)S(1)} %get-tuple-element.62), channel_id=1, source_target_pairs={{0,4},{4,0},{8,12},{12,8},{16,20},{20,16},{24,28},{28,24},{1,5},{5... | collective-permute-start | bytes 196616 | tf_op jit(solution)/shard_map/ppermute | solution.py:31
  65.7 5.7 %collective-permute-start.17 = (bf16[4,2048]{1,0:T(4,128)(2,1)S(1)}, bf16[4,2048]{1,0:T(4,128)(2,1)S(1)}, u32[]{:S(2)}, u32[]{:S(2)}) collective-permute-start(bf16[4,2048]{1,0:T(4,128)(2,1)S(1)} %get-tuple-element.68), channel_id=1, source_target_pairs={{0,8},{4,12},{8,0},{12,4},{16,24},{20,28},{24,16},{28,20},{1,9},{5... | collective-permute-start | bytes 49160 | tf_op jit(solution)/shard_map/ppermute | solution.py:31
  66.8 4.6 %collective-permute-start.18 = (bf16[4,2048]{1,0:T(4,128)(2,1)S(1)}, bf16[4,2048]{1,0:T(4,128)(2,1)S(1)}, u32[]{:S(2)}, u32[]{:S(2)}) collective-permute-start(bf16[4,2048]{1,0:T(4,128)(2,1)S(1)} %get-tuple-element.69), channel_id=1, source_target_pairs={{0,16},{4,20},{8,24},{12,28},{16,0},{20,4},{24,8},{28,12},{1,17},{... | collective-permute-start | bytes 49160 | tf_op jit(solution)/shard_map/ppermute | solution.py:31
  67.3 4.6 %collective-permute-start.19 = (bf16[4,2048]{1,0:T(4,128)(2,1)S(1)}, bf16[4,2048]{1,0:T(4,128)(2,1)S(1)}, u32[]{:S(2)}, u32[]{:S(2)}) collective-permute-start(bf16[4,2048]{1,0:T(4,128)(2,1)S(1)} %get-tuple-element.70), channel_id=1, source_target_pairs={{0,24},{4,28},{8,16},{12,20},{16,8},{20,12},{24,0},{28,4},{1,25},{... | collective-permute-start | bytes 49160 | tf_op jit(solution)/shard_map/ppermute | solution.py:31
  71.9 6.8 %collective-permute-start.22 = (bf16[4,2048]{1,0:T(4,128)(2,1)S(1)}, bf16[4,2048]{1,0:T(4,128)(2,1)S(1)}, u32[]{:S(2)}, u32[]{:S(2)}) collective-permute-start(bf16[4,2048]{1,0:T(4,128)(2,1)S(1)} %get-tuple-element.72), channel_id=1, source_target_pairs={{0,3},{1,2},{2,1},{3,0},{4,7},{5,6},{6,5},{7,4},{8,11},{9,10},{10,... | collective-permute-start | bytes 49160 | tf_op jit(solution)/shard_map/ppermute | solution.py:31
  74.4 4.6 %collective-permute-start.21 = (bf16[4,2048]{1,0:T(4,128)(2,1)S(1)}, bf16[4,2048]{1,0:T(4,128)(2,1)S(1)}, u32[]{:S(2)}, u32[]{:S(2)}) collective-permute-start(bf16[4,2048]{1,0:T(4,128)(2,1)S(1)} %get-tuple-element.72), channel_id=1, source_target_pairs={{0,2},{1,3},{2,0},{3,1},{4,6},{5,7},{6,4},{7,5},{8,10},{9,11},{10,... | collective-permute-start | bytes 49160 | tf_op jit(solution)/shard_map/ppermute | solution.py:31
  74.4 4.6 %collective-permute-start.20 = (bf16[4,2048]{1,0:T(4,128)(2,1)S(1)}, bf16[4,2048]{1,0:T(4,128)(2,1)S(1)}, u32[]{:S(2)}, u32[]{:S(2)}) collective-permute-start(bf16[4,2048]{1,0:T(4,128)(2,1)S(1)} %get-tuple-element.72), channel_id=1, source_target_pairs={{0,1},{1,0},{2,3},{3,2},{4,5},{5,4},{6,7},{7,6},{8,9},{9,8},{10,11... | collective-permute-start | bytes 49160 | tf_op jit(solution)/shard_map/ppermute | solution.py:31

commit v4 on v3

--- a/solution.py
+++ b/solution.py
@@ -117,16 +117,14 @@
         copy.wait()
 
 
-def fetch_kernel(table, _, lat, rope, lat_v, rope_v, token, sems):
+def fetch_kernel(parts, _, lat, rope, lat_v, rope_v, token, sems):
     token[...] = jnp.zeros_like(token)
-    requests, per_dev = table.shape
+    step = lat.shape[0] // parts
     copies = []
-    for r in range(requests):
-        for j in range(per_dev):
-            n = r * per_dev + j
-            page = table[r, j]
-            copies.append(pltpu.make_async_copy(lat.at[page], lat_v.at[n], sems.at[0, n]))
-            copies.append(pltpu.make_async_copy(rope.at[page], rope_v.at[n], sems.at[1, n]))
+    for i in range(parts):
+        piece = pl.ds(i * step, step)
+        copies.append(pltpu.make_async_copy(lat.at[piece], lat_v.at[piece], sems.at[i]))
+    copies.append(pltpu.make_async_copy(rope, rope_v, sems.at[parts]))
     for copy in copies:
         copy.start()
     for copy in copies:
@@ -161,27 +159,18 @@
 
 
 def attention_kernel(blocks, per_dev, requests, lat_size, *refs):
-    table, slot, lengths, rank = refs[:4]
-    queries = refs[4 : 4 + blocks]
-    lat, rope = refs[4 + blocks : 6 + blocks]
-    outs = refs[6 + blocks : 6 + 2 * blocks]
-    lat_out, rope_out, q_all, result, sems = refs[6 + 2 * blocks :]
-
-    def own_pages(r):
-        copies = []
-        for j in range(per_dev):
-            n = r * per_dev + j
-            page = table[r, j]
-            copies.append(pltpu.make_async_copy(lat.at[n], lat_out.at[page], sems.at[0, n]))
-            copies.append(pltpu.make_async_copy(rope.at[n], rope_out.at[page], sems.at[1, n]))
-        return copies
-
+    table, lengths, rank = refs[:3]
+    queries = refs[3 : 3 + blocks]
+    lat, rope = refs[3 + blocks : 5 + blocks]
+    outs = refs[5 + blocks : 5 + 2 * blocks]
+    lat_out, rope_out, q_all, result, sems = refs[5 + 2 * blocks :]
+    copies = []
     for r in range(requests):
-        @pl.when(slot[0] != r)
-        def _():
-            for copy in own_pages(r):
-                copy.start()
-
+        piece = pl.ds(r * per_dev, per_dev)
+        copies.append(pltpu.make_async_copy(lat.at[piece], lat_out.at[piece], sems.at[r]))
+    copies.append(pltpu.make_async_copy(rope, rope_out, sems.at[requests]))
+    for copy in copies:
+        copy.start()
     rows = queries[0].shape[0]
     heads = blocks * rows // requests
     scale = (NOPE + ROPE) ** (-0.5)
@@ -199,12 +188,11 @@
         length = lengths[r]
         q_lat = jnp.concatenate([q_all[i, mine, :] for i in range(tiles)], axis=1).astype(BF16)
         q_pos = q_all[tiles, mine, :][:, :ROPE].astype(BF16)
-        start = r * per_dev
-        latents = lat[start : start + count].reshape(count * PAGE, lat_size)
+        latents = jnp.concatenate([lat[table[r, j]] for j in range(count)], axis=0)
         scores = lax.dot_general(q_lat, latents, NT, preferred_element_type=F32)
         scores += jnp.concatenate(
             [
-                jnp.dot(q_pos, rope[start + j], preferred_element_type=F32)
+                jnp.dot(q_pos, rope[table[r, j]], preferred_element_type=F32)
                 for j in range(count)
             ],
             axis=1,
@@ -256,11 +244,8 @@
         share = 1.0 / safe
         pieces = [result[i, block, :] * share for i in range(tiles)] + [split]
         outs[k][...] = jnp.concatenate(pieces, axis=1).astype(BF16)
-    for r in range(requests):
-        @pl.when(slot[0] != r)
-        def _():
-            for copy in own_pages(r):
-                copy.wait()
+    for copy in copies:
+        copy.wait()
 
 
 def finish_kernel(blocks, requests, lat_size, *refs):
@@ -667,31 +652,31 @@
     q_blocks = [q_own] + [xored(q_own, "tp", k) for k in range(1, n_tp)]
 
     lat_v, rope_v, _ = call(
-        fetch_kernel,
+        functools.partial(fetch_kernel, requests),
         (
             pltpu.VMEM((pages,) + lat_page, BF16),
             pltpu.VMEM((pages,) + rope_page, BF16),
             struct((8, LANES), F32),
         ),
-        [SMEM, VMEM, ANY, ANY],
+        [VMEM, ANY, ANY],
         (VMEM,) * 3,
-        [dma((2, pages))],
+        [dma((requests + 1,))],
         vmem=6,
         flops=2 * requests * w_latent.size,
         nbytes=pages * page_bytes + 2 * (w_latent.size + w_output.size + w_value_up.size),
-    )(page_table, q_own, lat_hbm, rope_hbm)
+    )(q_own, lat_hbm, rope_hbm)
 
     *partial, lat_most, rope_most = call(
         functools.partial(attention_kernel, n_tp, per_dev, requests, lat_size),
         tuple(struct((rows, width), BF16) for _ in range(n_tp))
         + (struct(lat_pool.shape, BF16), struct(rope_pool.shape, BF16)),
-        [SMEM] * 4 + [VMEM] * (n_tp + 2),
+        [SMEM] * 3 + [VMEM] * (n_tp + 2),
         (VMEM,) * n_tp + (ANY, ANY),
-        [pltpu.VMEM((width // LANES, n_tp * rows, LANES), F32)] * 2 + [dma((2, pages))],
+        [pltpu.VMEM((width // LANES, n_tp * rows, LANES), F32)] * 2 + [dma((requests + 1,))],
         vmem=6,
         flops=4 * n_tp * rows * per_dev * PAGE * lat_size,
         nbytes=pages * page_bytes,
-    )(page_table, move_slot, lengths, tp_one, *q_blocks, lat_v, rope_v)
+    )(page_table, lengths, tp_one, *q_blocks, lat_v, rope_v)
     parts = [partial[0]] + [xored(partial[k], "tp", k) for k in range(1, n_tp)]
     value_v, out_v, new = call(
         token_weights_kernel,

time: 80.1 us -> 79.6 us (level)
  Pallas kernels: 38.4 us -> 35.6 us
  waiting for transfers between devices: 8.51 us -> 10.5 us
    ppermute x23, waiting for transfers between devices: 8.51 us -> 10.5 us  [xored(): return lax.ppermute(value, axis, pairs)]
    pallas_call x1, Pallas kernels: 4.8 us -> 3.17 us  [body(): call(functools.partial(attention_kernel, n_tp, per_dev, requests, lat_siz...]
    pallas_call x1, Pallas kernels: 4.66 us -> 3.31 us  [body(): call(functools.partial(fetch_kernel, requests), (pltpu.VMEM((pages,) + la...]
  transfers between devices with their start and end apart: 23 -> 23, of which waited for: 8 -> 7; matrix products, arithmetic and copies ran while one was open for 1% -> 1% of each run, Pallas kernels for 44% -> 40%
where the time goes in v4:
time: 79.6 us; the launch traced here: 79.7 us
  Pallas kernels  35.6 us (45%)
  starting transfers between devices  29.8 us (37%)
  waiting for transfers between devices  10.5 us (13%)
  between operations  1.63 us (2%)
  local copies, waits for them, and re-layouts  1.17 us (1%)
  other arithmetic  0.88 us (1%)
    ppermute x23, starting transfers between devices, xored(): return lax.ppermute(value, axis, pairs)  29.8 us
    pallas_call x1, Pallas kernels, body(): call(functools.partial(expert_kernel, requests, 512, units), (struct((gro...  12.6 us
    ppermute x23, waiting for transfers between devices, xored(): return lax.ppermute(value, axis, pairs)  10.5 us
    pallas_call x1, Pallas kernels, body(): call(functools.partial(shared_kernel, first_span, second_span), (struct((...  5.08 us
    pallas_call x1, Pallas kernels, body(): call(functools.partial(fetch_kernel, requests), (pltpu.VMEM((pages,) + la...  3.31 us
    pallas_call x1, Pallas kernels, body(): call(functools.partial(attention_kernel, n_tp, per_dev, requests, lat_siz...  3.17 us
    pallas_call x1, Pallas kernels, body(): call(token_weights_kernel, (pltpu.VMEM(w_value_up.shape, BF16), pltpu.VME...  3.05 us
    pallas_call x1, Pallas kernels, body(): call(functools.partial(query_kernel, first_span), (struct((rows, lat_size...  2.68 us
  transfers between devices with their start and end apart: 23, of which 7 were waited for; matrix products, arithmetic and copies ran while one was open for 1% of the time, Pallas kernels for 40%

profile of v4, /device:TPU:0, one launch (start us, length us, event | category | flops | bytes accessed | tf_op | source)
XLA Modules:
  0.0 79.7 jit_solution(14766667655947301123)
XLA Ops:
  1.3 0.7 copy-done.2
  2.0 2.7 %shard_map.229 = (bf16[16,576]{1,0:T(8,128)(2,1)S(1)}, bf16[4,2048]{1,0:T(4,128)(2,1)S(1)}, bf16[6,128,512]{2,1,0:T(8,128)(2,1)S(1)}, bf16[10,64,128]{2,1,0:T(8,128)(2,1)S(1)}) custom-call(s32[4,10]{1,0:T(4,128)S(1)} %copy-done.2, s32[1]{0:T(128)} %copy.40.slot_in.refs_0_.slot, bf16[4,2048]{1,0:T(4,128)(2,1)} %refs_5_.1, f32[1,2048]{1,0:T(1,128)} %bitcast.37, ...), custom_call_target="tpu_custom_call" | custom-call | flops 12582912 | bytes 3145728 | tf_op jit(solution)/shard_map/pallas_call | solution.py:623
  4.7 3.0 %collective-permute-start.9 = (bf16[6,128,512]{2,1,0:T(8,128)(2,1)S(1)}, bf16[6,128,512]{2,1,0:T(8,128)(2,1)S(1)}, u32[]{:S(2)}, u32[]{:S(2)}) collective-permute-start(bf16[6,128,512]{2,1,0:T(8,128)(2,1)S(1)} %get-tuple-element.53), channel_id=1, source_target_pairs={{0,16},{4,20},{8,24},{12,28},{16,0},{20,4},{24,8},{28,12},{1,17},{... | collective-permute-start | bytes 2359304 | tf_op jit(solution)/shard_map/ppermute | solution.py:31
  7.8 2.0 %collective-permute-start = (bf16[16,576]{1,0:T(8,128)(2,1)S(1)}, bf16[16,576]{1,0:T(8,128)(2,1)S(1)}, u32[]{:S(2)}, u32[]{:S(2)}) collective-permute-start(bf16[16,576]{1,0:T(8,128)(2,1)S(1)} %get-tuple-element.40._.refs_3_.refs_4_), channel_id=1, source_target_pairs={{0,1},{1,0},{2,3},{3,2},{4,5},{5,4},{6,7},{7,6},{8,9},{9,8},{10,11... | collective-permute-start | bytes 55304 | tf_op jit(solution)/shard_map/ppermute | solution.py:31
  9.8 2.6 %collective-permute-start.1 = (bf16[16,576]{1,0:T(8,128)(2,1)S(1)}, bf16[16,576]{1,0:T(8,128)(2,1)S(1)}, u32[]{:S(2)}, u32[]{:S(2)}) collective-permute-start(bf16[16,576]{1,0:T(8,128)(2,1)S(1)} %get-tuple-element.40._.refs_3_.refs_4_), channel_id=1, source_target_pairs={{0,2},{1,3},{2,0},{3,1},{4,6},{5,7},{6,4},{7,5},{8,10},{9,11},{10,... | collective-permute-start | bytes 55304 | tf_op jit(solution)/shard_map/ppermute | solution.py:31
  12.4 3.3 %shard_map.230 = (bf16[40,128,512]{2,1,0:T(8,128)(2,1)S(1)}, bf16[40,64,128]{2,1,0:T(8,128)(2,1)S(1)}, f32[8,128]{1,0:T(8,128)}) custom-call(bf16[16,576]{1,0:T(8,128)(2,1)S(1)} %get-tuple-element.40._.refs_3_.refs_4_, bf16[40,128,512]{2,1,0:T(8,128)(2,1)} %lat.5, bf16[40,64,128]{2,1,0:T(8,128)(2,1)} %rope.3), custom_call_target="tpu_custom_call" | custom-call | flops 9437184 | bytes 10878976 | tf_op jit(solution)/shard_map/pallas_call | solution.py:654
  15.7 2.2 %collective-permute-done.2.refs_6_ = bf16[16,576]{1,0:T(8,128)(2,1)S(1)} collective-permute-done((bf16[16,576]{1,0:T(8,128)(2,1)S(1)}, bf16[16,576]{1,0:T(8,128)(2,1)S(1)}, u32[]{:S(2)}, u32[]{:S(2)}) %collective-permute-start.2) | collective-permute-done | bytes 18464 | tf_op jit(solution)/shard_map/ppermute | solution.py:31
  18.0 3.2 %shard_map.231 = (bf16[16,640]{1,0:T(8,128)(2,1)S(1)}, bf16[16,640]{1,0:T(8,128)(2,1)S(1)}, bf16[16,640]{1,0:T(8,128)(2,1)S(1)}, bf16[16,640]{1,0:T(8,128)(2,1)S...) custom-call(s32[4,10]{1,0:T(4,128)S(1)} %copy-done.3, s32[4]{0:T(128)S(1)} %copy-done.6, ...), custom_call_target="tpu_custom_call" | custom-call | flops 167772160 | bytes 5898240 | tf_op jit(solution)/shard_map/pallas_call | solution.py:669
  21.3 2.2 %collective-permute-start.4 = (bf16[16,640]{1,0:T(8,128)(2,1)S(1)}, bf16[16,640]{1,0:T(8,128)(2,1)S(1)}, u32[]{:S(2)}, u32[]{:S(2)}) collective-permute-start(bf16[16,640]{1,0:T(8,128)(2,1)S(1)} %get-tuple-element.45), channel_id=1, source_target_pairs={{0,2},{1,3},{2,0},{3,1},{4,6},{5,7},{6,4},{7,5},{8,10},{9,11},{10,... | collective-permute-start | bytes 61448 | tf_op jit(solution)/shard_map/ppermute | solution.py:31
  23.4 2.2 %collective-permute-start.5 = (bf16[16,640]{1,0:T(8,128)(2,1)S(1)}, bf16[16,640]{1,0:T(8,128)(2,1)S(1)}, u32[]{:S(2)}, u32[]{:S(2)}) collective-permute-start(bf16[16,640]{1,0:T(8,128)(2,1)S(1)} %get-tuple-element.46), channel_id=1, source_target_pairs={{0,3},{1,2},{2,1},{3,0},{4,7},{5,6},{6,5},{7,4},{8,11},{9,10},{10,... | collective-permute-start | bytes 61448 | tf_op jit(solution)/shard_map/ppermute | solution.py:31
  25.6 3.1 %shard_map.232 = (bf16[4,512,128]{2,1,0:T(8,128)(2,1)S(1)}, bf16[512,2048]{1,0:T(8,128)(2,1)S(1)}, f32[4,640]{1,0:T(4,128)S(1)}) custom-call(s32[4]{0:T(128)S(1)} %copy-done.6, bf16[4,2048]{1,0:T(4,128)(2,1)S(1)} %get-tuple-element.47.normed, f32[1,512]{1,0:T(1,128)S(1)} %bitcast.28, bf16[16,640]{1,0:T(8,128)(2,1)S(1)} %get-tuple-element.43._.refs_0_, ...), custom_call_target="tpu_custom_call" | custom-call | flops 9437184 | bytes 4980736 | tf_op jit(solution)/shard_map/pallas_call | solution.py:681
  29.0 0.7 shard_map.233
  29.7 2.9 %collective-permute-start.7 = (bf16[4,2048]{1,0:T(4,128)(2,1)S(1)}, bf16[4,2048]{1,0:T(4,128)(2,1)S(1)}, u32[]{:S(2)}, u32[]{:S(2)}) collective-permute-start(bf16[4,2048]{1,0:T(4,128)(2,1)S(1)} %get-tuple-element.52), channel_id=1, source_target_pairs={{0,2},{1,3},{2,0},{3,1},{4,6},{5,7},{6,4},{7,5},{8,10},{9,11},{10,... | collective-permute-start | bytes 49160 | tf_op jit(solution)/shard_map/ppermute | solution.py:31
  32.6 1.5 %collective-permute-start.8 = (bf16[4,2048]{1,0:T(4,128)(2,1)S(1)}, bf16[4,2048]{1,0:T(4,128)(2,1)S(1)}, u32[]{:S(2)}, u32[]{:S(2)}) collective-permute-start(bf16[4,2048]{1,0:T(4,128)(2,1)S(1)} %get-tuple-element.52), channel_id=1, source_target_pairs={{0,3},{1,2},{2,1},{3,0},{4,7},{5,6},{6,5},{7,4},{8,11},{9,10},{10,... | collective-permute-start | bytes 49160 | tf_op jit(solution)/shard_map/ppermute | solution.py:31
  34.4 3.7 %collective-permute-done.8.refs_4_ = bf16[4,2048]{1,0:T(4,128)(2,1)S(1)} collective-permute-done((bf16[4,2048]{1,0:T(4,128)(2,1)S(1)}, bf16[4,2048]{1,0:T(4,128)(2,1)S(1)}, u32[]{:S(2)}, u32[]{:S(2)}) %collective-permute-start.8) | collective-permute-done | bytes 16416 | tf_op jit(solution)/shard_map/ppermute | solution.py:31
  38.4 1.2 %collective-permute-done.11 = bf16[4,2176]{1,0:T(4,128)(2,1)S(1)} collective-permute-done((bf16[4,2176]{1,0:T(4,128)(2,1)S(1)}, bf16[4,2176]{1,0:T(4,128)(2,1)S(1)}, u32[]{:S(2)}, u32[]{:S(2)}) %collective-permute-start.11) | collective-permute-done | bytes 17440 | tf_op jit(solution)/shard_map/ppermute | solution.py:31
  39.6 2.2 %collective-permute-start.12 = (bf16[8,2176]{1,0:T(8,128)(2,1)S(1)}, bf16[8,2176]{1,0:T(8,128)(2,1)S(1)}, u32[]{:S(2)}, u32[]{:S(2)}) collective-permute-start(bf16[8,2176]{1,0:T(8,128)(2,1)S(1)} %pad_maximum_fusion._.refs_0_), channel_id=1, source_target_pairs={{0,8},{4,12},{8,0},{12,4},{16,24},{20,28},{24,16},{28,20},{1,9},{5... | collective-permute-start | bytes 104456 | tf_op jit(solution)/shard_map/ppermute | solution.py:31
  41.7 1.2 %collective-permute-start.13 = (bf16[8,2176]{1,0:T(8,128)(2,1)S(1)}, bf16[8,2176]{1,0:T(8,128)(2,1)S(1)}, u32[]{:S(2)}, u32[]{:S(2)}) collective-permute-start(bf16[8,2176]{1,0:T(8,128)(2,1)S(1)} %pad_maximum_fusion._.refs_0_), channel_id=1, source_target_pairs={{0,16},{4,20},{8,24},{12,28},{16,0},{20,4},{24,8},{28,12},{1,17},{... | collective-permute-start | bytes 104456 | tf_op jit(solution)/shard_map/ppermute | solution.py:31
  43.4 5.1 %shard_map.235 = (f32[4,2048]{1,0:T(4,128)S(1)}, bf16[528,512]{1,0:T(8,128)(2,1)S(1)}) custom-call(s32[4,10]{1,0:T(4,128)S(1)} %copy-done.3, s32[1]{0:T(128)} %copy.40.slot_in.refs_0_.slot, bf16[4,2176]{1,0:T(4,128)(2,1)S(1)} %get-tuple-element.55.rows, bf16[4,2048]{1,0:T(4,128)(2,1)S(1)} %get-tuple-element.56.h_one, ...), custom_call_target="tpu_custom_call" | custom-call | flops 34603008 | bytes 8650752 | tf_op jit(solution)/shard_map/pallas_call | solution.py:725
  48.5 0.6 shard_map.236
  49.1 1.4 %collective-permute-start.15 = (bf16[528,512]{1,0:T(8,128)(2,1)S(1)}, bf16[528,512]{1,0:T(8,128)(2,1)S(1)}, u32[]{:S(2)}, u32[]{:S(2)}) collective-permute-start(bf16[528,512]{1,0:T(8,128)(2,1)S(1)} %get-tuple-element.58), channel_id=1, source_target_pairs={{0,16},{4,20},{8,24},{12,28},{16,0},{20,4},{24,8},{28,12},{1,17},{... | collective-permute-start | bytes 1622024 | tf_op jit(solution)/shard_map/ppermute | solution.py:31
  50.7 12.6 %shard_map.237 = (f32[16,2048]{1,0:T(8,128)S(1)}, bf16[16,2048]{1,0:T(8,128)(2,1)S(1)}) custom-call(s32[1]{0:T(128)} %bitcast.1.rank, bf16[32,2048]{1,0:T(8,128)(2,1)S(1)} %get-tuple-element.59.x, f32[32,64]{1,0:T(8,128)S(1)} %get-tuple-element.60.coef, bf16[2816,2048]{1,0:T(8,128)(2,1)} %bitcast.29, bf16[2816,2048]{1,0:T(8,128)(2,1)} %bitcast.30, ...), custom_call_target="tpu_custom_call" | custom-call | flops 1107296256 | bytes 34603008 | tf_op jit(solution)/shard_map/pallas_call | solution.py:764
  63.4 1.1 %collective-permute-done.16.got = bf16[16,2048]{1,0:T(8,128)(2,1)S(1)} collective-permute-done((bf16[16,2048]{1,0:T(8,128)(2,1)S(1)}, bf16[16,2048]{1,0:T(8,128)(2,1)S(1)}, u32[]{:S(2)}, u32[]{:S(2)}) %collective-permute-start.16) | collective-permute-done | bytes 65568 | tf_op jit(solution)/shard_map/ppermute | solution.py:31
  64.6 1.8 %collective-permute-start.17 = (bf16[4,2048]{1,0:T(4,128)(2,1)S(1)}, bf16[4,2048]{1,0:T(4,128)(2,1)S(1)}, u32[]{:S(2)}, u32[]{:S(2)}) collective-permute-start(bf16[4,2048]{1,0:T(4,128)(2,1)S(1)} %get-tuple-element.68), channel_id=1, source_target_pairs={{0,8},{4,12},{8,0},{12,4},{16,24},{20,28},{24,16},{28,20},{1,9},{5... | collective-permute-start | bytes 49160 | tf_op jit(solution)/shard_map/ppermute | solution.py:31
  66.4 0.8 %collective-permute-start.18 = (bf16[4,2048]{1,0:T(4,128)(2,1)S(1)}, bf16[4,2048]{1,0:T(4,128)(2,1)S(1)}, u32[]{:S(2)}, u32[]{:S(2)}) collective-permute-start(bf16[4,2048]{1,0:T(4,128)(2,1)S(1)} %get-tuple-element.69), channel_id=1, source_target_pairs={{0,16},{4,20},{8,24},{12,28},{16,0},{20,4},{24,8},{28,12},{1,17},{... | collective-permute-start | bytes 49160 | tf_op jit(solution)/shard_map/ppermute | solution.py:31
  67.3 0.9 %collective-permute-start.19 = (bf16[4,2048]{1,0:T(4,128)(2,1)S(1)}, bf16[4,2048]{1,0:T(4,128)(2,1)S(1)}, u32[]{:S(2)}, u32[]{:S(2)}) collective-permute-start(bf16[4,2048]{1,0:T(4,128)(2,1)S(1)} %get-tuple-element.70), channel_id=1, source_target_pairs={{0,24},{4,28},{8,16},{12,20},{16,8},{20,12},{24,0},{28,4},{1,25},{... | collective-permute-start | bytes 49160 | tf_op jit(solution)/shard_map/ppermute | solution.py:31
  68.3 1.9 %shard_map.239 = (bf16[40,128,512]{2,1,0:T(8,128)(2,1)}, bf16[40,64,128]{2,1,0:T(8,128)(2,1)}, f32[8,128]{1,0:T(8,128)S(1)}) custom-call(s32[4,10]{1,0:T(4,128)S(1)} %copy-done.3, s32[1]{0:T(128)} %copy.40.slot_in.refs_0_.slot, f32[4,2048]{1,0:T(4,128)S(1)} %get-tuple-element.63._.own, ...), custom_call_target="tpu_custom_call", output_to_operand_aliasing={{0}: (5, {}), {1}: (6, {})} | custom-call | bytes 1769472 | tf_op jit(solution)/shard_map/pallas_call | solution.py:789
  70.3 1.6 %collective-permute-done.19.refs_2_ = bf16[4,2048]{1,0:T(4,128)(2,1)S(1)} collective-permute-done((bf16[4,2048]{1,0:T(4,128)(2,1)S(1)}, bf16[4,2048]{1,0:T(4,128)(2,1)S(1)}, u32[]{:S(2)}, u32[]{:S(2)}) %collective-permute-start.19) | collective-permute-done | bytes 16416 | tf_op jit(solution)/shard_map/ppermute | solution.py:31
  71.9 1.4 %collective-permute-start.22 = (bf16[4,2048]{1,0:T(4,128)(2,1)S(1)}, bf16[4,2048]{1,0:T(4,128)(2,1)S(1)}, u32[]{:S(2)}, u32[]{:S(2)}) collective-permute-start(bf16[4,2048]{1,0:T(4,128)(2,1)S(1)} %get-tuple-element.72), channel_id=1, source_target_pairs={{0,3},{1,2},{2,1},{3,0},{4,7},{5,6},{6,5},{7,4},{8,11},{9,10},{10,... | collective-permute-start | bytes 49160 | tf_op jit(solution)/shard_map/ppermute | solution.py:31
  73.4 3.0 %collective-permute-start.20 = (bf16[4,2048]{1,0:T(4,128)(2,1)S(1)}, bf16[4,2048]{1,0:T(4,128)(2,1)S(1)}, u32[]{:S(2)}, u32[]{:S(2)}) collective-permute-start(bf16[4,2048]{1,0:T(4,128)(2,1)S(1)} %get-tuple-element.72), channel_id=1, source_target_pairs={{0,1},{1,0},{2,3},{3,2},{4,5},{5,4},{6,7},{7,6},{8,9},{9,8},{10,11... | collective-permute-start | bytes 49160 | tf_op jit(solution)/shard_map/ppermute | solution.py:31
  76.5 2.4 %shard_map.241 = (bf16[40,128,512]{2,1,0:T(8,128)(2,1)}, bf16[40,64,128]{2,1,0:T(8,128)(2,1)}) custom-call(s32[4,10]{1,0:T(4,128)S(1)} %copy-done.3, s32[1]{0:T(128)} %copy.40.slot_in.refs_0_.slot, s32[4]{0:T(128)S(1)} %add_bitcast_fusion.lengths, s32[1]{0:T(128)} %bitcast.3.refs_2_.rank, ...), custom_call_target="tpu_custom_call", output_to_operand_aliasing={{0}: (8, {}), {1}: (9, {})} | custom-call | bytes 1179648 | tf_op jit(solution)/shard_map/pallas_call | solution.py:819
  79.0 0.7 add_convert_fusion
  (58 shorter events, 2.2 us)
Async XLA Ops:
  1.3 0.7 copy-start.2
  4.7 13.3 %copy-start.3 = (s32[4,10]{1,0:T(4,128)S(1)}, s32[4,10]{1,0:T(4,128)}, u32[]{:S(2)}) copy-start(s32[4,10]{1,0:T(4,128)} %table.5) | copy-start | bytes 484
  4.7 13.3 %copy-start.6 = (s32[4]{0:T(128)S(1)}, s32[4]{0:T(128)}, u32[]{:S(2)}) copy-start(s32[4]{0:T(128)} %lengths.1) | copy-start | bytes 52
  4.7 33.5 %collective-permute-start.9 = (bf16[6,128,512]{2,1,0:T(8,128)(2,1)S(1)}, bf16[6,128,512]{2,1,0:T(8,128)(2,1)S(1)}, u32[]{:S(2)}, u32[]{:S(2)}) collective-permute-start(bf16[6,128,512]{2,1,0:T(8,128)(2,1)S(1)} %get-tuple-element.53), channel_id=1, source_target_pairs={{0,16},{4,20},{8,24},{12,28},{16,0},{20,4},{24,8},{28,12},{1,17},{... | collective-permute-start | bytes 2359304 | tf_op jit(solution)/shard_map/ppermute | solution.py:31
  7.7 30.4 %collective-permute-start.10 = (bf16[10,64,128]{2,1,0:T(8,128)(2,1)S(1)}, bf16[10,64,128]{2,1,0:T(8,128)(2,1)S(1)}, u32[]{:S(2)}, u32[]{:S(2)}) collective-permute-start(bf16[10,64,128]{2,1,0:T(8,128)(2,1)S(1)} %get-tuple-element.54), channel_id=1, source_target_pairs={{0,16},{4,20},{8,24},{12,28},{16,0},{20,4},{24,8},{28,12},{1,17},{... | collective-permute-start | bytes 491528 | tf_op jit(solution)/shard_map/ppermute | solution.py:31
  7.8 7.9 %collective-permute-start = (bf16[16,576]{1,0:T(8,128)(2,1)S(1)}, bf16[16,576]{1,0:T(8,128)(2,1)S(1)}, u32[]{:S(2)}, u32[]{:S(2)}) collective-permute-start(bf16[16,576]{1,0:T(8,128)(2,1)S(1)} %get-tuple-element.40._.refs_3_.refs_4_), channel_id=1, source_target_pairs={{0,1},{1,0},{2,3},{3,2},{4,5},{5,4},{6,7},{7,6},{8,9},{9,8},{10,11... | collective-permute-start | bytes 55304 | tf_op jit(solution)/shard_map/ppermute | solution.py:31
  9.8 5.9 %collective-permute-start.1 = (bf16[16,576]{1,0:T(8,128)(2,1)S(1)}, bf16[16,576]{1,0:T(8,128)(2,1)S(1)}, u32[]{:S(2)}, u32[]{:S(2)}) collective-permute-start(bf16[16,576]{1,0:T(8,128)(2,1)S(1)} %get-tuple-element.40._.refs_3_.refs_4_), channel_id=1, source_target_pairs={{0,2},{1,3},{2,0},{3,1},{4,6},{5,7},{6,4},{7,5},{8,10},{9,11},{10,... | collective-permute-start | bytes 55304 | tf_op jit(solution)/shard_map/ppermute | solution.py:31
  12.4 5.6 %collective-permute-start.2 = (bf16[16,576]{1,0:T(8,128)(2,1)S(1)}, bf16[16,576]{1,0:T(8,128)(2,1)S(1)}, u32[]{:S(2)}, u32[]{:S(2)}) collective-permute-start(bf16[16,576]{1,0:T(8,128)(2,1)S(1)} %get-tuple-element.40._.refs_3_.refs_4_), channel_id=1, source_target_pairs={{0,3},{1,2},{2,1},{3,0},{4,7},{5,6},{6,5},{7,4},{8,11},{9,10},{10,... | collective-permute-start | bytes 55304 | tf_op jit(solution)/shard_map/ppermute | solution.py:31
  12.4 13.3 %copy-start.5 = (f32[512]{0:T(512)S(1)}, f32[512]{0:T(512)}, u32[]{:S(2)}) copy-start(f32[512]{0:T(512)} %param.31) | copy-start | bytes 6148
  21.2 17.0 %copy-start.1 = (bf16[4,2048]{1,0:T(4,128)(2,1)S(1)}, bf16[4,2048]{1,0:T(4,128)(2,1)}, u32[]{:S(2)}) copy-start(bf16[4,2048]{1,0:T(4,128)(2,1)} %refs_5_.1) | copy-start | bytes 49156
  21.2 17.0 %copy-start.4 = (f32[2048]{0:T(1024)S(1)}, f32[2048]{0:T(1024)}, u32[]{:S(2)}) copy-start(f32[2048]{0:T(1024)} %param.35) | copy-start | bytes 24580
  21.2 22.1 %copy-start.7 = (s32[32,6]{0,1:T(8,128)S(1)}, s32[32,6]{0,1:T(8,128)}, u32[]{:S(2)}) copy-start(s32[32,6]{0,1:T(8,128)} %param.37) | copy-start | bytes 2308
  21.2 7.5 %collective-permute-start.3 = (bf16[16,640]{1,0:T(8,128)(2,1)S(1)}, bf16[16,640]{1,0:T(8,128)(2,1)S(1)}, u32[]{:S(2)}, u32[]{:S(2)}) collective-permute-start(bf16[16,640]{1,0:T(8,128)(2,1)S(1)} %get-tuple-element.44), channel_id=1, source_target_pairs={{0,1},{1,0},{2,3},{3,2},{4,5},{5,4},{6,7},{7,6},{8,9},{9,8},{10,11... | collective-permute-start | bytes 61448 | tf_op jit(solution)/shard_map/ppermute | solution.py:31
  21.3 7.4 %collective-permute-start.4 = (bf16[16,640]{1,0:T(8,128)(2,1)S(1)}, bf16[16,640]{1,0:T(8,128)(2,1)S(1)}, u32[]{:S(2)}, u32[]{:S(2)}) collective-permute-start(bf16[16,640]{1,0:T(8,128)(2,1)S(1)} %get-tuple-element.45), channel_id=1, source_target_pairs={{0,2},{1,3},{2,0},{3,1},{4,6},{5,7},{6,4},{7,5},{8,10},{9,11},{10,... | collective-permute-start | bytes 61448 | tf_op jit(solution)/shard_map/ppermute | solution.py:31
  23.4 5.6 %collective-permute-start.5 = (bf16[16,640]{1,0:T(8,128)(2,1)S(1)}, bf16[16,640]{1,0:T(8,128)(2,1)S(1)}, u32[]{:S(2)}, u32[]{:S(2)}) collective-permute-start(bf16[16,640]{1,0:T(8,128)(2,1)S(1)} %get-tuple-element.46), channel_id=1, source_target_pairs={{0,3},{1,2},{2,1},{3,0},{4,7},{5,6},{6,5},{7,4},{8,11},{9,10},{10,... | collective-permute-start | bytes 61448 | tf_op jit(solution)/shard_map/ppermute | solution.py:31
  29.7 4.4 %collective-permute-start.6 = (bf16[4,2048]{1,0:T(4,128)(2,1)S(1)}, bf16[4,2048]{1,0:T(4,128)(2,1)S(1)}, u32[]{:S(2)}, u32[]{:S(2)}) collective-permute-start(bf16[4,2048]{1,0:T(4,128)(2,1)S(1)} %get-tuple-element.52), channel_id=1, source_target_pairs={{0,1},{1,0},{2,3},{3,2},{4,5},{5,4},{6,7},{7,6},{8,9},{9,8},{10,11... | collective-permute-start | bytes 49160 | tf_op jit(solution)/shard_map/ppermute | solution.py:31
  29.7 4.7 %collective-permute-start.7 = (bf16[4,2048]{1,0:T(4,128)(2,1)S(1)}, bf16[4,2048]{1,0:T(4,128)(2,1)S(1)}, u32[]{:S(2)}, u32[]{:S(2)}) collective-permute-start(bf16[4,2048]{1,0:T(4,128)(2,1)S(1)} %get-tuple-element.52), channel_id=1, source_target_pairs={{0,2},{1,3},{2,0},{3,1},{4,6},{5,7},{6,4},{7,5},{8,10},{9,11},{10,... | collective-permute-start | bytes 49160 | tf_op jit(solution)/shard_map/ppermute | solution.py:31
  32.6 5.5 %collective-permute-start.8 = (bf16[4,2048]{1,0:T(4,128)(2,1)S(1)}, bf16[4,2048]{1,0:T(4,128)(2,1)S(1)}, u32[]{:S(2)}, u32[]{:S(2)}) collective-permute-start(bf16[4,2048]{1,0:T(4,128)(2,1)S(1)} %get-tuple-element.52), channel_id=1, source_target_pairs={{0,3},{1,2},{2,1},{3,0},{4,7},{5,6},{6,5},{7,4},{8,11},{9,10},{10,... | collective-permute-start | bytes 49160 | tf_op jit(solution)/shard_map/ppermute | solution.py:31
  38.3 1.3 %collective-permute-start.11 = (bf16[4,2176]{1,0:T(4,128)(2,1)S(1)}, bf16[4,2176]{1,0:T(4,128)(2,1)S(1)}, u32[]{:S(2)}, u32[]{:S(2)}) collective-permute-start(bf16[4,2176]{1,0:T(4,128)(2,1)S(1)} %get-tuple-element.55.rows), channel_id=1, source_target_pairs={{0,4},{4,0},{8,12},{12,8},{16,20},{20,16},{24,28},{28,24},{1,5},{5... | collective-permute-start | bytes 52232 | tf_op jit(solution)/shard_map/ppermute | solution.py:31
  39.6 8.9 %collective-permute-start.12 = (bf16[8,2176]{1,0:T(8,128)(2,1)S(1)}, bf16[8,2176]{1,0:T(8,128)(2,1)S(1)}, u32[]{:S(2)}, u32[]{:S(2)}) collective-permute-start(bf16[8,2176]{1,0:T(8,128)(2,1)S(1)} %pad_maximum_fusion._.refs_0_), channel_id=1, source_target_pairs={{0,8},{4,12},{8,0},{12,4},{16,24},{20,28},{24,16},{28,20},{1,9},{5... | collective-permute-start | bytes 104456 | tf_op jit(solution)/shard_map/ppermute | solution.py:31
  41.7 6.7 %collective-permute-start.13 = (bf16[8,2176]{1,0:T(8,128)(2,1)S(1)}, bf16[8,2176]{1,0:T(8,128)(2,1)S(1)}, u32[]{:S(2)}, u32[]{:S(2)}) collective-permute-start(bf16[8,2176]{1,0:T(8,128)(2,1)S(1)} %pad_maximum_fusion._.refs_0_), channel_id=1, source_target_pairs={{0,16},{4,20},{8,24},{12,28},{16,0},{20,4},{24,8},{28,12},{1,17},{... | collective-permute-start | bytes 104456 | tf_op jit(solution)/shard_map/ppermute | solution.py:31
  42.9 5.6 %collective-permute-start.14 = (bf16[8,2176]{1,0:T(8,128)(2,1)S(1)}, bf16[8,2176]{1,0:T(8,128)(2,1)S(1)}, u32[]{:S(2)}, u32[]{:S(2)}) collective-permute-start(bf16[8,2176]{1,0:T(8,128)(2,1)S(1)} %pad_maximum_fusion._.refs_0_), channel_id=1, source_target_pairs={{0,24},{4,28},{8,16},{12,20},{16,8},{20,12},{24,0},{28,4},{1,25},{... | collective-permute-start | bytes 104456 | tf_op jit(solution)/shard_map/ppermute | solution.py:31
  43.4 5.1 %copy-start = (bf16[2048,64]{0,1:T(8,128)(2,1)S(1)}, bf16[2048,64]{0,1:T(8,128)(2,1)}, u32[]{:S(2)}) copy-start(bf16[2048,64]{0,1:T(8,128)(2,1)} %param.36) | copy-start | bytes 786436
  49.1 14.2 %collective-permute-start.15 = (bf16[528,512]{1,0:T(8,128)(2,1)S(1)}, bf16[528,512]{1,0:T(8,128)(2,1)S(1)}, u32[]{:S(2)}, u32[]{:S(2)}) collective-permute-start(bf16[528,512]{1,0:T(8,128)(2,1)S(1)} %get-tuple-element.58), channel_id=1, source_target_pairs={{0,16},{4,20},{8,24},{12,28},{16,0},{20,4},{24,8},{28,12},{1,17},{... | collective-permute-start | bytes 1622024 | tf_op jit(solution)/shard_map/ppermute | solution.py:31
  63.2 1.3 %collective-permute-start.16 = (bf16[16,2048]{1,0:T(8,128)(2,1)S(1)}, bf16[16,2048]{1,0:T(8,128)(2,1)S(1)}, u32[]{:S(2)}, u32[]{:S(2)}) collective-permute-start(bf16[16,2048]{1,0:T(8,128)(2,1)S(1)} %get-tuple-element.62), channel_id=1, source_target_pairs={{0,4},{4,0},{8,12},{12,8},{16,20},{20,16},{24,28},{28,24},{1,5},{5... | collective-permute-start | bytes 196616 | tf_op jit(solution)/shard_map/ppermute | solution.py:31
  64.6 5.7 %collective-permute-start.17 = (bf16[4,2048]{1,0:T(4,128)(2,1)S(1)}, bf16[4,2048]{1,0:T(4,128)(2,1)S(1)}, u32[]{:S(2)}, u32[]{:S(2)}) collective-permute-start(bf16[4,2048]{1,0:T(4,128)(2,1)S(1)} %get-tuple-element.68), channel_id=1, source_target_pairs={{0,8},{4,12},{8,0},{12,4},{16,24},{20,28},{24,16},{28,20},{1,9},{5... | collective-permute-start | bytes 49160 | tf_op jit(solution)/shard_map/ppermute | solution.py:31
  66.4 3.8 %collective-permute-start.18 = (bf16[4,2048]{1,0:T(4,128)(2,1)S(1)}, bf16[4,2048]{1,0:T(4,128)(2,1)S(1)}, u32[]{:S(2)}, u32[]{:S(2)}) collective-permute-start(bf16[4,2048]{1,0:T(4,128)(2,1)S(1)} %get-tuple-element.69), channel_id=1, source_target_pairs={{0,16},{4,20},{8,24},{12,28},{16,0},{20,4},{24,8},{28,12},{1,17},{... | collective-permute-start | bytes 49160 | tf_op jit(solution)/shard_map/ppermute | solution.py:31
  67.3 4.6 %collective-permute-start.19 = (bf16[4,2048]{1,0:T(4,128)(2,1)S(1)}, bf16[4,2048]{1,0:T(4,128)(2,1)S(1)}, u32[]{:S(2)}, u32[]{:S(2)}) collective-permute-start(bf16[4,2048]{1,0:T(4,128)(2,1)S(1)} %get-tuple-element.70), channel_id=1, source_target_pairs={{0,24},{4,28},{8,16},{12,20},{16,8},{20,12},{24,0},{28,4},{1,25},{... | collective-permute-start | bytes 49160 | tf_op jit(solution)/shard_map/ppermute | solution.py:31
  71.9 7.0 %collective-permute-start.22 = (bf16[4,2048]{1,0:T(4,128)(2,1)S(1)}, bf16[4,2048]{1,0:T(4,128)(2,1)S(1)}, u32[]{:S(2)}, u32[]{:S(2)}) collective-permute-start(bf16[4,2048]{1,0:T(4,128)(2,1)S(1)} %get-tuple-element.72), channel_id=1, source_target_pairs={{0,3},{1,2},{2,1},{3,0},{4,7},{5,6},{6,5},{7,4},{8,11},{9,10},{10,... | collective-permute-start | bytes 49160 | tf_op jit(solution)/shard_map/ppermute | solution.py:31
  73.4 5.6 %collective-permute-start.21 = (bf16[4,2048]{1,0:T(4,128)(2,1)S(1)}, bf16[4,2048]{1,0:T(4,128)(2,1)S(1)}, u32[]{:S(2)}, u32[]{:S(2)}) collective-permute-start(bf16[4,2048]{1,0:T(4,128)(2,1)S(1)} %get-tuple-element.72), channel_id=1, source_target_pairs={{0,2},{1,3},{2,0},{3,1},{4,6},{5,7},{6,4},{7,5},{8,10},{9,11},{10,... | collective-permute-start | bytes 49160 | tf_op jit(solution)/shard_map/ppermute | solution.py:31
  73.4 5.6 %collective-permute-start.20 = (bf16[4,2048]{1,0:T(4,128)(2,1)S(1)}, bf16[4,2048]{1,0:T(4,128)(2,1)S(1)}, u32[]{:S(2)}, u32[]{:S(2)}) collective-permute-start(bf16[4,2048]{1,0:T(4,128)(2,1)S(1)} %get-tuple-element.72), channel_id=1, source_target_pairs={{0,1},{1,0},{2,3},{3,2},{4,5},{5,4},{6,7},{7,6},{8,9},{9,8},{10,11... | collective-permute-start | bytes 49160 | tf_op jit(solution)/shard_map/ppermute | solution.py:31

commit v5 on v4

--- a/solution.py
+++ b/solution.py
@@ -398,13 +398,12 @@
 
 
 def shared_kernel(
-    first, count, table, slot, rows, h_one, new, _, gate, up, down, lat,
-    out, next_out, gate_v, up_v, down_v, sems, page_sems,
+    first, count, table, slot, rows, h_one, new, _, gate, up, lat,
+    out, next_out, gate_v, up_v, sems, page_sems,
 ):
     copies = [
         pltpu.make_async_copy(gate, gate_v, sems.at[0]),
         pltpu.make_async_copy(up, up_v, sems.at[1]),
-        pltpu.make_async_copy(down, down_v, sems.at[2]),
     ]
     for copy in copies:
         copy.start()
@@ -414,11 +413,9 @@
     gate_val = lax.dot_general(x, gate_v[...], NT, preferred_element_type=F32)
     copies[1].wait()
     up_val = lax.dot_general(x, up_v[...], NT, preferred_element_type=F32)
-    hid = (silu(gate_val) * up_val).astype(BF16)
-    copies[2].wait()
-    shared = jnp.dot(hid, down_v[...], preferred_element_type=F32)
-    out[...] = shared
-    every = jnp.concatenate([h_one[...].astype(F32), new[...], shared], axis=1)
+    hid = silu(gate_val) * up_val
+    out[...] = hid.astype(BF16)
+    every = jnp.concatenate([h_one[...].astype(F32), new[...], hid], axis=1)
     row = lax.broadcasted_iota(jnp.int32, every.shape, 0)
     every = jnp.sum(jnp.where(row == slot[0], every, 0.0), axis=0, keepdims=True)
     lat_size = next_out.shape[1]
@@ -430,10 +427,9 @@
         copy.wait()
 
 
-def total_kernel(slot, got, own, shared, _, *refs):
+def total_kernel(own, shared, *refs):
     others, (total, sent) = refs[:-2], refs[-2:]
-    row = lax.broadcasted_iota(jnp.int32, own.shape, 0)
-    value = own[...] + jnp.where(row == slot[0], got[...].astype(F32), shared[...])
+    value = own[...] + shared[...]
     for other in others:
         value += other[...].astype(F32)
     total[...] = value
@@ -450,13 +446,14 @@
 
 
 def cache_kernel(
-    first, table, slot, _, got_lat, got_rope, lat_in, rope_in,
-    lat_out, rope_out, token, lat_v, rope_v, got_sems, sems,
+    first, table, slot, _, hid, got_hid, down, got_lat, got_rope, lat_in, rope_in,
+    lat_out, rope_out, shared, lat_v, rope_v, down_v, got_sems, sems,
 ):
     del lat_in, rope_in
     per_dev = table.shape[1]
     moved = slot[0]
-    token[...] = jnp.zeros_like(token)
+    weights = pltpu.make_async_copy(down, down_v, got_sems.at[2])
+    weights.start()
     fetches = [
         pltpu.make_async_copy(got_rope, rope_v, got_sems.at[0]),
         pltpu.make_async_copy(got_lat, lat_v, got_sems.at[1]),
@@ -473,6 +470,10 @@
         copies.append(pltpu.make_async_copy(rope_v.at[j], rope_out.at[page], sems.at[1, j]))
     for copy in copies:
         copy.start()
+    row = lax.broadcasted_iota(jnp.int32, hid.shape, 0)
+    served = jnp.where(row == moved, got_hid[...].astype(F32), hid[...].astype(F32)).astype(BF16)
+    weights.wait()
+    shared[...] = jnp.dot(served, down_v[...], preferred_element_type=F32)
     for copy in copies:
         copy.wait()
 
@@ -722,19 +723,18 @@
     pair = jnp.concatenate([ffn_row, xored(ffn_row, "rep", 1)], axis=0)
     pieces = [pair] + [xored(pair, "rep", 2 * k) for k in range(1, groups)]
 
-    shared_part, out_second = call(
+    shared_hid, out_second = call(
         functools.partial(shared_kernel, first_span, second_span),
         (
-            struct((requests, size), F32),
+            struct((requests, shared_gate.shape[1]), BF16),
             struct((second_span * PAGE + ROWS, lat_size), BF16),
         ),
-        [SMEM, SMEM] + [VMEM] * 4 + [ANY] * 4,
+        [SMEM, SMEM] + [VMEM] * 4 + [ANY] * 3,
         (VMEM, VMEM),
         [
             pltpu.VMEM((shared_gate.shape[1], size), BF16),
             pltpu.VMEM((shared_gate.shape[1], size), BF16),
-            pltpu.VMEM(shared_down.shape, BF16),
-            dma((3,)),
+            dma((2,)),
             dma((second_span,)),
         ],
         vmem=12,
@@ -742,7 +742,7 @@
         nbytes=6 * shared_gate.size,
     )(
         page_table, move_slot, ffn_row, h_one, new, pair, in_hbm(shared_gate.T),
-        in_hbm(shared_up.T), in_hbm(shared_down), lat_hbm,
+        in_hbm(shared_up.T), lat_hbm,
     )
     x_all, coef, out_second = call(
         functools.partial(order_kernel, groups, requests),
@@ -759,7 +759,7 @@
         aliases={3 + groups: 2},
     )(rep_one, route_ids, w_router.T, *pieces, out_second)
     got_second = xored(out_second, "rep", half)
-    got_row = got_second[second_span * PAGE :].reshape(1, -1)[:, : size + width + size]
+    got_row = got_second[second_span * PAGE :].reshape(1, -1)
 
     kept, sent = call(
         functools.partial(expert_kernel, requests, 512, units),
@@ -786,29 +786,34 @@
         nbytes=8 * everyone * size,
     )(kept, xored(sent, "rep", 1), got_second)
     others = [xored(summed[k], "rep", 2 * k) for k in range(1, groups)]
-    lat_most, rope_most, cache_token = call(
+    lat_most, rope_most, shared_part = call(
         functools.partial(cache_kernel, first_span),
-        (struct(lat_pool.shape, BF16), struct(rope_pool.shape, BF16), struct((8, LANES), F32)),
-        [SMEM] * 2 + [VMEM] + [ANY] * 4,
+        (struct(lat_pool.shape, BF16), struct(rope_pool.shape, BF16), struct((requests, size), F32)),
+        [SMEM] * 2 + [VMEM] * 3 + [ANY] * 5,
         (ANY, ANY, VMEM),
         [
             pltpu.VMEM((first_span,) + lat_page, BF16),
             pltpu.VMEM((per_dev,) + rope_page, BF16),
-            dma((2,)),
+            pltpu.VMEM(shared_down.shape, BF16),
+            dma((3,)),
             dma((2, per_dev)),
         ],
-        vmem=4,
+        vmem=8,
         nbytes=2 * first_span * page_bytes,
-        aliases={5: 0, 6: 1},
-    )(page_table, move_slot, summed[0], got_first, got_rope, lat_most, rope_most)
+        aliases={8: 0, 9: 1},
+    )(
+        page_table, move_slot, summed[0], shared_hid,
+        got_row[:, size + width : size + width + shared_gate.shape[1]], in_hbm(shared_down),
+        got_first, got_rope, lat_most, rope_most,
+    )
     total, total_sent = call(
         total_kernel,
         (struct((requests, size), F32), struct((requests, size), BF16)),
-        [SMEM] + [VMEM] * (groups + 3),
+        [VMEM] * (groups + 1),
         (VMEM, VMEM),
         vmem=4,
         nbytes=8 * everyone * size,
-    )(move_slot, got_row[:, size + width :], summed[0], shared_part, cache_token, *others)
+    )(summed[0], shared_part, *others)
 
     is_moved = (jnp.arange(requests, dtype=jnp.int32) == move_slot[0])[:, None]
     new_served = jnp.where(is_moved, got_row[:, size : size + width].astype(F32), new)

time: 79.6 us -> 79.4 us (level)
  waiting for transfers between devices: 10.5 us -> 8.75 us
  Pallas kernels: 35.6 us -> 36.9 us
    ppermute x23, waiting for transfers between devices: 10.5 us -> 8.75 us  [xored(): return lax.ppermute(value, axis, pairs)]
    pallas_call x1, Pallas kernels: 1.94 us -> 3.45 us  [body(): call(functools.partial(cache_kernel, first_span), (struct(lat_pool.shape,...]
  transfers between devices with their start and end apart: 23 -> 23, of which waited for: 7 -> 5; matrix products, arithmetic and copies ran while one was open for 1% -> 1% of each run, Pallas kernels for 40% -> 42%
where the time goes in v5:
time: 79.4 us; the launch traced here: 78.9 us
  Pallas kernels  36.9 us (46%)
  starting transfers between devices  29.5 us (37%)
  waiting for transfers between devices  8.75 us (11%)
  between operations  1.65 us (2%)
  local copies, waits for them, and re-layouts  1.17 us (1%)
  other arithmetic  0.88 us (1%)
    ppermute x23, starting transfers between devices, xored(): return lax.ppermute(value, axis, pairs)  29.5 us
    pallas_call x1, Pallas kernels, body(): call(functools.partial(expert_kernel, requests, 512, units), (struct((gro...  12.6 us
    ppermute x23, waiting for transfers between devices, xored(): return lax.ppermute(value, axis, pairs)  8.75 us
    pallas_call x1, Pallas kernels, body(): call(functools.partial(shared_kernel, first_span, second_span), (struct((...  4.58 us
    pallas_call x1, Pallas kernels, body(): call(functools.partial(attention_kernel, n_tp, per_dev, requests, lat_siz...  3.46 us
    pallas_call x1, Pallas kernels, body(): call(functools.partial(cache_kernel, first_span), (struct(lat_pool.shape,...  3.45 us
    pallas_call x1, Pallas kernels, body(): call(functools.partial(fetch_kernel, requests), (pltpu.VMEM((pages,) + la...  3.31 us
    pallas_call x1, Pallas kernels, body(): call(token_weights_kernel, (pltpu.VMEM(w_value_up.shape, BF16), pltpu.VME...  3.05 us
  transfers between devices with their start and end apart: 23, of which 5 were waited for; matrix products, arithmetic and copies ran while one was open for 1% of the time, Pallas kernels for 42%

profile of v5, /device:TPU:0, one launch (start us, length us, event | category | flops | bytes accessed | tf_op | source)
XLA Modules:
  0.0 78.9 jit_solution(16557620257836182219)
XLA Ops:
  1.3 0.7 copy-done.2
  2.0 2.7 %shard_map.229 = (bf16[16,576]{1,0:T(8,128)(2,1)S(1)}, bf16[4,2048]{1,0:T(4,128)(2,1)S(1)}, bf16[6,128,512]{2,1,0:T(8,128)(2,1)S(1)}, bf16[10,64,128]{2,1,0:T(8,128)(2,1)S(1)}) custom-call(s32[4,10]{1,0:T(4,128)S(1)} %copy-done.2, s32[1]{0:T(128)} %copy.40.slot_in.refs_0_.slot, bf16[4,2048]{1,0:T(4,128)(2,1)} %refs_5_.1, f32[1,2048]{1,0:T(1,128)} %bitcast.38, ...), custom_call_target="tpu_custom_call" | custom-call | flops 12582912 | bytes 3145728 | tf_op jit(solution)/shard_map/pallas_call | solution.py:624
  4.7 3.0 %collective-permute-start.9 = (bf16[6,128,512]{2,1,0:T(8,128)(2,1)S(1)}, bf16[6,128,512]{2,1,0:T(8,128)(2,1)S(1)}, u32[]{:S(2)}, u32[]{:S(2)}) collective-permute-start(bf16[6,128,512]{2,1,0:T(8,128)(2,1)S(1)} %get-tuple-element.53), channel_id=1, source_target_pairs={{0,16},{4,20},{8,24},{12,28},{16,0},{20,4},{24,8},{28,12},{1,17},{... | collective-permute-start | bytes 2359304 | tf_op jit(solution)/shard_map/ppermute | solution.py:31
  7.8 2.0 %collective-permute-start = (bf16[16,576]{1,0:T(8,128)(2,1)S(1)}, bf16[16,576]{1,0:T(8,128)(2,1)S(1)}, u32[]{:S(2)}, u32[]{:S(2)}) collective-permute-start(bf16[16,576]{1,0:T(8,128)(2,1)S(1)} %get-tuple-element.40._.refs_3_.refs_4_), channel_id=1, source_target_pairs={{0,1},{1,0},{2,3},{3,2},{4,5},{5,4},{6,7},{7,6},{8,9},{9,8},{10,11... | collective-permute-start | bytes 55304 | tf_op jit(solution)/shard_map/ppermute | solution.py:31
  9.8 2.6 %collective-permute-start.1 = (bf16[16,576]{1,0:T(8,128)(2,1)S(1)}, bf16[16,576]{1,0:T(8,128)(2,1)S(1)}, u32[]{:S(2)}, u32[]{:S(2)}) collective-permute-start(bf16[16,576]{1,0:T(8,128)(2,1)S(1)} %get-tuple-element.40._.refs_3_.refs_4_), channel_id=1, source_target_pairs={{0,2},{1,3},{2,0},{3,1},{4,6},{5,7},{6,4},{7,5},{8,10},{9,11},{10,... | collective-permute-start | bytes 55304 | tf_op jit(solution)/shard_map/ppermute | solution.py:31
  12.4 3.3 %shard_map.230 = (bf16[40,128,512]{2,1,0:T(8,128)(2,1)S(1)}, bf16[40,64,128]{2,1,0:T(8,128)(2,1)S(1)}, f32[8,128]{1,0:T(8,128)}) custom-call(bf16[16,576]{1,0:T(8,128)(2,1)S(1)} %get-tuple-element.40._.refs_3_.refs_4_, bf16[40,128,512]{2,1,0:T(8,128)(2,1)} %lat.5, bf16[40,64,128]{2,1,0:T(8,128)(2,1)} %rope.3), custom_call_target="tpu_custom_call" | custom-call | flops 9437184 | bytes 10878976 | tf_op jit(solution)/shard_map/pallas_call | solution.py:655
  15.7 2.2 %collective-permute-done.2.refs_6_ = bf16[16,576]{1,0:T(8,128)(2,1)S(1)} collective-permute-done((bf16[16,576]{1,0:T(8,128)(2,1)S(1)}, bf16[16,576]{1,0:T(8,128)(2,1)S(1)}, u32[]{:S(2)}, u32[]{:S(2)}) %collective-permute-start.2) | collective-permute-done | bytes 18464 | tf_op jit(solution)/shard_map/ppermute | solution.py:31
  18.0 3.5 %shard_map.231 = (bf16[16,640]{1,0:T(8,128)(2,1)S(1)}, bf16[16,640]{1,0:T(8,128)(2,1)S(1)}, bf16[16,640]{1,0:T(8,128)(2,1)S(1)}, bf16[16,640]{1,0:T(8,128)(2,1)S...) custom-call(s32[4,10]{1,0:T(4,128)S(1)} %copy-done.3, s32[4]{0:T(128)S(1)} %copy-done.6, ...), custom_call_target="tpu_custom_call" | custom-call | flops 167772160 | bytes 5898240 | tf_op jit(solution)/shard_map/pallas_call | solution.py:670
  21.6 1.9 %collective-permute-start.4 = (bf16[16,640]{1,0:T(8,128)(2,1)S(1)}, bf16[16,640]{1,0:T(8,128)(2,1)S(1)}, u32[]{:S(2)}, u32[]{:S(2)}) collective-permute-start(bf16[16,640]{1,0:T(8,128)(2,1)S(1)} %get-tuple-element.45), channel_id=1, source_target_pairs={{0,2},{1,3},{2,0},{3,1},{4,6},{5,7},{6,4},{7,5},{8,10},{9,11},{10,... | collective-permute-start | bytes 61448 | tf_op jit(solution)/shard_map/ppermute | solution.py:31
  23.4 2.5 %collective-permute-start.5 = (bf16[16,640]{1,0:T(8,128)(2,1)S(1)}, bf16[16,640]{1,0:T(8,128)(2,1)S(1)}, u32[]{:S(2)}, u32[]{:S(2)}) collective-permute-start(bf16[16,640]{1,0:T(8,128)(2,1)S(1)} %get-tuple-element.46), channel_id=1, source_target_pairs={{0,3},{1,2},{2,1},{3,0},{4,7},{5,6},{6,5},{7,4},{8,11},{9,10},{10,... | collective-permute-start | bytes 61448 | tf_op jit(solution)/shard_map/ppermute | solution.py:31
  25.9 3.1 %shard_map.232 = (bf16[4,512,128]{2,1,0:T(8,128)(2,1)S(1)}, bf16[512,2048]{1,0:T(8,128)(2,1)S(1)}, f32[4,640]{1,0:T(4,128)S(1)}) custom-call(s32[4]{0:T(128)S(1)} %copy-done.6, bf16[4,2048]{1,0:T(4,128)(2,1)S(1)} %get-tuple-element.47.normed, f32[1,512]{1,0:T(1,128)S(1)} %bitcast.28, bf16[16,640]{1,0:T(8,128)(2,1)S(1)} %get-tuple-element.43._.refs_0_, ...), custom_call_target="tpu_custom_call" | custom-call | flops 9437184 | bytes 4980736 | tf_op jit(solution)/shard_map/pallas_call | solution.py:682
  29.0 0.7 shard_map.233
  29.7 3.2 %collective-permute-start.7 = (bf16[4,2048]{1,0:T(4,128)(2,1)S(1)}, bf16[4,2048]{1,0:T(4,128)(2,1)S(1)}, u32[]{:S(2)}, u32[]{:S(2)}) collective-permute-start(bf16[4,2048]{1,0:T(4,128)(2,1)S(1)} %get-tuple-element.52), channel_id=1, source_target_pairs={{0,2},{1,3},{2,0},{3,1},{4,6},{5,7},{6,4},{7,5},{8,10},{9,11},{10,... | collective-permute-start | bytes 49160 | tf_op jit(solution)/shard_map/ppermute | solution.py:31
  32.9 1.2 %collective-permute-start.8 = (bf16[4,2048]{1,0:T(4,128)(2,1)S(1)}, bf16[4,2048]{1,0:T(4,128)(2,1)S(1)}, u32[]{:S(2)}, u32[]{:S(2)}) collective-permute-start(bf16[4,2048]{1,0:T(4,128)(2,1)S(1)} %get-tuple-element.52), channel_id=1, source_target_pairs={{0,3},{1,2},{2,1},{3,0},{4,7},{5,6},{6,5},{7,4},{8,11},{9,10},{10,... | collective-permute-start | bytes 49160 | tf_op jit(solution)/shard_map/ppermute | solution.py:31
  34.6 3.8 %collective-permute-done.8.refs_4_ = bf16[4,2048]{1,0:T(4,128)(2,1)S(1)} collective-permute-done((bf16[4,2048]{1,0:T(4,128)(2,1)S(1)}, bf16[4,2048]{1,0:T(4,128)(2,1)S(1)}, u32[]{:S(2)}, u32[]{:S(2)}) %collective-permute-start.8) | collective-permute-done | bytes 16416 | tf_op jit(solution)/shard_map/ppermute | solution.py:31
  38.6 1.2 %collective-permute-done.11 = bf16[4,2176]{1,0:T(4,128)(2,1)S(1)} collective-permute-done((bf16[4,2176]{1,0:T(4,128)(2,1)S(1)}, bf16[4,2176]{1,0:T(4,128)(2,1)S(1)}, u32[]{:S(2)}, u32[]{:S(2)}) %collective-permute-start.11) | collective-permute-done | bytes 17440 | tf_op jit(solution)/shard_map/ppermute | solution.py:31
  39.8 1.6 %collective-permute-start.12 = (bf16[8,2176]{1,0:T(8,128)(2,1)S(1)}, bf16[8,2176]{1,0:T(8,128)(2,1)S(1)}, u32[]{:S(2)}, u32[]{:S(2)}) collective-permute-start(bf16[8,2176]{1,0:T(8,128)(2,1)S(1)} %pad_maximum_fusion._.refs_0_), channel_id=1, source_target_pairs={{0,8},{4,12},{8,0},{12,4},{16,24},{20,28},{24,16},{28,20},{1,9},{5... | collective-permute-start | bytes 104456 | tf_op jit(solution)/shard_map/ppermute | solution.py:31
  41.4 1.2 %collective-permute-start.13 = (bf16[8,2176]{1,0:T(8,128)(2,1)S(1)}, bf16[8,2176]{1,0:T(8,128)(2,1)S(1)}, u32[]{:S(2)}, u32[]{:S(2)}) collective-permute-start(bf16[8,2176]{1,0:T(8,128)(2,1)S(1)} %pad_maximum_fusion._.refs_0_), channel_id=1, source_target_pairs={{0,16},{4,20},{8,24},{12,28},{16,0},{20,4},{24,8},{28,12},{1,17},{... | collective-permute-start | bytes 104456 | tf_op jit(solution)/shard_map/ppermute | solution.py:31
  42.6 0.8 collective-permute-start.14
  43.5 4.6 %shard_map.235 = (bf16[4,704]{1,0:T(4,128)(2,1)S(1)}, bf16[528,512]{1,0:T(8,128)(2,1)S(1)}) custom-call(s32[4,10]{1,0:T(4,128)S(1)} %copy-done.3, s32[1]{0:T(128)} %copy.40.slot_in.refs_0_.slot, bf16[4,2176]{1,0:T(4,128)(2,1)S(1)} %get-tuple-element.55.rows, bf16[4,2048]{1,0:T(4,128)(2,1)S(1)} %get-tuple-element.56.h_one, ...), custom_call_target="tpu_custom_call" | custom-call | flops 34603008 | bytes 8650752 | tf_op jit(solution)/shard_map/pallas_call | solution.py:726
  48.1 0.6 shard_map.236
  48.7 1.3 %collective-permute-start.15 = (bf16[528,512]{1,0:T(8,128)(2,1)S(1)}, bf16[528,512]{1,0:T(8,128)(2,1)S(1)}, u32[]{:S(2)}, u32[]{:S(2)}) collective-permute-start(bf16[528,512]{1,0:T(8,128)(2,1)S(1)} %get-tuple-element.58), channel_id=1, source_target_pairs={{0,16},{4,20},{8,24},{12,28},{16,0},{20,4},{24,8},{28,12},{1,17},{... | collective-permute-start | bytes 1622024 | tf_op jit(solution)/shard_map/ppermute | solution.py:31
  50.2 12.6 %shard_map.237 = (f32[16,2048]{1,0:T(8,128)S(1)}, bf16[16,2048]{1,0:T(8,128)(2,1)S(1)}) custom-call(s32[1]{0:T(128)} %bitcast.1.rank, bf16[32,2048]{1,0:T(8,128)(2,1)S(1)} %get-tuple-element.59.x, f32[32,64]{1,0:T(8,128)S(1)} %get-tuple-element.60.coef, bf16[2816,2048]{1,0:T(8,128)(2,1)} %bitcast.29, bf16[2816,2048]{1,0:T(8,128)(2,1)} %bitcast.30, ...), custom_call_target="tpu_custom_call" | custom-call | flops 1107296256 | bytes 34603008 | tf_op jit(solution)/shard_map/pallas_call | solution.py:764
  63.1 1.0 %collective-permute-done.16.got = bf16[16,2048]{1,0:T(8,128)(2,1)S(1)} collective-permute-done((bf16[16,2048]{1,0:T(8,128)(2,1)S(1)}, bf16[16,2048]{1,0:T(8,128)(2,1)S(1)}, u32[]{:S(2)}, u32[]{:S(2)}) %collective-permute-start.16) | collective-permute-done | bytes 65568 | tf_op jit(solution)/shard_map/ppermute | solution.py:31
  64.1 1.6 %collective-permute-start.17 = (bf16[4,2048]{1,0:T(4,128)(2,1)S(1)}, bf16[4,2048]{1,0:T(4,128)(2,1)S(1)}, u32[]{:S(2)}, u32[]{:S(2)}) collective-permute-start(bf16[4,2048]{1,0:T(4,128)(2,1)S(1)} %get-tuple-element.68), channel_id=1, source_target_pairs={{0,8},{4,12},{8,0},{12,4},{16,24},{20,28},{24,16},{28,20},{1,9},{5... | collective-permute-start | bytes 49160 | tf_op jit(solution)/shard_map/ppermute | solution.py:31
  65.6 0.8 %collective-permute-start.18 = (bf16[4,2048]{1,0:T(4,128)(2,1)S(1)}, bf16[4,2048]{1,0:T(4,128)(2,1)S(1)}, u32[]{:S(2)}, u32[]{:S(2)}) collective-permute-start(bf16[4,2048]{1,0:T(4,128)(2,1)S(1)} %get-tuple-element.69), channel_id=1, source_target_pairs={{0,16},{4,20},{8,24},{12,28},{16,0},{20,4},{24,8},{28,12},{1,17},{... | collective-permute-start | bytes 49160 | tf_op jit(solution)/shard_map/ppermute | solution.py:31
  66.4 1.2 %collective-permute-start.19 = (bf16[4,2048]{1,0:T(4,128)(2,1)S(1)}, bf16[4,2048]{1,0:T(4,128)(2,1)S(1)}, u32[]{:S(2)}, u32[]{:S(2)}) collective-permute-start(bf16[4,2048]{1,0:T(4,128)(2,1)S(1)} %get-tuple-element.70), channel_id=1, source_target_pairs={{0,24},{4,28},{8,16},{12,20},{16,8},{20,12},{24,0},{28,4},{1,25},{... | collective-permute-start | bytes 49160 | tf_op jit(solution)/shard_map/ppermute | solution.py:31
  67.7 3.4 %shard_map.239 = (bf16[40,128,512]{2,1,0:T(8,128)(2,1)}, bf16[40,64,128]{2,1,0:T(8,128)(2,1)}, f32[4,2048]{1,0:T(4,128)S(1)}) custom-call(s32[4,10]{1,0:T(4,128)S(1)} %copy-done.3, s32[1]{0:T(128)} %copy.40.slot_in.refs_0_.slot, f32[4,2048]{1,0:T(4,128)S(1)} %get-tuple-element.63._.own, ...), custom_call_target="tpu_custom_call", output_to_operand_aliasing={{0}: (8, {}), {1}: (9, {})} | custom-call | bytes 1769472 | tf_op jit(solution)/shard_map/pallas_call | solution.py:789
  71.2 1.6 %collective-permute-start.22 = (bf16[4,2048]{1,0:T(4,128)(2,1)S(1)}, bf16[4,2048]{1,0:T(4,128)(2,1)S(1)}, u32[]{:S(2)}, u32[]{:S(2)}) collective-permute-start(bf16[4,2048]{1,0:T(4,128)(2,1)S(1)} %get-tuple-element.72), channel_id=1, source_target_pairs={{0,3},{1,2},{2,1},{3,0},{4,7},{5,6},{6,5},{7,4},{8,11},{9,10},{10,... | collective-permute-start | bytes 49160 | tf_op jit(solution)/shard_map/ppermute | solution.py:31
  72.7 2.9 %collective-permute-start.20 = (bf16[4,2048]{1,0:T(4,128)(2,1)S(1)}, bf16[4,2048]{1,0:T(4,128)(2,1)S(1)}, u32[]{:S(2)}, u32[]{:S(2)}) collective-permute-start(bf16[4,2048]{1,0:T(4,128)(2,1)S(1)} %get-tuple-element.72), channel_id=1, source_target_pairs={{0,1},{1,0},{2,3},{3,2},{4,5},{5,4},{6,7},{7,6},{8,9},{9,8},{10,11... | collective-permute-start | bytes 49160 | tf_op jit(solution)/shard_map/ppermute | solution.py:31
  75.8 2.4 %shard_map.241 = (bf16[40,128,512]{2,1,0:T(8,128)(2,1)}, bf16[40,64,128]{2,1,0:T(8,128)(2,1)}) custom-call(s32[4,10]{1,0:T(4,128)S(1)} %copy-done.3, s32[1]{0:T(128)} %copy.40.slot_in.refs_0_.slot, s32[4]{0:T(128)S(1)} %add_bitcast_fusion.lengths, s32[1]{0:T(128)} %bitcast.3.refs_2_.rank, ...), custom_call_target="tpu_custom_call", output_to_operand_aliasing={{0}: (8, {}), {1}: (9, {})} | custom-call | bytes 1179648 | tf_op jit(solution)/shard_map/pallas_call | solution.py:824
  78.2 0.7 add_convert_fusion
  (59 shorter events, 1.7 us)
Async XLA Ops:
  1.3 0.7 copy-start.2
  4.7 13.3 %copy-start.3 = (s32[4,10]{1,0:T(4,128)S(1)}, s32[4,10]{1,0:T(4,128)}, u32[]{:S(2)}) copy-start(s32[4,10]{1,0:T(4,128)} %table.5) | copy-start | bytes 484
  4.7 13.3 %copy-start.6 = (s32[4]{0:T(128)S(1)}, s32[4]{0:T(128)}, u32[]{:S(2)}) copy-start(s32[4]{0:T(128)} %lengths.1) | copy-start | bytes 52
  4.7 33.7 %collective-permute-start.9 = (bf16[6,128,512]{2,1,0:T(8,128)(2,1)S(1)}, bf16[6,128,512]{2,1,0:T(8,128)(2,1)S(1)}, u32[]{:S(2)}, u32[]{:S(2)}) collective-permute-start(bf16[6,128,512]{2,1,0:T(8,128)(2,1)S(1)} %get-tuple-element.53), channel_id=1, source_target_pairs={{0,16},{4,20},{8,24},{12,28},{16,0},{20,4},{24,8},{28,12},{1,17},{... | collective-permute-start | bytes 2359304 | tf_op jit(solution)/shard_map/ppermute | solution.py:31
  7.7 30.7 %collective-permute-start.10 = (bf16[10,64,128]{2,1,0:T(8,128)(2,1)S(1)}, bf16[10,64,128]{2,1,0:T(8,128)(2,1)S(1)}, u32[]{:S(2)}, u32[]{:S(2)}) collective-permute-start(bf16[10,64,128]{2,1,0:T(8,128)(2,1)S(1)} %get-tuple-element.54), channel_id=1, source_target_pairs={{0,16},{4,20},{8,24},{12,28},{16,0},{20,4},{24,8},{28,12},{1,17},{... | collective-permute-start | bytes 491528 | tf_op jit(solution)/shard_map/ppermute | solution.py:31
  7.8 7.9 %collective-permute-start = (bf16[16,576]{1,0:T(8,128)(2,1)S(1)}, bf16[16,576]{1,0:T(8,128)(2,1)S(1)}, u32[]{:S(2)}, u32[]{:S(2)}) collective-permute-start(bf16[16,576]{1,0:T(8,128)(2,1)S(1)} %get-tuple-element.40._.refs_3_.refs_4_), channel_id=1, source_target_pairs={{0,1},{1,0},{2,3},{3,2},{4,5},{5,4},{6,7},{7,6},{8,9},{9,8},{10,11... | collective-permute-start | bytes 55304 | tf_op jit(solution)/shard_map/ppermute | solution.py:31
  9.8 5.9 %collective-permute-start.1 = (bf16[16,576]{1,0:T(8,128)(2,1)S(1)}, bf16[16,576]{1,0:T(8,128)(2,1)S(1)}, u32[]{:S(2)}, u32[]{:S(2)}) collective-permute-start(bf16[16,576]{1,0:T(8,128)(2,1)S(1)} %get-tuple-element.40._.refs_3_.refs_4_), channel_id=1, source_target_pairs={{0,2},{1,3},{2,0},{3,1},{4,6},{5,7},{6,4},{7,5},{8,10},{9,11},{10,... | collective-permute-start | bytes 55304 | tf_op jit(solution)/shard_map/ppermute | solution.py:31
  12.4 5.6 %collective-permute-start.2 = (bf16[16,576]{1,0:T(8,128)(2,1)S(1)}, bf16[16,576]{1,0:T(8,128)(2,1)S(1)}, u32[]{:S(2)}, u32[]{:S(2)}) collective-permute-start(bf16[16,576]{1,0:T(8,128)(2,1)S(1)} %get-tuple-element.40._.refs_3_.refs_4_), channel_id=1, source_target_pairs={{0,3},{1,2},{2,1},{3,0},{4,7},{5,6},{6,5},{7,4},{8,11},{9,10},{10,... | collective-permute-start | bytes 55304 | tf_op jit(solution)/shard_map/ppermute | solution.py:31
  12.4 13.5 %copy-start.5 = (f32[512]{0:T(512)S(1)}, f32[512]{0:T(512)}, u32[]{:S(2)}) copy-start(f32[512]{0:T(512)} %param.31) | copy-start | bytes 6148
  21.4 17.0 %copy-start.1 = (bf16[4,2048]{1,0:T(4,128)(2,1)S(1)}, bf16[4,2048]{1,0:T(4,128)(2,1)}, u32[]{:S(2)}) copy-start(bf16[4,2048]{1,0:T(4,128)(2,1)} %refs_5_.1) | copy-start | bytes 49156
  21.4 17.0 %copy-start.4 = (f32[2048]{0:T(1024)S(1)}, f32[2048]{0:T(1024)}, u32[]{:S(2)}) copy-start(f32[2048]{0:T(1024)} %param.35) | copy-start | bytes 24580
  21.5 21.9 %copy-start.7 = (s32[32,6]{0,1:T(8,128)S(1)}, s32[32,6]{0,1:T(8,128)}, u32[]{:S(2)}) copy-start(s32[32,6]{0,1:T(8,128)} %param.37) | copy-start | bytes 2308
  21.5 7.5 %collective-permute-start.3 = (bf16[16,640]{1,0:T(8,128)(2,1)S(1)}, bf16[16,640]{1,0:T(8,128)(2,1)S(1)}, u32[]{:S(2)}, u32[]{:S(2)}) collective-permute-start(bf16[16,640]{1,0:T(8,128)(2,1)S(1)} %get-tuple-element.44), channel_id=1, source_target_pairs={{0,1},{1,0},{2,3},{3,2},{4,5},{5,4},{6,7},{7,6},{8,9},{9,8},{10,11... | collective-permute-start | bytes 61448 | tf_op jit(solution)/shard_map/ppermute | solution.py:31
  21.6 7.4 %collective-permute-start.4 = (bf16[16,640]{1,0:T(8,128)(2,1)S(1)}, bf16[16,640]{1,0:T(8,128)(2,1)S(1)}, u32[]{:S(2)}, u32[]{:S(2)}) collective-permute-start(bf16[16,640]{1,0:T(8,128)(2,1)S(1)} %get-tuple-element.45), channel_id=1, source_target_pairs={{0,2},{1,3},{2,0},{3,1},{4,6},{5,7},{6,4},{7,5},{8,10},{9,11},{10,... | collective-permute-start | bytes 61448 | tf_op jit(solution)/shard_map/ppermute | solution.py:31
  23.4 5.6 %collective-permute-start.5 = (bf16[16,640]{1,0:T(8,128)(2,1)S(1)}, bf16[16,640]{1,0:T(8,128)(2,1)S(1)}, u32[]{:S(2)}, u32[]{:S(2)}) collective-permute-start(bf16[16,640]{1,0:T(8,128)(2,1)S(1)} %get-tuple-element.46), channel_id=1, source_target_pairs={{0,3},{1,2},{2,1},{3,0},{4,7},{5,6},{6,5},{7,4},{8,11},{9,10},{10,... | collective-permute-start | bytes 61448 | tf_op jit(solution)/shard_map/ppermute | solution.py:31
  29.7 4.4 %collective-permute-start.6 = (bf16[4,2048]{1,0:T(4,128)(2,1)S(1)}, bf16[4,2048]{1,0:T(4,128)(2,1)S(1)}, u32[]{:S(2)}, u32[]{:S(2)}) collective-permute-start(bf16[4,2048]{1,0:T(4,128)(2,1)S(1)} %get-tuple-element.52), channel_id=1, source_target_pairs={{0,1},{1,0},{2,3},{3,2},{4,5},{5,4},{6,7},{7,6},{8,9},{9,8},{10,11... | collective-permute-start | bytes 49160 | tf_op jit(solution)/shard_map/ppermute | solution.py:31
  29.7 4.9 %collective-permute-start.7 = (bf16[4,2048]{1,0:T(4,128)(2,1)S(1)}, bf16[4,2048]{1,0:T(4,128)(2,1)S(1)}, u32[]{:S(2)}, u32[]{:S(2)}) collective-permute-start(bf16[4,2048]{1,0:T(4,128)(2,1)S(1)} %get-tuple-element.52), channel_id=1, source_target_pairs={{0,2},{1,3},{2,0},{3,1},{4,6},{5,7},{6,4},{7,5},{8,10},{9,11},{10,... | collective-permute-start | bytes 49160 | tf_op jit(solution)/shard_map/ppermute | solution.py:31
  32.9 5.5 %collective-permute-start.8 = (bf16[4,2048]{1,0:T(4,128)(2,1)S(1)}, bf16[4,2048]{1,0:T(4,128)(2,1)S(1)}, u32[]{:S(2)}, u32[]{:S(2)}) collective-permute-start(bf16[4,2048]{1,0:T(4,128)(2,1)S(1)} %get-tuple-element.52), channel_id=1, source_target_pairs={{0,3},{1,2},{2,1},{3,0},{4,7},{5,6},{6,5},{7,4},{8,11},{9,10},{10,... | collective-permute-start | bytes 49160 | tf_op jit(solution)/shard_map/ppermute | solution.py:31
  38.6 1.3 %collective-permute-start.11 = (bf16[4,2176]{1,0:T(4,128)(2,1)S(1)}, bf16[4,2176]{1,0:T(4,128)(2,1)S(1)}, u32[]{:S(2)}, u32[]{:S(2)}) collective-permute-start(bf16[4,2176]{1,0:T(4,128)(2,1)S(1)} %get-tuple-element.55.rows), channel_id=1, source_target_pairs={{0,4},{4,0},{8,12},{12,8},{16,20},{20,16},{24,28},{28,24},{1,5},{5... | collective-permute-start | bytes 52232 | tf_op jit(solution)/shard_map/ppermute | solution.py:31
  39.8 8.2 %collective-permute-start.12 = (bf16[8,2176]{1,0:T(8,128)(2,1)S(1)}, bf16[8,2176]{1,0:T(8,128)(2,1)S(1)}, u32[]{:S(2)}, u32[]{:S(2)}) collective-permute-start(bf16[8,2176]{1,0:T(8,128)(2,1)S(1)} %pad_maximum_fusion._.refs_0_), channel_id=1, source_target_pairs={{0,8},{4,12},{8,0},{12,4},{16,24},{20,28},{24,16},{28,20},{1,9},{5... | collective-permute-start | bytes 104456 | tf_op jit(solution)/shard_map/ppermute | solution.py:31
  41.4 6.7 %collective-permute-start.13 = (bf16[8,2176]{1,0:T(8,128)(2,1)S(1)}, bf16[8,2176]{1,0:T(8,128)(2,1)S(1)}, u32[]{:S(2)}, u32[]{:S(2)}) collective-permute-start(bf16[8,2176]{1,0:T(8,128)(2,1)S(1)} %pad_maximum_fusion._.refs_0_), channel_id=1, source_target_pairs={{0,16},{4,20},{8,24},{12,28},{16,0},{20,4},{24,8},{28,12},{1,17},{... | collective-permute-start | bytes 104456 | tf_op jit(solution)/shard_map/ppermute | solution.py:31
  42.6 5.5 %collective-permute-start.14 = (bf16[8,2176]{1,0:T(8,128)(2,1)S(1)}, bf16[8,2176]{1,0:T(8,128)(2,1)S(1)}, u32[]{:S(2)}, u32[]{:S(2)}) collective-permute-start(bf16[8,2176]{1,0:T(8,128)(2,1)S(1)} %pad_maximum_fusion._.refs_0_), channel_id=1, source_target_pairs={{0,24},{4,28},{8,16},{12,20},{16,8},{20,12},{24,0},{28,4},{1,25},{... | collective-permute-start | bytes 104456 | tf_op jit(solution)/shard_map/ppermute | solution.py:31
  43.5 4.6 %copy-start = (bf16[2048,64]{0,1:T(8,128)(2,1)S(1)}, bf16[2048,64]{0,1:T(8,128)(2,1)}, u32[]{:S(2)}) copy-start(bf16[2048,64]{0,1:T(8,128)(2,1)} %param.36) | copy-start | bytes 786436
  48.7 14.1 %collective-permute-start.15 = (bf16[528,512]{1,0:T(8,128)(2,1)S(1)}, bf16[528,512]{1,0:T(8,128)(2,1)S(1)}, u32[]{:S(2)}, u32[]{:S(2)}) collective-permute-start(bf16[528,512]{1,0:T(8,128)(2,1)S(1)} %get-tuple-element.58), channel_id=1, source_target_pairs={{0,16},{4,20},{8,24},{12,28},{16,0},{20,4},{24,8},{28,12},{1,17},{... | collective-permute-start | bytes 1622024 | tf_op jit(solution)/shard_map/ppermute | solution.py:31
  62.7 1.3 %collective-permute-start.16 = (bf16[16,2048]{1,0:T(8,128)(2,1)S(1)}, bf16[16,2048]{1,0:T(8,128)(2,1)S(1)}, u32[]{:S(2)}, u32[]{:S(2)}) collective-permute-start(bf16[16,2048]{1,0:T(8,128)(2,1)S(1)} %get-tuple-element.62), channel_id=1, source_target_pairs={{0,4},{4,0},{8,12},{12,8},{16,20},{20,16},{24,28},{28,24},{1,5},{5... | collective-permute-start | bytes 196616 | tf_op jit(solution)/shard_map/ppermute | solution.py:31
  64.1 7.0 %collective-permute-start.17 = (bf16[4,2048]{1,0:T(4,128)(2,1)S(1)}, bf16[4,2048]{1,0:T(4,128)(2,1)S(1)}, u32[]{:S(2)}, u32[]{:S(2)}) collective-permute-start(bf16[4,2048]{1,0:T(4,128)(2,1)S(1)} %get-tuple-element.68), channel_id=1, source_target_pairs={{0,8},{4,12},{8,0},{12,4},{16,24},{20,28},{24,16},{28,20},{1,9},{5... | collective-permute-start | bytes 49160 | tf_op jit(solution)/shard_map/ppermute | solution.py:31
  65.6 5.5 %collective-permute-start.18 = (bf16[4,2048]{1,0:T(4,128)(2,1)S(1)}, bf16[4,2048]{1,0:T(4,128)(2,1)S(1)}, u32[]{:S(2)}, u32[]{:S(2)}) collective-permute-start(bf16[4,2048]{1,0:T(4,128)(2,1)S(1)} %get-tuple-element.69), channel_id=1, source_target_pairs={{0,16},{4,20},{8,24},{12,28},{16,0},{20,4},{24,8},{28,12},{1,17},{... | collective-permute-start | bytes 49160 | tf_op jit(solution)/shard_map/ppermute | solution.py:31
  66.4 4.7 %collective-permute-start.19 = (bf16[4,2048]{1,0:T(4,128)(2,1)S(1)}, bf16[4,2048]{1,0:T(4,128)(2,1)S(1)}, u32[]{:S(2)}, u32[]{:S(2)}) collective-permute-start(bf16[4,2048]{1,0:T(4,128)(2,1)S(1)} %get-tuple-element.70), channel_id=1, source_target_pairs={{0,24},{4,28},{8,16},{12,20},{16,8},{20,12},{24,0},{28,4},{1,25},{... | collective-permute-start | bytes 49160 | tf_op jit(solution)/shard_map/ppermute | solution.py:31
  71.2 7.1 %collective-permute-start.22 = (bf16[4,2048]{1,0:T(4,128)(2,1)S(1)}, bf16[4,2048]{1,0:T(4,128)(2,1)S(1)}, u32[]{:S(2)}, u32[]{:S(2)}) collective-permute-start(bf16[4,2048]{1,0:T(4,128)(2,1)S(1)} %get-tuple-element.72), channel_id=1, source_target_pairs={{0,3},{1,2},{2,1},{3,0},{4,7},{5,6},{6,5},{7,4},{8,11},{9,10},{10,... | collective-permute-start | bytes 49160 | tf_op jit(solution)/shard_map/ppermute | solution.py:31
  72.7 5.5 %collective-permute-start.21 = (bf16[4,2048]{1,0:T(4,128)(2,1)S(1)}, bf16[4,2048]{1,0:T(4,128)(2,1)S(1)}, u32[]{:S(2)}, u32[]{:S(2)}) collective-permute-start(bf16[4,2048]{1,0:T(4,128)(2,1)S(1)} %get-tuple-element.72), channel_id=1, source_target_pairs={{0,2},{1,3},{2,0},{3,1},{4,6},{5,7},{6,4},{7,5},{8,10},{9,11},{10,... | collective-permute-start | bytes 49160 | tf_op jit(solution)/shard_map/ppermute | solution.py:31
  72.7 5.5 %collective-permute-start.20 = (bf16[4,2048]{1,0:T(4,128)(2,1)S(1)}, bf16[4,2048]{1,0:T(4,128)(2,1)S(1)}, u32[]{:S(2)}, u32[]{:S(2)}) collective-permute-start(bf16[4,2048]{1,0:T(4,128)(2,1)S(1)} %get-tuple-element.72), channel_id=1, source_target_pairs={{0,1},{1,0},{2,3},{3,2},{4,5},{5,4},{6,7},{7,6},{8,9},{9,8},{10,11... | collective-permute-start | bytes 49160 | tf_op jit(solution)/shard_map/ppermute | solution.py:31

commit v6 on v5

--- a/solution.py
+++ b/solution.py
@@ -639,7 +639,7 @@
             pltpu.VMEM(w_query.shape, BF16),
             pltpu.VMEM(w_key_up.shape, BF16),
             dma((2, per_dev)),
-            dma((9,)),
+            dma((7,)),
         ],
         vmem=8,
         flops=2 * requests * w_query.size,

time: 79.4 us -> 80.1 us (level)
  no operation moved by 1% of the time
where the time goes in v6:
time: 80.1 us; the launch traced here: 79.5 us
  Pallas kernels  37.2 us (46%)
  starting transfers between devices  29.8 us (37%)
  waiting for transfers between devices  8.75 us (11%)
  between operations  1.65 us (2%)
  local copies, waits for them, and re-layouts  1.17 us (1%)
  other arithmetic  0.88 us (1%)
    ppermute x23, starting transfers between devices, xored(): return lax.ppermute(value, axis, pairs)  29.8 us
    pallas_call x1, Pallas kernels, body(): call(functools.partial(expert_kernel, requests, 512, units), (struct((gro...  12.6 us
    ppermute x23, waiting for transfers between devices, xored(): return lax.ppermute(value, axis, pairs)  8.75 us
    pallas_call x1, Pallas kernels, body(): call(functools.partial(shared_kernel, first_span, second_span), (struct((...  4.58 us
    pallas_call x1, Pallas kernels, body(): call(functools.partial(attention_kernel, n_tp, per_dev, requests, lat_siz...  3.47 us
    pallas_call x1, Pallas kernels, body(): call(functools.partial(cache_kernel, first_span), (struct(lat_pool.shape,...  3.45 us
    pallas_call x1, Pallas kernels, body(): call(functools.partial(fetch_kernel, requests), (pltpu.VMEM((pages,) + la...  3.31 us
    pallas_call x1, Pallas kernels, body(): call(token_weights_kernel, (pltpu.VMEM(w_value_up.shape, BF16), pltpu.VME...  3.05 us
  transfers between devices with their start and end apart: 23, of which 5 were waited for; matrix products, arithmetic and copies ran while one was open for 1% of the time, Pallas kernels for 42%

profile of v6, /device:TPU:0, one launch (start us, length us, event | category | flops | bytes accessed | tf_op | source)
XLA Modules:
  0.0 79.5 jit_solution(12465804282834004806)
XLA Ops:
  1.3 0.7 copy-done.2
  2.0 3.0 %shard_map.229 = (bf16[16,576]{1,0:T(8,128)(2,1)S(1)}, bf16[4,2048]{1,0:T(4,128)(2,1)S(1)}, bf16[6,128,512]{2,1,0:T(8,128)(2,1)S(1)}, bf16[10,64,128]{2,1,0:T(8,128)(2,1)S(1)}) custom-call(s32[4,10]{1,0:T(4,128)S(1)} %copy-done.2, s32[1]{0:T(128)} %copy.40.slot_in.refs_0_.slot, bf16[4,2048]{1,0:T(4,128)(2,1)} %refs_5_.1, f32[1,2048]{1,0:T(1,128)} %bitcast.38, ...), custom_call_target="tpu_custom_call" | custom-call | flops 12582912 | bytes 3145728 | tf_op jit(solution)/shard_map/pallas_call | solution.py:624
  5.0 3.0 %collective-permute-start.9 = (bf16[6,128,512]{2,1,0:T(8,128)(2,1)S(1)}, bf16[6,128,512]{2,1,0:T(8,128)(2,1)S(1)}, u32[]{:S(2)}, u32[]{:S(2)}) collective-permute-start(bf16[6,128,512]{2,1,0:T(8,128)(2,1)S(1)} %get-tuple-element.53), channel_id=1, source_target_pairs={{0,16},{4,20},{8,24},{12,28},{16,0},{20,4},{24,8},{28,12},{1,17},{... | collective-permute-start | bytes 2359304 | tf_op jit(solution)/shard_map/ppermute | solution.py:31
  8.1 2.0 %collective-permute-start = (bf16[16,576]{1,0:T(8,128)(2,1)S(1)}, bf16[16,576]{1,0:T(8,128)(2,1)S(1)}, u32[]{:S(2)}, u32[]{:S(2)}) collective-permute-start(bf16[16,576]{1,0:T(8,128)(2,1)S(1)} %get-tuple-element.40._.refs_3_.refs_4_), channel_id=1, source_target_pairs={{0,1},{1,0},{2,3},{3,2},{4,5},{5,4},{6,7},{7,6},{8,9},{9,8},{10,11... | collective-permute-start | bytes 55304 | tf_op jit(solution)/shard_map/ppermute | solution.py:31
  10.2 2.6 %collective-permute-start.1 = (bf16[16,576]{1,0:T(8,128)(2,1)S(1)}, bf16[16,576]{1,0:T(8,128)(2,1)S(1)}, u32[]{:S(2)}, u32[]{:S(2)}) collective-permute-start(bf16[16,576]{1,0:T(8,128)(2,1)S(1)} %get-tuple-element.40._.refs_3_.refs_4_), channel_id=1, source_target_pairs={{0,2},{1,3},{2,0},{3,1},{4,6},{5,7},{6,4},{7,5},{8,10},{9,11},{10,... | collective-permute-start | bytes 55304 | tf_op jit(solution)/shard_map/ppermute | solution.py:31
  12.7 3.3 %shard_map.230 = (bf16[40,128,512]{2,1,0:T(8,128)(2,1)S(1)}, bf16[40,64,128]{2,1,0:T(8,128)(2,1)S(1)}, f32[8,128]{1,0:T(8,128)}) custom-call(bf16[16,576]{1,0:T(8,128)(2,1)S(1)} %get-tuple-element.40._.refs_3_.refs_4_, bf16[40,128,512]{2,1,0:T(8,128)(2,1)} %lat.5, bf16[40,64,128]{2,1,0:T(8,128)(2,1)} %rope.3), custom_call_target="tpu_custom_call" | custom-call | flops 9437184 | bytes 10878976 | tf_op jit(solution)/shard_map/pallas_call | solution.py:655
  16.1 2.2 %collective-permute-done.2.refs_6_ = bf16[16,576]{1,0:T(8,128)(2,1)S(1)} collective-permute-done((bf16[16,576]{1,0:T(8,128)(2,1)S(1)}, bf16[16,576]{1,0:T(8,128)(2,1)S(1)}, u32[]{:S(2)}, u32[]{:S(2)}) %collective-permute-start.2) | collective-permute-done | bytes 18464 | tf_op jit(solution)/shard_map/ppermute | solution.py:31
  18.3 3.5 %shard_map.231 = (bf16[16,640]{1,0:T(8,128)(2,1)S(1)}, bf16[16,640]{1,0:T(8,128)(2,1)S(1)}, bf16[16,640]{1,0:T(8,128)(2,1)S(1)}, bf16[16,640]{1,0:T(8,128)(2,1)S...) custom-call(s32[4,10]{1,0:T(4,128)S(1)} %copy-done.3, s32[4]{0:T(128)S(1)} %copy-done.6, ...), custom_call_target="tpu_custom_call" | custom-call | flops 167772160 | bytes 5898240 | tf_op jit(solution)/shard_map/pallas_call | solution.py:670
  21.9 1.9 %collective-permute-start.4 = (bf16[16,640]{1,0:T(8,128)(2,1)S(1)}, bf16[16,640]{1,0:T(8,128)(2,1)S(1)}, u32[]{:S(2)}, u32[]{:S(2)}) collective-permute-start(bf16[16,640]{1,0:T(8,128)(2,1)S(1)} %get-tuple-element.45), channel_id=1, source_target_pairs={{0,2},{1,3},{2,0},{3,1},{4,6},{5,7},{6,4},{7,5},{8,10},{9,11},{10,... | collective-permute-start | bytes 61448 | tf_op jit(solution)/shard_map/ppermute | solution.py:31
  23.8 2.5 %collective-permute-start.5 = (bf16[16,640]{1,0:T(8,128)(2,1)S(1)}, bf16[16,640]{1,0:T(8,128)(2,1)S(1)}, u32[]{:S(2)}, u32[]{:S(2)}) collective-permute-start(bf16[16,640]{1,0:T(8,128)(2,1)S(1)} %get-tuple-element.46), channel_id=1, source_target_pairs={{0,3},{1,2},{2,1},{3,0},{4,7},{5,6},{6,5},{7,4},{8,11},{9,10},{10,... | collective-permute-start | bytes 61448 | tf_op jit(solution)/shard_map/ppermute | solution.py:31
  26.3 3.1 %shard_map.232 = (bf16[4,512,128]{2,1,0:T(8,128)(2,1)S(1)}, bf16[512,2048]{1,0:T(8,128)(2,1)S(1)}, f32[4,640]{1,0:T(4,128)S(1)}) custom-call(s32[4]{0:T(128)S(1)} %copy-done.6, bf16[4,2048]{1,0:T(4,128)(2,1)S(1)} %get-tuple-element.47.normed, f32[1,512]{1,0:T(1,128)S(1)} %bitcast.28, bf16[16,640]{1,0:T(8,128)(2,1)S(1)} %get-tuple-element.43._.refs_0_, ...), custom_call_target="tpu_custom_call" | custom-call | flops 9437184 | bytes 4980736 | tf_op jit(solution)/shard_map/pallas_call | solution.py:682
  29.4 0.7 shard_map.233
  30.1 3.2 %collective-permute-start.7 = (bf16[4,2048]{1,0:T(4,128)(2,1)S(1)}, bf16[4,2048]{1,0:T(4,128)(2,1)S(1)}, u32[]{:S(2)}, u32[]{:S(2)}) collective-permute-start(bf16[4,2048]{1,0:T(4,128)(2,1)S(1)} %get-tuple-element.52), channel_id=1, source_target_pairs={{0,2},{1,3},{2,0},{3,1},{4,6},{5,7},{6,4},{7,5},{8,10},{9,11},{10,... | collective-permute-start | bytes 49160 | tf_op jit(solution)/shard_map/ppermute | solution.py:31
  33.2 1.2 %collective-permute-start.8 = (bf16[4,2048]{1,0:T(4,128)(2,1)S(1)}, bf16[4,2048]{1,0:T(4,128)(2,1)S(1)}, u32[]{:S(2)}, u32[]{:S(2)}) collective-permute-start(bf16[4,2048]{1,0:T(4,128)(2,1)S(1)} %get-tuple-element.52), channel_id=1, source_target_pairs={{0,3},{1,2},{2,1},{3,0},{4,7},{5,6},{6,5},{7,4},{8,11},{9,10},{10,... | collective-permute-start | bytes 49160 | tf_op jit(solution)/shard_map/ppermute | solution.py:31
  35.0 3.8 %collective-permute-done.8.refs_4_ = bf16[4,2048]{1,0:T(4,128)(2,1)S(1)} collective-permute-done((bf16[4,2048]{1,0:T(4,128)(2,1)S(1)}, bf16[4,2048]{1,0:T(4,128)(2,1)S(1)}, u32[]{:S(2)}, u32[]{:S(2)}) %collective-permute-start.8) | collective-permute-done | bytes 16416 | tf_op jit(solution)/shard_map/ppermute | solution.py:31
  39.0 1.2 %collective-permute-done.11 = bf16[4,2176]{1,0:T(4,128)(2,1)S(1)} collective-permute-done((bf16[4,2176]{1,0:T(4,128)(2,1)S(1)}, bf16[4,2176]{1,0:T(4,128)(2,1)S(1)}, u32[]{:S(2)}, u32[]{:S(2)}) %collective-permute-start.11) | collective-permute-done | bytes 17440 | tf_op jit(solution)/shard_map/ppermute | solution.py:31
  40.2 1.3 %collective-permute-start.12 = (bf16[8,2176]{1,0:T(8,128)(2,1)S(1)}, bf16[8,2176]{1,0:T(8,128)(2,1)S(1)}, u32[]{:S(2)}, u32[]{:S(2)}) collective-permute-start(bf16[8,2176]{1,0:T(8,128)(2,1)S(1)} %pad_maximum_fusion._.refs_0_), channel_id=1, source_target_pairs={{0,8},{4,12},{8,0},{12,4},{16,24},{20,28},{24,16},{28,20},{1,9},{5... | collective-permute-start | bytes 104456 | tf_op jit(solution)/shard_map/ppermute | solution.py:31
  41.5 1.4 %collective-permute-start.13 = (bf16[8,2176]{1,0:T(8,128)(2,1)S(1)}, bf16[8,2176]{1,0:T(8,128)(2,1)S(1)}, u32[]{:S(2)}, u32[]{:S(2)}) collective-permute-start(bf16[8,2176]{1,0:T(8,128)(2,1)S(1)} %pad_maximum_fusion._.refs_0_), channel_id=1, source_target_pairs={{0,16},{4,20},{8,24},{12,28},{16,0},{20,4},{24,8},{28,12},{1,17},{... | collective-permute-start | bytes 104456 | tf_op jit(solution)/shard_map/ppermute | solution.py:31
  42.9 0.9 %collective-permute-start.14 = (bf16[8,2176]{1,0:T(8,128)(2,1)S(1)}, bf16[8,2176]{1,0:T(8,128)(2,1)S(1)}, u32[]{:S(2)}, u32[]{:S(2)}) collective-permute-start(bf16[8,2176]{1,0:T(8,128)(2,1)S(1)} %pad_maximum_fusion._.refs_0_), channel_id=1, source_target_pairs={{0,24},{4,28},{8,16},{12,20},{16,8},{20,12},{24,0},{28,4},{1,25},{... | collective-permute-start | bytes 104456 | tf_op jit(solution)/shard_map/ppermute | solution.py:31
  43.8 4.6 %shard_map.235 = (bf16[4,704]{1,0:T(4,128)(2,1)S(1)}, bf16[528,512]{1,0:T(8,128)(2,1)S(1)}) custom-call(s32[4,10]{1,0:T(4,128)S(1)} %copy-done.3, s32[1]{0:T(128)} %copy.40.slot_in.refs_0_.slot, bf16[4,2176]{1,0:T(4,128)(2,1)S(1)} %get-tuple-element.55.rows, bf16[4,2048]{1,0:T(4,128)(2,1)S(1)} %get-tuple-element.56.h_one, ...), custom_call_target="tpu_custom_call" | custom-call | flops 34603008 | bytes 8650752 | tf_op jit(solution)/shard_map/pallas_call | solution.py:726
  48.5 0.6 shard_map.236
  49.1 1.6 %collective-permute-start.15 = (bf16[528,512]{1,0:T(8,128)(2,1)S(1)}, bf16[528,512]{1,0:T(8,128)(2,1)S(1)}, u32[]{:S(2)}, u32[]{:S(2)}) collective-permute-start(bf16[528,512]{1,0:T(8,128)(2,1)S(1)} %get-tuple-element.58), channel_id=1, source_target_pairs={{0,16},{4,20},{8,24},{12,28},{16,0},{20,4},{24,8},{28,12},{1,17},{... | collective-permute-start | bytes 1622024 | tf_op jit(solution)/shard_map/ppermute | solution.py:31
  50.8 12.6 %shard_map.237 = (f32[16,2048]{1,0:T(8,128)S(1)}, bf16[16,2048]{1,0:T(8,128)(2,1)S(1)}) custom-call(s32[1]{0:T(128)} %bitcast.1.rank, bf16[32,2048]{1,0:T(8,128)(2,1)S(1)} %get-tuple-element.59.x, f32[32,64]{1,0:T(8,128)S(1)} %get-tuple-element.60.coef, bf16[2816,2048]{1,0:T(8,128)(2,1)} %bitcast.29, bf16[2816,2048]{1,0:T(8,128)(2,1)} %bitcast.30, ...), custom_call_target="tpu_custom_call" | custom-call | flops 1107296256 | bytes 34603008 | tf_op jit(solution)/shard_map/pallas_call | solution.py:764
  63.7 1.0 %collective-permute-done.16.got = bf16[16,2048]{1,0:T(8,128)(2,1)S(1)} collective-permute-done((bf16[16,2048]{1,0:T(8,128)(2,1)S(1)}, bf16[16,2048]{1,0:T(8,128)(2,1)S(1)}, u32[]{:S(2)}, u32[]{:S(2)}) %collective-permute-start.16) | collective-permute-done | bytes 65568 | tf_op jit(solution)/shard_map/ppermute | solution.py:31
  64.7 1.1 %collective-permute-start.17 = (bf16[4,2048]{1,0:T(4,128)(2,1)S(1)}, bf16[4,2048]{1,0:T(4,128)(2,1)S(1)}, u32[]{:S(2)}, u32[]{:S(2)}) collective-permute-start(bf16[4,2048]{1,0:T(4,128)(2,1)S(1)} %get-tuple-element.68), channel_id=1, source_target_pairs={{0,8},{4,12},{8,0},{12,4},{16,24},{20,28},{24,16},{28,20},{1,9},{5... | collective-permute-start | bytes 49160 | tf_op jit(solution)/shard_map/ppermute | solution.py:31
  65.9 0.6 collective-permute-start.18
  66.5 1.8 %collective-permute-start.19 = (bf16[4,2048]{1,0:T(4,128)(2,1)S(1)}, bf16[4,2048]{1,0:T(4,128)(2,1)S(1)}, u32[]{:S(2)}, u32[]{:S(2)}) collective-permute-start(bf16[4,2048]{1,0:T(4,128)(2,1)S(1)} %get-tuple-element.70), channel_id=1, source_target_pairs={{0,24},{4,28},{8,16},{12,20},{16,8},{20,12},{24,0},{28,4},{1,25},{... | collective-permute-start | bytes 49160 | tf_op jit(solution)/shard_map/ppermute | solution.py:31
  68.3 3.4 %shard_map.239 = (bf16[40,128,512]{2,1,0:T(8,128)(2,1)}, bf16[40,64,128]{2,1,0:T(8,128)(2,1)}, f32[4,2048]{1,0:T(4,128)S(1)}) custom-call(s32[4,10]{1,0:T(4,128)S(1)} %copy-done.3, s32[1]{0:T(128)} %copy.40.slot_in.refs_0_.slot, f32[4,2048]{1,0:T(4,128)S(1)} %get-tuple-element.63._.own, ...), custom_call_target="tpu_custom_call", output_to_operand_aliasing={{0}: (8, {}), {1}: (9, {})} | custom-call | bytes 1769472 | tf_op jit(solution)/shard_map/pallas_call | solution.py:789
  71.8 1.3 %collective-permute-start.22 = (bf16[4,2048]{1,0:T(4,128)(2,1)S(1)}, bf16[4,2048]{1,0:T(4,128)(2,1)S(1)}, u32[]{:S(2)}, u32[]{:S(2)}) collective-permute-start(bf16[4,2048]{1,0:T(4,128)(2,1)S(1)} %get-tuple-element.72), channel_id=1, source_target_pairs={{0,3},{1,2},{2,1},{3,0},{4,7},{5,6},{6,5},{7,4},{8,11},{9,10},{10,... | collective-permute-start | bytes 49160 | tf_op jit(solution)/shard_map/ppermute | solution.py:31
  73.1 3.2 %collective-permute-start.20 = (bf16[4,2048]{1,0:T(4,128)(2,1)S(1)}, bf16[4,2048]{1,0:T(4,128)(2,1)S(1)}, u32[]{:S(2)}, u32[]{:S(2)}) collective-permute-start(bf16[4,2048]{1,0:T(4,128)(2,1)S(1)} %get-tuple-element.72), channel_id=1, source_target_pairs={{0,1},{1,0},{2,3},{3,2},{4,5},{5,4},{6,7},{7,6},{8,9},{9,8},{10,11... | collective-permute-start | bytes 49160 | tf_op jit(solution)/shard_map/ppermute | solution.py:31
  76.4 2.3 %shard_map.241 = (bf16[40,128,512]{2,1,0:T(8,128)(2,1)}, bf16[40,64,128]{2,1,0:T(8,128)(2,1)}) custom-call(s32[4,10]{1,0:T(4,128)S(1)} %copy-done.3, s32[1]{0:T(128)} %copy.40.slot_in.refs_0_.slot, s32[4]{0:T(128)S(1)} %add_bitcast_fusion.lengths, s32[1]{0:T(128)} %bitcast.3.refs_2_.rank, ...), custom_call_target="tpu_custom_call", output_to_operand_aliasing={{0}: (8, {}), {1}: (9, {})} | custom-call | bytes 1179648 | tf_op jit(solution)/shard_map/pallas_call | solution.py:824
  78.8 0.7 add_convert_fusion
  (59 shorter events, 1.7 us)
Async XLA Ops:
  1.3 0.7 copy-start.2
  5.0 13.3 %copy-start.3 = (s32[4,10]{1,0:T(4,128)S(1)}, s32[4,10]{1,0:T(4,128)}, u32[]{:S(2)}) copy-start(s32[4,10]{1,0:T(4,128)} %table.5) | copy-start | bytes 484
  5.0 13.3 %copy-start.6 = (s32[4]{0:T(128)S(1)}, s32[4]{0:T(128)}, u32[]{:S(2)}) copy-start(s32[4]{0:T(128)} %lengths.1) | copy-start | bytes 52
  5.0 33.7 %collective-permute-start.9 = (bf16[6,128,512]{2,1,0:T(8,128)(2,1)S(1)}, bf16[6,128,512]{2,1,0:T(8,128)(2,1)S(1)}, u32[]{:S(2)}, u32[]{:S(2)}) collective-permute-start(bf16[6,128,512]{2,1,0:T(8,128)(2,1)S(1)} %get-tuple-element.53), channel_id=1, source_target_pairs={{0,16},{4,20},{8,24},{12,28},{16,0},{20,4},{24,8},{28,12},{1,17},{... | collective-permute-start | bytes 2359304 | tf_op jit(solution)/shard_map/ppermute | solution.py:31
  8.1 30.7 %collective-permute-start.10 = (bf16[10,64,128]{2,1,0:T(8,128)(2,1)S(1)}, bf16[10,64,128]{2,1,0:T(8,128)(2,1)S(1)}, u32[]{:S(2)}, u32[]{:S(2)}) collective-permute-start(bf16[10,64,128]{2,1,0:T(8,128)(2,1)S(1)} %get-tuple-element.54), channel_id=1, source_target_pairs={{0,16},{4,20},{8,24},{12,28},{16,0},{20,4},{24,8},{28,12},{1,17},{... | collective-permute-start | bytes 491528 | tf_op jit(solution)/shard_map/ppermute | solution.py:31
  8.1 7.9 %collective-permute-start = (bf16[16,576]{1,0:T(8,128)(2,1)S(1)}, bf16[16,576]{1,0:T(8,128)(2,1)S(1)}, u32[]{:S(2)}, u32[]{:S(2)}) collective-permute-start(bf16[16,576]{1,0:T(8,128)(2,1)S(1)} %get-tuple-element.40._.refs_3_.refs_4_), channel_id=1, source_target_pairs={{0,1},{1,0},{2,3},{3,2},{4,5},{5,4},{6,7},{7,6},{8,9},{9,8},{10,11... | collective-permute-start | bytes 55304 | tf_op jit(solution)/shard_map/ppermute | solution.py:31
  10.2 5.9 %collective-permute-start.1 = (bf16[16,576]{1,0:T(8,128)(2,1)S(1)}, bf16[16,576]{1,0:T(8,128)(2,1)S(1)}, u32[]{:S(2)}, u32[]{:S(2)}) collective-permute-start(bf16[16,576]{1,0:T(8,128)(2,1)S(1)} %get-tuple-element.40._.refs_3_.refs_4_), channel_id=1, source_target_pairs={{0,2},{1,3},{2,0},{3,1},{4,6},{5,7},{6,4},{7,5},{8,10},{9,11},{10,... | collective-permute-start | bytes 55304 | tf_op jit(solution)/shard_map/ppermute | solution.py:31
  12.7 5.6 %collective-permute-start.2 = (bf16[16,576]{1,0:T(8,128)(2,1)S(1)}, bf16[16,576]{1,0:T(8,128)(2,1)S(1)}, u32[]{:S(2)}, u32[]{:S(2)}) collective-permute-start(bf16[16,576]{1,0:T(8,128)(2,1)S(1)} %get-tuple-element.40._.refs_3_.refs_4_), channel_id=1, source_target_pairs={{0,3},{1,2},{2,1},{3,0},{4,7},{5,6},{6,5},{7,4},{8,11},{9,10},{10,... | collective-permute-start | bytes 55304 | tf_op jit(solution)/shard_map/ppermute | solution.py:31
  12.7 13.6 %copy-start.5 = (f32[512]{0:T(512)S(1)}, f32[512]{0:T(512)}, u32[]{:S(2)}) copy-start(f32[512]{0:T(512)} %param.31) | copy-start | bytes 6148
  21.8 17.0 %copy-start.1 = (bf16[4,2048]{1,0:T(4,128)(2,1)S(1)}, bf16[4,2048]{1,0:T(4,128)(2,1)}, u32[]{:S(2)}) copy-start(bf16[4,2048]{1,0:T(4,128)(2,1)} %refs_5_.1) | copy-start | bytes 49156
  21.8 17.0 %copy-start.4 = (f32[2048]{0:T(1024)S(1)}, f32[2048]{0:T(1024)}, u32[]{:S(2)}) copy-start(f32[2048]{0:T(1024)} %param.35) | copy-start | bytes 24580
  21.8 21.9 %copy-start.7 = (s32[32,6]{0,1:T(8,128)S(1)}, s32[32,6]{0,1:T(8,128)}, u32[]{:S(2)}) copy-start(s32[32,6]{0,1:T(8,128)} %param.37) | copy-start | bytes 2308
  21.8 7.5 %collective-permute-start.3 = (bf16[16,640]{1,0:T(8,128)(2,1)S(1)}, bf16[16,640]{1,0:T(8,128)(2,1)S(1)}, u32[]{:S(2)}, u32[]{:S(2)}) collective-permute-start(bf16[16,640]{1,0:T(8,128)(2,1)S(1)} %get-tuple-element.44), channel_id=1, source_target_pairs={{0,1},{1,0},{2,3},{3,2},{4,5},{5,4},{6,7},{7,6},{8,9},{9,8},{10,11... | collective-permute-start | bytes 61448 | tf_op jit(solution)/shard_map/ppermute | solution.py:31
  21.9 7.4 %collective-permute-start.4 = (bf16[16,640]{1,0:T(8,128)(2,1)S(1)}, bf16[16,640]{1,0:T(8,128)(2,1)S(1)}, u32[]{:S(2)}, u32[]{:S(2)}) collective-permute-start(bf16[16,640]{1,0:T(8,128)(2,1)S(1)} %get-tuple-element.45), channel_id=1, source_target_pairs={{0,2},{1,3},{2,0},{3,1},{4,6},{5,7},{6,4},{7,5},{8,10},{9,11},{10,... | collective-permute-start | bytes 61448 | tf_op jit(solution)/shard_map/ppermute | solution.py:31
  23.8 5.6 %collective-permute-start.5 = (bf16[16,640]{1,0:T(8,128)(2,1)S(1)}, bf16[16,640]{1,0:T(8,128)(2,1)S(1)}, u32[]{:S(2)}, u32[]{:S(2)}) collective-permute-start(bf16[16,640]{1,0:T(8,128)(2,1)S(1)} %get-tuple-element.46), channel_id=1, source_target_pairs={{0,3},{1,2},{2,1},{3,0},{4,7},{5,6},{6,5},{7,4},{8,11},{9,10},{10,... | collective-permute-start | bytes 61448 | tf_op jit(solution)/shard_map/ppermute | solution.py:31
  30.1 4.4 %collective-permute-start.6 = (bf16[4,2048]{1,0:T(4,128)(2,1)S(1)}, bf16[4,2048]{1,0:T(4,128)(2,1)S(1)}, u32[]{:S(2)}, u32[]{:S(2)}) collective-permute-start(bf16[4,2048]{1,0:T(4,128)(2,1)S(1)} %get-tuple-element.52), channel_id=1, source_target_pairs={{0,1},{1,0},{2,3},{3,2},{4,5},{5,4},{6,7},{7,6},{8,9},{9,8},{10,11... | collective-permute-start | bytes 49160 | tf_op jit(solution)/shard_map/ppermute | solution.py:31
  30.1 4.9 %collective-permute-start.7 = (bf16[4,2048]{1,0:T(4,128)(2,1)S(1)}, bf16[4,2048]{1,0:T(4,128)(2,1)S(1)}, u32[]{:S(2)}, u32[]{:S(2)}) collective-permute-start(bf16[4,2048]{1,0:T(4,128)(2,1)S(1)} %get-tuple-element.52), channel_id=1, source_target_pairs={{0,2},{1,3},{2,0},{3,1},{4,6},{5,7},{6,4},{7,5},{8,10},{9,11},{10,... | collective-permute-start | bytes 49160 | tf_op jit(solution)/shard_map/ppermute | solution.py:31
  33.2 5.5 %collective-permute-start.8 = (bf16[4,2048]{1,0:T(4,128)(2,1)S(1)}, bf16[4,2048]{1,0:T(4,128)(2,1)S(1)}, u32[]{:S(2)}, u32[]{:S(2)}) collective-permute-start(bf16[4,2048]{1,0:T(4,128)(2,1)S(1)} %get-tuple-element.52), channel_id=1, source_target_pairs={{0,3},{1,2},{2,1},{3,0},{4,7},{5,6},{6,5},{7,4},{8,11},{9,10},{10,... | collective-permute-start | bytes 49160 | tf_op jit(solution)/shard_map/ppermute | solution.py:31
  38.9 1.3 %collective-permute-start.11 = (bf16[4,2176]{1,0:T(4,128)(2,1)S(1)}, bf16[4,2176]{1,0:T(4,128)(2,1)S(1)}, u32[]{:S(2)}, u32[]{:S(2)}) collective-permute-start(bf16[4,2176]{1,0:T(4,128)(2,1)S(1)} %get-tuple-element.55.rows), channel_id=1, source_target_pairs={{0,4},{4,0},{8,12},{12,8},{16,20},{20,16},{24,28},{28,24},{1,5},{5... | collective-permute-start | bytes 52232 | tf_op jit(solution)/shard_map/ppermute | solution.py:31
  40.2 8.2 %collective-permute-start.12 = (bf16[8,2176]{1,0:T(8,128)(2,1)S(1)}, bf16[8,2176]{1,0:T(8,128)(2,1)S(1)}, u32[]{:S(2)}, u32[]{:S(2)}) collective-permute-start(bf16[8,2176]{1,0:T(8,128)(2,1)S(1)} %pad_maximum_fusion._.refs_0_), channel_id=1, source_target_pairs={{0,8},{4,12},{8,0},{12,4},{16,24},{20,28},{24,16},{28,20},{1,9},{5... | collective-permute-start | bytes 104456 | tf_op jit(solution)/shard_map/ppermute | solution.py:31
  41.5 7.0 %collective-permute-start.13 = (bf16[8,2176]{1,0:T(8,128)(2,1)S(1)}, bf16[8,2176]{1,0:T(8,128)(2,1)S(1)}, u32[]{:S(2)}, u32[]{:S(2)}) collective-permute-start(bf16[8,2176]{1,0:T(8,128)(2,1)S(1)} %pad_maximum_fusion._.refs_0_), channel_id=1, source_target_pairs={{0,16},{4,20},{8,24},{12,28},{16,0},{20,4},{24,8},{28,12},{1,17},{... | collective-permute-start | bytes 104456 | tf_op jit(solution)/shard_map/ppermute | solution.py:31
  42.9 5.6 %collective-permute-start.14 = (bf16[8,2176]{1,0:T(8,128)(2,1)S(1)}, bf16[8,2176]{1,0:T(8,128)(2,1)S(1)}, u32[]{:S(2)}, u32[]{:S(2)}) collective-permute-start(bf16[8,2176]{1,0:T(8,128)(2,1)S(1)} %pad_maximum_fusion._.refs_0_), channel_id=1, source_target_pairs={{0,24},{4,28},{8,16},{12,20},{16,8},{20,12},{24,0},{28,4},{1,25},{... | collective-permute-start | bytes 104456 | tf_op jit(solution)/shard_map/ppermute | solution.py:31
  43.8 4.6 %copy-start = (bf16[2048,64]{0,1:T(8,128)(2,1)S(1)}, bf16[2048,64]{0,1:T(8,128)(2,1)}, u32[]{:S(2)}) copy-start(bf16[2048,64]{0,1:T(8,128)(2,1)} %param.36) | copy-start | bytes 786436
  49.1 14.4 %collective-permute-start.15 = (bf16[528,512]{1,0:T(8,128)(2,1)S(1)}, bf16[528,512]{1,0:T(8,128)(2,1)S(1)}, u32[]{:S(2)}, u32[]{:S(2)}) collective-permute-start(bf16[528,512]{1,0:T(8,128)(2,1)S(1)} %get-tuple-element.58), channel_id=1, source_target_pairs={{0,16},{4,20},{8,24},{12,28},{16,0},{20,4},{24,8},{28,12},{1,17},{... | collective-permute-start | bytes 1622024 | tf_op jit(solution)/shard_map/ppermute | solution.py:31
  63.4 1.3 %collective-permute-start.16 = (bf16[16,2048]{1,0:T(8,128)(2,1)S(1)}, bf16[16,2048]{1,0:T(8,128)(2,1)S(1)}, u32[]{:S(2)}, u32[]{:S(2)}) collective-permute-start(bf16[16,2048]{1,0:T(8,128)(2,1)S(1)} %get-tuple-element.62), channel_id=1, source_target_pairs={{0,4},{4,0},{8,12},{12,8},{16,20},{20,16},{24,28},{28,24},{1,5},{5... | collective-permute-start | bytes 196616 | tf_op jit(solution)/shard_map/ppermute | solution.py:31
  64.7 7.0 %collective-permute-start.17 = (bf16[4,2048]{1,0:T(4,128)(2,1)S(1)}, bf16[4,2048]{1,0:T(4,128)(2,1)S(1)}, u32[]{:S(2)}, u32[]{:S(2)}) collective-permute-start(bf16[4,2048]{1,0:T(4,128)(2,1)S(1)} %get-tuple-element.68), channel_id=1, source_target_pairs={{0,8},{4,12},{8,0},{12,4},{16,24},{20,28},{24,16},{28,20},{1,9},{5... | collective-permute-start | bytes 49160 | tf_op jit(solution)/shard_map/ppermute | solution.py:31
  65.9 5.9 %collective-permute-start.18 = (bf16[4,2048]{1,0:T(4,128)(2,1)S(1)}, bf16[4,2048]{1,0:T(4,128)(2,1)S(1)}, u32[]{:S(2)}, u32[]{:S(2)}) collective-permute-start(bf16[4,2048]{1,0:T(4,128)(2,1)S(1)} %get-tuple-element.69), channel_id=1, source_target_pairs={{0,16},{4,20},{8,24},{12,28},{16,0},{20,4},{24,8},{28,12},{1,17},{... | collective-permute-start | bytes 49160 | tf_op jit(solution)/shard_map/ppermute | solution.py:31
  66.5 5.3 %collective-permute-start.19 = (bf16[4,2048]{1,0:T(4,128)(2,1)S(1)}, bf16[4,2048]{1,0:T(4,128)(2,1)S(1)}, u32[]{:S(2)}, u32[]{:S(2)}) collective-permute-start(bf16[4,2048]{1,0:T(4,128)(2,1)S(1)} %get-tuple-element.70), channel_id=1, source_target_pairs={{0,24},{4,28},{8,16},{12,20},{16,8},{20,12},{24,0},{28,4},{1,25},{... | collective-permute-start | bytes 49160 | tf_op jit(solution)/shard_map/ppermute | solution.py:31
  71.8 7.0 %collective-permute-start.22 = (bf16[4,2048]{1,0:T(4,128)(2,1)S(1)}, bf16[4,2048]{1,0:T(4,128)(2,1)S(1)}, u32[]{:S(2)}, u32[]{:S(2)}) collective-permute-start(bf16[4,2048]{1,0:T(4,128)(2,1)S(1)} %get-tuple-element.72), channel_id=1, source_target_pairs={{0,3},{1,2},{2,1},{3,0},{4,7},{5,6},{6,5},{7,4},{8,11},{9,10},{10,... | collective-permute-start | bytes 49160 | tf_op jit(solution)/shard_map/ppermute | solution.py:31
  73.1 5.7 %collective-permute-start.21 = (bf16[4,2048]{1,0:T(4,128)(2,1)S(1)}, bf16[4,2048]{1,0:T(4,128)(2,1)S(1)}, u32[]{:S(2)}, u32[]{:S(2)}) collective-permute-start(bf16[4,2048]{1,0:T(4,128)(2,1)S(1)} %get-tuple-element.72), channel_id=1, source_target_pairs={{0,2},{1,3},{2,0},{3,1},{4,6},{5,7},{6,4},{7,5},{8,10},{9,11},{10,... | collective-permute-start | bytes 49160 | tf_op jit(solution)/shard_map/ppermute | solution.py:31
  73.1 5.7 %collective-permute-start.20 = (bf16[4,2048]{1,0:T(4,128)(2,1)S(1)}, bf16[4,2048]{1,0:T(4,128)(2,1)S(1)}, u32[]{:S(2)}, u32[]{:S(2)}) collective-permute-start(bf16[4,2048]{1,0:T(4,128)(2,1)S(1)} %get-tuple-element.72), channel_id=1, source_target_pairs={{0,1},{1,0},{2,3},{3,2},{4,5},{5,4},{6,7},{7,6},{8,9},{9,8},{10,11... | collective-permute-start | bytes 49160 | tf_op jit(solution)/shard_map/ppermute | solution.py:31
